TPU v7x, 512 devices: a whole 4x8x8 slice. The times are simulated.
512 devices in a mesh: ctx: 32 (over x_lo, z, core), tp: 16 (over x_hi, y).
Axes of the slice: x: 4 (x_hi: 2, x_lo: 2; x = x_hi * 2 + x_lo), y: 8, z: 8, core: 2. Of those that a mesh axis runs over, the one named last changes fastest.
Arguments:
- signal: bfloat16 [256, 32768], P('tp', 'ctx'), may hold values from -6 to 6
- filter_taps: float32 [16, 32768], P(None, 'ctx'), may hold values from -6 to 6
- skip_gain: float32 [256], P('tp'), may hold values from 0.5 to 1.5
- grad_out: bfloat16 [256, 32768], P('tp', 'ctx'), may hold values from -6 to 6
Outputs:
- output: bfloat16 [256, 32768], P('tp', 'ctx')
- grad_signal: bfloat16 [256, 32768], P('tp', 'ctx')
- grad_filter: float32 [16, 32768], P(None, 'ctx')
All inputs are finite; a program needn't handle non-finite values.
Results may differ from a plain program's by a relative error of at most 0.0012.
Values sent between devices are 32-bit elements; how exact they have to be, the bound alone decides.
No kernel may reach another device: no remote copies, remote signals or barrier semaphores. Data moves between devices by JAX's collectives and lax.ppermute only.
A program may use at most 64 MiB of HBM per device.

v0:
```python
import functools
import math

import jax
import jax.numpy as jnp
import ml_dtypes
import numpy as np
from jax import lax
from jax.experimental import pallas as pl
from jax.experimental.pallas import tpu as pltpu
from jax.sharding import PartitionSpec as P

LANES = 128
SUBLANES = 8
VMEM_BYTES = 24 * 1024 * 1024


def split_table(table):
    high = table.astype(np.float32).astype(ml_dtypes.bfloat16)
    low = (table - high.astype(np.float64)).astype(ml_dtypes.bfloat16)
    return high, low


def make_tables(rows, scale):
    period = 2 * rows
    padded = period * LANES
    a = np.arange(rows)
    f1 = np.arange(rows)
    turn = 2.0 * np.pi * (np.outer(f1, a) % period) / period
    alternating = np.where(a % 2 == 0, 1.0, -1.0)
    cosines = np.cos(turn)
    sines = -np.sin(turn)
    sines[0] = alternating
    outer = np.concatenate([cosines, sines], axis=0)
    weights = np.full((rows,), 2.0)
    weights[0] = 1.0
    weights = np.concatenate([weights, weights])
    outer_back = (outer * weights[:, None]).T * (scale / padded)
    b = np.arange(LANES)
    kept = np.arange(rows + 1)
    angle = 2.0 * np.pi * (np.outer(kept, b) % padded) / padded
    twist = np.zeros((rows + 16, 2 * LANES))
    twist[: rows + 1, :LANES] = np.cos(angle)
    twist[: rows + 1, LANES:] = -np.sin(angle)
    inner = 2.0 * np.pi * (np.outer(b, b) % LANES) / LANES
    c, s = np.cos(inner), np.sin(inner)
    inner_there = np.block([[c, -s], [s, c]])
    inner_back = np.block([[c, s], [-s, c]])
    return (
        *split_table(outer),
        twist.astype(np.float32),
        *split_table(inner_there),
        *split_table(inner_back),
        *split_table(outer_back),
    )


def split(x):
    high = x.astype(jnp.bfloat16)
    low = (x - high.astype(jnp.float32)).astype(jnp.bfloat16)
    return high, low


def dot(x, y):
    return jnp.dot(x, y, preferred_element_type=jnp.float32)


def pack_kernel(signal_ref, grad_ref, filter_ref, out_ref):
    channels = signal_ref.shape[0]
    values = signal_ref[...].astype(jnp.float32)
    cotangent = grad_ref[...].astype(jnp.float32)
    taps = filter_ref[...]
    for core, order in enumerate(((values, cotangent, taps), (cotangent, values, taps))):
        for part, array in enumerate(order):
            for chunk in range(SUBLANES):
                start = core * 24 + part * 8 + chunk
                out_ref[pl.ds(start, channels, stride=48), :] = array[:, chunk * LANES : (chunk + 1) * LANES]


def convolve_kernel(
    sign_ref, in_ref, outer_h, outer_l, twist, there_h, there_l, back_h, back_l, outer_back_h, outer_back_l,
    out_ref, a_ref, u_h, u_l,
):
    blocks = in_ref.shape[0]
    rows = blocks * SUBLANES
    sign = sign_ref[0]

    def sequence(part):
        return in_ref[:, part * 8 : part * 8 + 8, :].reshape(rows, LANES)

    both = jnp.concatenate([sequence(0), sequence(1)], axis=1).astype(jnp.bfloat16)
    taps_h, taps_l = split(sequence(2))
    a_ref[:, : 2 * LANES] = dot(outer_h[...], both) + dot(outer_l[...], both)
    taps = dot(outer_h[...], jnp.concatenate([taps_h, taps_l], axis=1))
    a_ref[:, 2 * LANES :] = taps[:, :LANES] + taps[:, LANES:] + dot(outer_l[...], taps_h)

    last = a_ref[rows : rows + 1, :]
    first_row = lax.broadcasted_iota(jnp.int32, (16, 1), 0) == 0

    for start, count in ((0, rows // 2), (rows // 2, rows // 2), (rows, 16)):
        tr = twist[start : start + count, :LANES]
        ti = twist[start : start + count, LANES:]
        pieces = []
        for part in range(3):
            lanes = slice(part * LANES, (part + 1) * LANES)
            if start == rows:
                ar = jnp.where(first_row, last[:, lanes], 0.0)
                pieces.append(jnp.concatenate([ar * tr, ar * ti], axis=1))
                continue
            ar = a_ref[start : start + count, lanes]
            ai = a_ref[rows + start : rows + start + count, lanes]
            if start == 0:
                row = lax.broadcasted_iota(jnp.int32, (count, 1), 0)
                ai = jnp.where(row == 0, 0.0, ai)
            pieces.append(jnp.concatenate([ar * tr - ai * ti, ar * ti + ai * tr], axis=1))
        z_h, z_l = split(jnp.concatenate(pieces, axis=0))
        spec = dot(z_h, there_h[...]) + dot(z_l, there_h[...]) + dot(z_h, there_l[...])
        mr, mi = spec[:count, :LANES], spec[:count, LANES:]
        qr, qi = spec[count : 2 * count, :LANES], spec[count : 2 * count, LANES:]
        hr, hi = spec[2 * count :, :LANES], spec[2 * count :, LANES:] * sign
        conv = jnp.concatenate([mr * hr - mi * hi, mr * hi + mi * hr], axis=1)
        corr = jnp.concatenate([qr * mr + qi * mi, (qi * mr - qr * mi) * sign], axis=1)
        p_h, p_l = split(jnp.concatenate([conv, corr], axis=0))
        v = dot(p_h, back_h[...]) + dot(p_l, back_h[...]) + dot(p_h, back_l[...])
        for part in range(2):
            vr = v[part * count : (part + 1) * count, :LANES]
            vi = v[part * count : (part + 1) * count, LANES:]
            lanes = slice(part * LANES, (part + 1) * LANES)
            real_h, real_l = split(vr * tr + vi * ti)
            if start == rows:
                u_h[rows : rows + 16, lanes] = jnp.where(first_row, real_h, u_h[rows : rows + 16, lanes])
                u_l[rows : rows + 16, lanes] = jnp.where(first_row, real_l, u_l[rows : rows + 16, lanes])
                continue
            imag_h, imag_l = split(vi * tr - vr * ti)
            u_h[start : start + count, lanes] = real_h
            u_l[start : start + count, lanes] = real_l
            u_h[rows + start : rows + start + count, lanes] = imag_h
            u_l[rows + start : rows + start + count, lanes] = imag_l

    y = dot(outer_back_h[...], u_h[...]) + dot(outer_back_h[...], u_l[...]) + dot(outer_back_l[...], u_h[...])
    out_ref[:, :8, :] = y[:, :LANES].reshape(blocks, SUBLANES, LANES)
    out_ref[:, 8:, :] = y[:, LANES:].reshape(blocks, SUBLANES, LANES)


def collect_kernel(in_ref, corr_ref):
    channels = corr_ref.shape[0]
    for chunk in range(SUBLANES):
        corr_ref[:, chunk * LANES : (chunk + 1) * LANES] = in_ref[pl.ds(8 + chunk, channels, stride=32), :]


def finish_kernel(in_ref, gain_ref, signal_ref, grad_ref, out_ref, back_ref):
    channels = signal_ref.shape[0]
    gains = gain_ref[...]
    for chunk in range(SUBLANES):
        lanes = slice(chunk * LANES, (chunk + 1) * LANES)
        for core, (own, result) in enumerate(((signal_ref, out_ref), (grad_ref, back_ref))):
            conv = in_ref[pl.ds(core * 16 + chunk, channels, stride=32), :]
            result[:, lanes] = (conv + gains * own[:, lanes].astype(jnp.float32)).astype(jnp.bfloat16)


def call(kernel, out_shape, operands, scratch=(), smem=0):
    in_specs = [pl.BlockSpec(memory_space=pltpu.SMEM)] * smem
    in_specs += [pl.BlockSpec(memory_space=pltpu.VMEM)] * (len(operands) - smem)
    return pl.pallas_call(
        kernel,
        out_shape=out_shape,
        in_specs=in_specs,
        out_specs=jax.tree.map(lambda _: pl.BlockSpec(memory_space=pltpu.VMEM), out_shape),
        scratch_shapes=list(scratch),
        compiler_params=pltpu.CompilerParams(vmem_limit_bytes=VMEM_BYTES),
    )(*operands)


def on_device(signal, filter_taps, skip_gain, grad_out):
    channels, tokens = signal.shape
    ctx = lax.axis_size("ctx")
    tp = lax.axis_size("tp")
    length = tokens * ctx
    rows = length // LANES
    tables = make_tables(rows, 1.0 / math.sqrt(length))
    sign = (1 - 2 * (lax.axis_index("ctx") % 2)).astype(jnp.float32).reshape(1)

    packed = call(
        pack_kernel, jax.ShapeDtypeStruct((ctx * 24, LANES), jnp.float32), (signal, grad_out, filter_taps)
    )
    sequences = lax.all_to_all(packed.reshape(ctx, 24, LANES), "ctx", 0, 0, tiled=True)
    results = call(
        convolve_kernel,
        jax.ShapeDtypeStruct((ctx, 16, LANES), jnp.float32),
        (sign, sequences, *tables),
        scratch=(
            pltpu.VMEM((2 * rows, 3 * LANES), jnp.float32),
            pltpu.VMEM((2 * rows, 2 * LANES), jnp.bfloat16),
            pltpu.VMEM((2 * rows, 2 * LANES), jnp.bfloat16),
        ),
        smem=1,
    )
    returned = lax.all_to_all(results, "ctx", 0, 0, tiled=True).reshape(ctx * 16, LANES)
    corr = call(collect_kernel, jax.ShapeDtypeStruct((channels, tokens), jnp.float32), (returned,))
    everyone = jnp.broadcast_to(corr[None], (tp, channels, tokens))
    shares = lax.all_to_all(everyone, "tp", 0, 0, tiled=True)
    grad_filter = jnp.sum(shares, axis=0)
    output, grad_signal = call(
        finish_kernel,
        (
            jax.ShapeDtypeStruct((channels, tokens), jnp.bfloat16),
            jax.ShapeDtypeStruct((channels, tokens), jnp.bfloat16),
        ),
        (returned, skip_gain[:, None], signal, grad_out),
    )
    return (output, grad_signal, grad_filter)


def solution(mesh):
    in_specs = (P("tp", "ctx"), P(None, "ctx"), P("tp"), P("tp", "ctx"))
    out_specs = (P("tp", "ctx"), P("tp", "ctx"), P(None, "ctx"))
    return jax.shard_map(
        on_device, mesh=mesh, in_specs=in_specs, out_specs=out_specs, check_vma=False
    )
```

profile of v0, /device:TPU:8, one launch (start us, length us, event | category | flops | bytes accessed | tf_op | source)
XLA Modules:
  0.0 92.8 jit_solution(2416017858285461743)
XLA Ops:
  0.6 0.0 copy-start.9
  0.6 0.7 copy-done.9
  1.4 0.0 copy-start.11
  1.4 0.8 copy-done.11
  2.1 0.0 copy-start.13
  2.2 0.8 copy-done.13
  3.0 0.0 copy-start.3
  3.0 0.0 copy-start.4
  3.0 0.9 shard_map.148
  3.9 0.0 copy-start
  3.9 0.0 copy-start.1
  3.9 0.0 copy-start.2
  3.9 11.8 %all-to-all-start = ((f32[32,24,128]{2,1,0:T(8,128)}), f32[32,24,128]{2,1,0:T(8,128)S(1)}, u32[]{:S(2)}, u32[]{:S(2)}) async-start(f32[32,24,128]{2,1,0:T(8,128)} %bitcast.1), calls=%async_computation | async-start | bytes 786432 | tf_op jit(solution)/shard_map/all_to_all | solution.py:186
  15.7 15.9 %all-to-all-done.in_ref = f32[32,24,128]{2,1,0:T(8,128)S(1)} async-done(((f32[32,24,128]{2,1,0:T(8,128)}), f32[32,24,128]{2,1,0:T(8,128)S(1)}, u32[]{:S(2)}, u32[]{:S(2)}) %all-to-all-start) | async-done | bytes 393248 | tf_op jit(solution)/shard_map/all_to_all | solution.py:186
  31.6 0.0 copy-done.3
  31.6 0.0 copy-done.4
  31.6 0.0 copy-done
  31.6 0.0 copy-done.1
  31.6 0.0 copy-done.2
  31.6 0.0 copy-start.5
  31.6 0.9 copy-done.5
  32.5 0.0 copy-start.6
  32.5 0.9 copy-done.6
  33.4 0.0 copy-start.7
  33.4 0.9 copy-done.7
  34.3 0.0 copy-start.8
  34.3 0.9 copy-done.8
  35.2 2.7 %shard_map.149 = f32[32,16,128]{2,1,0:T(8,128)S(1)} custom-call(f32[1]{0:T(128)} %bitcast.sign_ref, f32[32,24,128]{2,1,0:T(8,128)S(1)} %all-to-all-done.in_ref, bf16[512,256]{1,0:T(8,128)(2,1)S(1)} %copy-done.4, bf16[512,256]{1,0:T(8,128)(2,1)S(1)} %copy-done.3, f32[272,256]{1,0:T(8,128)S(1)} %copy-done, bf16[256,256]{1,0:T(8,128)(2,1)S(1)} %copy-done.8, ...), custom_call_target="tpu_custom_call" | custom-call | tf_op jit(solution)/shard_map/pallas_call | solution.py:164
  37.9 16.2 %all_to_all.15 = f32[32,16,128]{2,1,0:T(8,128)S(1)} all-to-all(f32[32,16,128]{2,1,0:T(8,128)S(1)} %shard_map.149), channel_id=1, replica_groups=mesh['ctx'=32,'tp'=16] {'ctx'}, dimensions={0} | all-to-all | bytes 524288 | tf_op jit(solution)/shard_map/all_to_all | solution.py:198
  54.1 1.1 %broadcast_in_dim.10 = f32[16,16,1024]{2,1,0:T(8,128)} broadcast(f32[16,1024]{1,0:T(8,128)S(1)} %shard_map.151), dimensions={1,2} | broadcast | bytes 1114112 | tf_op jit(solution)/shard_map/broadcast_in_dim | solution.py:200
  55.2 0.0 copy-start.10
  55.2 0.0 copy-start.12
  55.2 9.9 %all-to-all-start.2 = ((f32[16,16,1024]{2,1,0:T(8,128)}), f32[16,16,1024]{2,1,0:T(8,128)S(1)}, u32[]{:S(2)}, u32[]{:S(2)}) async-start(f32[16,16,1024]{2,1,0:T(8,128)} %broadcast_in_dim.10), calls=%async_computation.2 | async-start | bytes 2097152 | tf_op jit(solution)/shard_map/all_to_all | solution.py:201
  65.1 0.0 copy-start.14
  65.1 0.6 copy-done.14
  65.7 0.1 copy.17.gain_ref
  65.8 0.0 copy-done.10
  65.8 0.0 copy-done.12
  65.8 0.7 shard_map.150
  66.5 25.6 %all-to-all-done.2 = f32[16,16,1024]{2,1,0:T(8,128)S(1)} async-done(((f32[16,16,1024]{2,1,0:T(8,128)}), f32[16,16,1024]{2,1,0:T(8,128)S(1)}, u32[]{:S(2)}, u32[]{:S(2)}) %all-to-all-start.2) | async-done | bytes 1048608 | tf_op jit(solution)/shard_map/all_to_all | solution.py:201
  92.1 0.7 reduce_sum.9
  (1 shorter events, 0.0 us)
Async XLA Ops:
  0.6 0.8 copy-start.9
  1.4 0.8 copy-start.11
  2.1 0.8 copy-start.13
  3.0 28.6 %copy-start.3 = (bf16[512,256]{1,0:T(8,128)(2,1)S(1)}, bf16[512,256]{1,0:T(8,128)(2,1)}, u32[]{:S(2)}) copy-start(bf16[512,256]{1,0:T(8,128)(2,1)} %constant.41.clone.outer_l) | copy-start | bytes 786436
  3.0 28.6 %copy-start.4 = (bf16[512,256]{1,0:T(8,128)(2,1)S(1)}, bf16[512,256]{1,0:T(8,128)(2,1)}, u32[]{:S(2)}) copy-start(bf16[512,256]{1,0:T(8,128)(2,1)} %constant.40.clone.outer_h) | copy-start | bytes 786436
  3.9 27.7 %copy-start = (f32[272,256]{1,0:T(8,128)S(1)}, f32[272,256]{1,0:T(8,128)}, u32[]{:S(2)}) copy-start(f32[272,256]{1,0:T(8,128)} %constant.42.clone.twist) | copy-start | bytes 835588
  3.9 27.7 %copy-start.1 = (bf16[256,512]{1,0:T(8,128)(2,1)S(1)}, bf16[256,512]{1,0:T(8,128)(2,1)}, u32[]{:S(2)}) copy-start(bf16[256,512]{1,0:T(8,128)(2,1)} %constant.48.clone.outer_back_l) | copy-start | bytes 786436
  3.9 27.7 %copy-start.2 = (bf16[256,512]{1,0:T(8,128)(2,1)S(1)}, bf16[256,512]{1,0:T(8,128)(2,1)}, u32[]{:S(2)}) copy-start(bf16[256,512]{1,0:T(8,128)(2,1)} %constant.47.clone.outer_back_h) | copy-start | bytes 786436
  3.9 27.7 %all-to-all-start = ((f32[32,24,128]{2,1,0:T(8,128)}), f32[32,24,128]{2,1,0:T(8,128)S(1)}, u32[]{:S(2)}, u32[]{:S(2)}) async-start(f32[32,24,128]{2,1,0:T(8,128)} %bitcast.1), calls=%async_computation | async-start | bytes 786432 | tf_op jit(solution)/shard_map/all_to_all | solution.py:186
  31.6 0.9 copy-start.5
  32.5 0.9 copy-start.6
  33.4 0.9 copy-start.7
  34.3 0.9 copy-start.8
  55.2 10.6 %copy-start.10 = (bf16[16,1024]{1,0:T(8,128)(2,1)S(1)}, bf16[16,1024]{1,0:T(8,128)(2,1)}, u32[]{:S(2)}) copy-start(bf16[16,1024]{1,0:T(8,128)(2,1)} %signal_ref.3) | copy-start | bytes 98308
  55.2 10.6 %copy-start.12 = (bf16[16,1024]{1,0:T(8,128)(2,1)S(1)}, bf16[16,1024]{1,0:T(8,128)(2,1)}, u32[]{:S(2)}) copy-start(bf16[16,1024]{1,0:T(8,128)(2,1)} %grad_ref.3) | copy-start | bytes 98308
  55.2 36.9 %all-to-all-start.2 = ((f32[16,16,1024]{2,1,0:T(8,128)}), f32[16,16,1024]{2,1,0:T(8,128)S(1)}, u32[]{:S(2)}, u32[]{:S(2)}) async-start(f32[16,16,1024]{2,1,0:T(8,128)} %broadcast_in_dim.10), calls=%async_computation.2 | async-start | bytes 2097152 | tf_op jit(solution)/shard_map/all_to_all | solution.py:201
  65.1 0.7 copy-start.14
where the time goes:
time: 93.4 us; the launch traced here: 92.8 us
  waiting for transfers between devices  41.5 us (44%)
  starting transfers between devices  21.6 us (23%)
  blocking collectives  16.2 us (17%)
  local copies, waits for them, and re-layouts  7.82 us (8%)
  Pallas kernels  4.33 us (5%)
    all_to_all x1, waiting for transfers between devices, on_device(): shares = lax.all_to_all(everyone, 'tp', 0, 0, tiled=True)  25.6 us
    all_to_all x1, blocking collectives, on_device(): lax.all_to_all(results, 'ctx', 0, 0, tiled=True).reshape(ctx * 16, LANES)  16.2 us
    all_to_all x1, waiting for transfers between devices, on_device(): lax.all_to_all(packed.reshape(ctx, 24, LANES), 'ctx', 0, 0, tiled=True)  15.9 us
    all_to_all x1, starting transfers between devices, on_device(): lax.all_to_all(packed.reshape(ctx, 24, LANES), 'ctx', 0, 0, tiled=True)  11.8 us
    all_to_all x1, starting transfers between devices, on_device(): shares = lax.all_to_all(everyone, 'tp', 0, 0, tiled=True)  9.86 us
    unnamed x30, local copies, waits for them, and re-layouts  6.64 us
    pallas_call x4, Pallas kernels, call(): pl.pallas_call(kernel, out_shape=out_shape, in_specs=in_specs, out_specs=...  4.33 us
  transfers between devices with their start and end apart: 2, of which 2 were waited for; matrix products, arithmetic and copies ran while one was open for 0% of the time, Pallas kernels for 1%

commit v1 on v0

v1 whole, which is shorter than its diff:
```python
import math

import jax
import jax.numpy as jnp
import ml_dtypes
import numpy as np
from jax import lax
from jax.experimental import pallas as pl
from jax.experimental.pallas import tpu as pltpu
from jax.sharding import Mesh
from jax.sharding import PartitionSpec as P

LANES = 128
SUBLANES = 8
CTX = ("chip", "core")
TP = ("tp_far", "tp_near")
VMEM_BYTES = 24 * 1024 * 1024


def split_table(table):
    high = table.astype(np.float32).astype(ml_dtypes.bfloat16)
    low = (table - high.astype(np.float64)).astype(ml_dtypes.bfloat16)
    return high, low


def make_tables(rows, blocks, scale):
    period = 2 * rows
    padded = period * LANES
    place = np.arange(rows)
    a = place % blocks * SUBLANES + place // blocks
    f1 = np.arange(rows)
    turn = 2.0 * np.pi * (np.outer(f1, a) % period) / period
    cosines = np.cos(turn)
    sines = -np.sin(turn)
    sines[0] = np.where(a % 2 == 0, 1.0, -1.0)
    outer = np.concatenate([cosines, sines], axis=0)
    weights = np.full((rows,), 2.0)
    weights[0] = 1.0
    outer_back = (outer * np.concatenate([weights, weights])[:, None]).T * (scale / padded)
    b = np.arange(LANES)
    kept = np.arange(rows + 1)
    angle = 2.0 * np.pi * (np.outer(kept, b) % padded) / padded
    twist = np.zeros((rows + 16, 2 * LANES))
    twist[: rows + 1, :LANES] = np.cos(angle)
    twist[: rows + 1, LANES:] = -np.sin(angle)
    inner = 2.0 * np.pi * (np.outer(b, b) % LANES) / LANES
    c, s = np.cos(inner), np.sin(inner)
    inner_there = np.block([[c, -s], [s, c]])
    inner_back = np.block([[c, s], [-s, c]])
    back_columns = np.concatenate(np.split(outer_back, 2 * rows // (2 * LANES), axis=1), axis=0)
    stacked = np.concatenate([outer, inner_there, inner_back, back_columns], axis=0)
    high, low = split_table(stacked)
    return np.stack([high, low]), twist.astype(np.float32)


def split(x):
    high = x.astype(jnp.bfloat16)
    low = (x - high.astype(jnp.float32)).astype(jnp.bfloat16)
    return high, low


def dot(x, y):
    return jnp.dot(x, y, preferred_element_type=jnp.float32)


def pack_kernel(
    signal_hbm, grad_hbm, filter_hbm, table_hbm, twist_hbm, out_ref, table_ref, twist_ref, signal_ref, grad_ref, filter_ref, sems
):
    pairs = (
        (signal_hbm, signal_ref),
        (grad_hbm, grad_ref),
        (filter_hbm, filter_ref),
        (table_hbm, table_ref),
        (twist_hbm, twist_ref),
    )
    copies = [pltpu.make_async_copy(source, target, sems.at[k]) for k, (source, target) in enumerate(pairs)]
    for copy in copies:
        copy.start()
    channels = signal_ref.shape[0]

    def put(core, w, chunk, array):
        out_ref[pl.ds(core * 12 + w, channels, stride=24), :] = array[:, chunk * LANES : (chunk + 1) * LANES]

    for core, ref in enumerate((signal_ref, grad_ref)):
        copies[core].wait()
        array = ref[...].astype(jnp.float32)
        for chunk in range(SUBLANES):
            put(core, chunk, chunk, array)
    copies[2].wait()
    taps = filter_ref[...]
    for chunk in range(SUBLANES):
        put(chunk // 4, 8 + chunk % 4, chunk, taps)
    for copy in copies[3:]:
        copy.wait()


def convolve_kernel(core_ref, in_ref, table, twist, out_ref, a_ref, u_h, u_l):
    blocks = in_ref.shape[0] // 24
    rows = blocks * SUBLANES
    on_second = core_ref[0] == 1
    sign = jnp.where(on_second, -1.0, 1.0)

    def part(number, start, count):
        return table[number, start : start + count, :]

    def chunk(core, w):
        return in_ref[pl.ds(core * blocks * 12 + w, blocks, stride=12), :]

    signal = jnp.concatenate([chunk(0, w) for w in range(8)], axis=0)
    grad = jnp.concatenate([chunk(1, w) for w in range(8)], axis=0)
    taps = jnp.concatenate([chunk(core, 8 + w) for core in range(2) for w in range(4)], axis=0)
    both = jnp.concatenate([signal, grad], axis=1).astype(jnp.bfloat16)
    taps_h, taps_l = split(taps)
    outer_h, outer_l = part(0, 0, 2 * rows), part(1, 0, 2 * rows)
    a_ref[:, : 2 * LANES] = dot(outer_h, both) + dot(outer_l, both)
    turned = dot(outer_h, jnp.concatenate([taps_h, taps_l], axis=1))
    a_ref[:, 2 * LANES :] = turned[:, :LANES] + turned[:, LANES:] + dot(outer_l, taps_h)
    at = 2 * rows
    there_h, there_l = part(0, at, 2 * LANES), part(1, at, 2 * LANES)
    at += 2 * LANES
    back_h, back_l = part(0, at, 2 * LANES), part(1, at, 2 * LANES)
    at += 2 * LANES

    last = a_ref[rows : rows + 1, :]
    first_row = lax.broadcasted_iota(jnp.int32, (16, 1), 0) == 0

    for start, count in ((0, rows // 2), (rows // 2, rows // 2), (rows, 16)):
        tr = twist[start : start + count, :LANES]
        ti = twist[start : start + count, LANES:]
        pieces = []
        for number in range(3):
            lanes = slice(number * LANES, (number + 1) * LANES)
            if start == rows:
                ar = jnp.where(first_row, last[:, lanes], 0.0)
                pieces.append(jnp.concatenate([ar * tr, ar * ti], axis=1))
                continue
            ar = a_ref[start : start + count, lanes]
            ai = a_ref[rows + start : rows + start + count, lanes]
            if start == 0:
                row = lax.broadcasted_iota(jnp.int32, (count, 1), 0)
                ai = jnp.where(row == 0, 0.0, ai)
            pieces.append(jnp.concatenate([ar * tr - ai * ti, ar * ti + ai * tr], axis=1))
        z_h, z_l = split(jnp.concatenate(pieces, axis=0))
        spec = dot(z_h, there_h) + dot(z_l, there_h) + dot(z_h, there_l)
        sr, si = spec[:count, :LANES], spec[:count, LANES:]
        gr, gi = spec[count : 2 * count, :LANES], spec[count : 2 * count, LANES:]
        hr, hi = spec[2 * count :, :LANES], spec[2 * count :, LANES:] * sign
        mr, mi = jnp.where(on_second, gr, sr), jnp.where(on_second, gi, si)
        conv = jnp.concatenate([mr * hr - mi * hi, mr * hi + mi * hr], axis=1)
        corr = jnp.concatenate([gr * sr + gi * si, gi * sr - gr * si], axis=1)
        p_h, p_l = split(jnp.concatenate([conv, corr], axis=0))
        v = dot(p_h, back_h) + dot(p_l, back_h) + dot(p_h, back_l)
        for number in range(2):
            vr = v[number * count : (number + 1) * count, :LANES]
            vi = v[number * count : (number + 1) * count, LANES:]
            lanes = slice(number * LANES, (number + 1) * LANES)
            real_h, real_l = split(vr * tr + vi * ti)
            if start == rows:
                u_h[rows : rows + 16, lanes] = jnp.where(first_row, real_h, u_h[rows : rows + 16, lanes])
                u_l[rows : rows + 16, lanes] = jnp.where(first_row, real_l, u_l[rows : rows + 16, lanes])
                continue
            imag_h, imag_l = split(vi * tr - vr * ti)
            u_h[start : start + count, lanes] = real_h
            u_l[start : start + count, lanes] = real_l
            u_h[rows + start : rows + start + count, lanes] = imag_h
            u_l[rows + start : rows + start + count, lanes] = imag_l

    y = jnp.zeros((rows, 2 * LANES), jnp.float32)
    for inner in range(0, 2 * rows, 2 * LANES):
        here = slice(inner, inner + 2 * LANES)
        columns_h, columns_l = part(0, at, rows), part(1, at, rows)
        y += dot(columns_h, u_h[here, :]) + dot(columns_h, u_l[here, :]) + dot(columns_l, u_h[here, :])
        at += rows
    half = rows // 2
    corr = jnp.where(on_second, y[half:, LANES:], y[:half, LANES:])
    for w in range(8):
        out_ref[pl.ds(w, blocks, stride=12), :] = y[w * blocks : (w + 1) * blocks, :LANES]
    for w in range(4):
        out_ref[pl.ds(8 + w, blocks, stride=12), :] = corr[w * blocks : (w + 1) * blocks]


def collect_kernel(in_ref, corr_ref):
    channels = corr_ref.shape[0]
    for chunk in range(SUBLANES):
        start = chunk // 4 * 12 + 8 + chunk % 4
        corr_ref[:, chunk * LANES : (chunk + 1) * LANES] = in_ref[pl.ds(start, channels, stride=24), :]


def add_kernel(in_ref, out_ref):
    total = in_ref[0] + in_ref[1]
    for place in range(out_ref.shape[0]):
        out_ref[place] = total


def finish_kernel(in_ref, gain_ref, signal_ref, grad_ref, out_ref, back_ref):
    channels = signal_ref.shape[0]
    gains = gain_ref[...]
    for chunk in range(SUBLANES):
        lanes = slice(chunk * LANES, (chunk + 1) * LANES)
        for core, (own, result) in enumerate(((signal_ref, out_ref), (grad_ref, back_ref))):
            conv = in_ref[pl.ds(core * 12 + chunk, channels, stride=24), :]
            result[:, lanes] = (conv + gains * own[:, lanes].astype(jnp.float32)).astype(jnp.bfloat16)


def call(kernel, out_shape, operands, scratch=(), spaces=None):
    if spaces is None:
        spaces = [pltpu.VMEM] * len(operands)
    return pl.pallas_call(
        kernel,
        out_shape=out_shape,
        in_specs=[pl.BlockSpec(memory_space=space) for space in spaces],
        out_specs=jax.tree.map(lambda _: pl.BlockSpec(memory_space=pltpu.VMEM), out_shape),
        scratch_shapes=list(scratch),
        compiler_params=pltpu.CompilerParams(vmem_limit_bytes=VMEM_BYTES),
    )(*operands)


def on_device(signal, filter_taps, skip_gain, grad_out):
    channels, tokens = signal.shape
    ctx = lax.axis_size(CTX)
    length = tokens * ctx
    rows = length // LANES
    table, twist = make_tables(rows, ctx, 1.0 / math.sqrt(length))
    core = lax.axis_index("core").astype(jnp.int32).reshape(1)

    in_hbm = [pltpu.with_memory_space_constraint(x, pltpu.HBM) for x in (signal, grad_out, filter_taps, table, twist)]
    packed, table, twist = call(
        pack_kernel,
        (
            pltpu.VMEM((ctx * 12, LANES), jnp.float32),
            pltpu.VMEM(table.shape, table.dtype),
            pltpu.VMEM(twist.shape, twist.dtype),
        ),
        in_hbm,
        scratch=(
            pltpu.VMEM(signal.shape, signal.dtype),
            pltpu.VMEM(grad_out.shape, grad_out.dtype),
            pltpu.VMEM(filter_taps.shape, filter_taps.dtype),
            pltpu.SemaphoreType.DMA((5,)),
        ),
        spaces=[pltpu.HBM] * 5,
    )
    spread = lax.all_to_all(packed.reshape(ctx * 3, 4, LANES), CTX, 0, 0, tiled=True)
    sequences = lax.all_gather(spread, "core", tiled=True).reshape(ctx * 24, LANES)
    results = call(
        convolve_kernel,
        jax.ShapeDtypeStruct((ctx * 12, LANES), jnp.float32),
        (core, sequences, table, twist),
        scratch=(
            pltpu.VMEM((2 * rows, 3 * LANES), jnp.float32),
            pltpu.VMEM((2 * rows, 2 * LANES), jnp.bfloat16),
            pltpu.VMEM((2 * rows, 2 * LANES), jnp.bfloat16),
        ),
        spaces=[pltpu.SMEM] + [pltpu.VMEM] * 3,
    )
    returned = lax.all_to_all(results.reshape(ctx * 3, 4, LANES), CTX, 0, 0, tiled=True)
    returned = returned.reshape(ctx * 12, LANES)
    corr = call(collect_kernel, jax.ShapeDtypeStruct((channels, tokens), jnp.float32), (returned,))
    pair = lax.all_gather(corr, "tp_far")
    near = lax.axis_size("tp_near")
    everyone = call(add_kernel, jax.ShapeDtypeStruct((near, channels, tokens), jnp.float32), (pair,))
    shares = lax.all_to_all(everyone, "tp_near", 0, 0, tiled=True)
    grad_filter = jnp.sum(shares, axis=0)
    output, grad_signal = call(
        finish_kernel,
        (
            jax.ShapeDtypeStruct((channels, tokens), jnp.bfloat16),
            jax.ShapeDtypeStruct((channels, tokens), jnp.bfloat16),
        ),
        (returned, skip_gain[:, None], signal, grad_out),
    )
    return (output, grad_signal, grad_filter)


def solution(mesh):
    ctx, tp = mesh.shape["ctx"], mesh.shape["tp"]
    far = 2 if tp % 2 == 0 else 1
    parted = Mesh(mesh.devices.reshape(ctx // 2, 2, far, tp // far), ("chip", "core", "tp_far", "tp_near"))
    in_specs = (P(TP, CTX), P(None, CTX), P(TP), P(TP, CTX))
    out_specs = (P(TP, CTX), P(TP, CTX), P(None, CTX))
    return jax.shard_map(
        on_device, mesh=parted, in_specs=in_specs, out_specs=out_specs, check_vma=False
    )
```

time: 93.4 us -> 76.2 us (0.82)
  the two profiles are of different devices: /device:TPU:8 before, /device:TPU:4 now
where the time goes in v1:
time: 76.2 us; the launch traced here: 75.8 us
  waiting for transfers between devices  26.2 us (34%)
  blocking collectives  23.4 us (31%)
  starting transfers between devices  18.5 us (24%)
  Pallas kernels  6.3 us (8%)
    all_to_all x1, blocking collectives, on_device(): lax.all_to_all(results.reshape(ctx * 3, 4, LANES), CTX, 0, 0, tiled=True)  14.9 us
    all_to_all x1, waiting for transfers between devices, on_device(): shares = lax.all_to_all(everyone, 'tp_near', 0, 0, tiled=True)  14.4 us
    all_to_all x1, waiting for transfers between devices, on_device(): lax.all_to_all(packed.reshape(ctx * 3, 4, LANES), CTX, 0, 0, tiled=True)  11.8 us
    all_to_all x1, starting transfers between devices, on_device(): lax.all_to_all(packed.reshape(ctx * 3, 4, LANES), CTX, 0, 0, tiled=True)  11.4 us
    all_to_all x1, starting transfers between devices, on_device(): shares = lax.all_to_all(everyone, 'tp_near', 0, 0, tiled=True)  7.1 us
    all_gather x1, blocking collectives, on_device(): pair = lax.all_gather(corr, 'tp_far')  6.45 us
    pallas_call x5, Pallas kernels, call(): pl.pallas_call(kernel, out_shape=out_shape, in_specs=[pl.BlockSpec(memory...  6.3 us
    all_gather x1, blocking collectives, on_device(): lax.all_gather(spread, 'core', tiled=True).reshape(ctx * 24, LANES)  2.08 us
  transfers between devices with their start and end apart: 2, of which 2 were waited for; matrix products, arithmetic and copies ran while one was open for 0% of the time, Pallas kernels for 1%

profile of v1, /device:TPU:4, one launch (start us, length us, event | category | flops | bytes accessed | tf_op | source)
XLA Modules:
  0.0 75.8 jit_solution(16054288373636891591)
XLA Ops:
  0.6 2.2 %shard_map.85 = (f32[384,128]{1,0:T(8,128)}, bf16[2,1536,256]{2,1,0:T(8,128)(2,1)S(1)}, f32[272,256]{1,0:T(8,128)S(1)}) custom-call(bf16[16,1024]{1,0:T(8,128)(2,1)} %signal_ref.1, bf16[16,1024]{1,0:T(8,128)(2,1)} %grad_ref.1, f32[16,1024]{1,0:T(8,128)} %filter_hbm.1, bf16[2,1536,256]{2,1,0:T(8,128)(2,1)} %constant.12.clone.table_hbm, ...), custom_call_target="tpu_custom_call" | custom-call | tf_op jit(solution)/shard_map/pallas_call | solution.py:208
  2.9 11.4 %all-to-all-start = ((f32[96,4,128]{2,1,0:T(4,128)}), f32[96,4,128]{2,1,0:T(4,128)S(1)}, u32[]{:S(2)}, u32[]{:S(2)}) async-start(f32[96,4,128]{2,1,0:T(4,128)} %bitcast.1), calls=%async_computation | async-start | bytes 393216 | tf_op jit(solution)/shard_map/all_to_all | solution.py:243
  14.2 11.8 %all-to-all-done = f32[96,4,128]{2,1,0:T(4,128)S(1)} async-done(((f32[96,4,128]{2,1,0:T(4,128)}), f32[96,4,128]{2,1,0:T(4,128)S(1)}, u32[]{:S(2)}, u32[]{:S(2)}) %all-to-all-start) | async-done | bytes 196640 | tf_op jit(solution)/shard_map/all_to_all | solution.py:243
  26.0 2.1 %all_gather.9 = f32[192,4,128]{2,1,0:T(4,128)S(1)} all-gather(f32[96,4,128]{2,1,0:T(4,128)S(1)} %all-to-all-done), channel_id=1, replica_groups=mesh['chip'=16,'core'=2,'tp_far'=2,'tp_near'=8] {'core'}, dimensions={0}, use_global_device_ids=true | all-gather | bytes 589824 | tf_op jit(solution)/shard_map/all_gather | solution.py:244
  28.1 2.5 %shard_map.86 = f32[384,128]{1,0:T(8,128)S(1)} custom-call(s32[1]{0:T(128)} %bitcast.core_ref, f32[768,128]{1,0:T(8,128)S(1)} %bitcast.9, bf16[2,1536,256]{2,1,0:T(8,128)(2,1)S(1)} %get-tuple-element.9.table, f32[272,256]{1,0:T(8,128)S(1)} %get-tuple-element.10.twist), custom_call_target="tpu_custom_call" | custom-call | tf_op jit(solution)/shard_map/pallas_call | solution.py:208
  30.6 0.0 copy-start.2
  30.6 0.0 copy-start
  30.7 0.0 copy-start.1
  30.7 14.9 %all_to_all.15 = f32[96,4,128]{2,1,0:T(4,128)S(1)} all-to-all(f32[96,4,128]{2,1,0:T(4,128)S(1)} %bitcast.10), channel_id=1, replica_groups=mesh['chip'=16,'core'=2,'tp_far'=2,'tp_near'=8] {'chip','core'}, dimensions={0} | all-to-all | bytes 393216 | tf_op jit(solution)/shard_map/all_to_all | solution.py:256
  45.6 6.4 %all-gather = f32[32,1024]{1,0:T(8,128)S(1)} all-gather(f32[16,1024]{1,0:T(8,128)S(1)} %shard_map.88), channel_id=2, replica_groups=mesh['chip'=16,'core'=2,'tp_far'=2,'tp_near'=8] {'tp_far'}, dimensions={0}, use_global_device_ids=true | all-gather | bytes 196608 | tf_op jit(solution)/shard_map/all_gather | solution.py:259
  52.1 0.8 %shard_map.89 = f32[8,16,1024]{2,1,0:T(8,128)} custom-call(f32[2,16,1024]{2,1,0:T(8,128)S(1)} %bitcast.11), custom_call_target="tpu_custom_call" | custom-call | tf_op jit(solution)/shard_map/pallas_call | solution.py:208
  52.9 7.1 %all-to-all-start.2 = ((f32[8,16,1024]{2,1,0:T(8,128)}), f32[8,16,1024]{2,1,0:T(8,128)S(1)}, u32[]{:S(2)}, u32[]{:S(2)}) async-start(f32[8,16,1024]{2,1,0:T(8,128)} %shard_map.89), calls=%async_computation.2 | async-start | bytes 1048576 | tf_op jit(solution)/shard_map/all_to_all | solution.py:262
  60.0 0.0 copy-done.2
  60.0 0.1 copy.10.gain_ref
  60.1 0.0 copy-done
  60.1 0.0 copy-done.1
  60.1 0.7 shard_map.87
  60.8 14.4 %all-to-all-done.2 = f32[8,16,1024]{2,1,0:T(8,128)S(1)} async-done(((f32[8,16,1024]{2,1,0:T(8,128)}), f32[8,16,1024]{2,1,0:T(8,128)S(1)}, u32[]{:S(2)}, u32[]{:S(2)}) %all-to-all-start.2) | async-done | bytes 524320 | tf_op jit(solution)/shard_map/all_to_all | solution.py:262
  75.2 0.7 reduce_sum.9
  (1 shorter events, 0.0 us)
Async XLA Ops:
  2.9 23.2 %all-to-all-start = ((f32[96,4,128]{2,1,0:T(4,128)}), f32[96,4,128]{2,1,0:T(4,128)S(1)}, u32[]{:S(2)}, u32[]{:S(2)}) async-start(f32[96,4,128]{2,1,0:T(4,128)} %bitcast.1), calls=%async_computation | async-start | bytes 393216 | tf_op jit(solution)/shard_map/all_to_all | solution.py:243
  30.6 29.4 %copy-start.2 = (f32[16]{0:T(128)S(1)}, f32[16]{0:T(128)}, u32[]{:S(2)}) copy-start(f32[16]{0:T(128)} %param.8) | copy-start | bytes 196
  30.6 29.4 %copy-start = (bf16[16,1024]{1,0:T(8,128)(2,1)S(1)}, bf16[16,1024]{1,0:T(8,128)(2,1)}, u32[]{:S(2)}) copy-start(bf16[16,1024]{1,0:T(8,128)(2,1)} %signal_ref.1) | copy-start | bytes 98308
  30.7 29.4 %copy-start.1 = (bf16[16,1024]{1,0:T(8,128)(2,1)S(1)}, bf16[16,1024]{1,0:T(8,128)(2,1)}, u32[]{:S(2)}) copy-start(bf16[16,1024]{1,0:T(8,128)(2,1)} %grad_ref.1) | copy-start | bytes 98308
  52.9 22.3 %all-to-all-start.2 = ((f32[8,16,1024]{2,1,0:T(8,128)}), f32[8,16,1024]{2,1,0:T(8,128)S(1)}, u32[]{:S(2)}, u32[]{:S(2)}) async-start(f32[8,16,1024]{2,1,0:T(8,128)} %shard_map.89), calls=%async_computation.2 | async-start | bytes 1048576 | tf_op jit(solution)/shard_map/all_to_all | solution.py:262

commit v2 on v1

--- a/solution.py
+++ b/solution.py
@@ -186,13 +186,12 @@
         corr_ref[:, chunk * LANES : (chunk + 1) * LANES] = in_ref[pl.ds(start, channels, stride=24), :]
 
 
-def add_kernel(in_ref, out_ref):
-    total = in_ref[0] + in_ref[1]
-    for place in range(out_ref.shape[0]):
-        out_ref[place] = total
-
-
-def finish_kernel(in_ref, gain_ref, signal_ref, grad_ref, out_ref, back_ref):
+def finish_kernel(pair_ref, in_ref, gain_ref, signal_ref, grad_ref, everyone_ref, out_ref, back_ref):
+    total = pair_ref[0]
+    for place in range(1, pair_ref.shape[0]):
+        total += pair_ref[place]
+    for place in range(everyone_ref.shape[0]):
+        everyone_ref[place] = total
     channels = signal_ref.shape[0]
     gains = gain_ref[...]
     for chunk in range(SUBLANES):
@@ -258,17 +257,17 @@
     corr = call(collect_kernel, jax.ShapeDtypeStruct((channels, tokens), jnp.float32), (returned,))
     pair = lax.all_gather(corr, "tp_far")
     near = lax.axis_size("tp_near")
-    everyone = call(add_kernel, jax.ShapeDtypeStruct((near, channels, tokens), jnp.float32), (pair,))
+    everyone, output, grad_signal = call(
+        finish_kernel,
+        (
+            jax.ShapeDtypeStruct((near, channels, tokens), jnp.float32),
+            jax.ShapeDtypeStruct((channels, tokens), jnp.bfloat16),
+            jax.ShapeDtypeStruct((channels, tokens), jnp.bfloat16),
+        ),
+        (pair, returned, skip_gain[:, None], signal, grad_out),
+    )
     shares = lax.all_to_all(everyone, "tp_near", 0, 0, tiled=True)
     grad_filter = jnp.sum(shares, axis=0)
-    output, grad_signal = call(
-        finish_kernel,
-        (
-            jax.ShapeDtypeStruct((channels, tokens), jnp.bfloat16),
-            jax.ShapeDtypeStruct((channels, tokens), jnp.bfloat16),
-        ),
-        (returned, skip_gain[:, None], signal, grad_out),
-    )
     return (output, grad_signal, grad_filter)
 
 

time: 76.2 us -> 77.2 us (1.013)
  blocking collectives: 23.4 us -> 30.6 us
  starting transfers between devices: 18.5 us -> 15.2 us
  waiting for transfers between devices: 26.2 us -> 23.5 us
    all_to_all x1, blocking collectives: 14.9 us -> 22.1 us  [on_device(): shares = lax.all_to_all(everyone, 'tp_near', 0, 0, tiled=True)]
    all_to_all x1, starting transfers between devices: 7.1 us -> 3.86 us  [on_device(): lax.all_to_all(results.reshape(ctx * 3, 4, LANES), CTX, 0, 0, tiled=True)]
    all_to_all x1, waiting for transfers between devices: 14.4 us -> 11.7 us  [on_device(): lax.all_to_all(results.reshape(ctx * 3, 4, LANES), CTX, 0, 0, tiled=True)]
    pallas_call x5 -> x4, Pallas kernels: 6.3 us -> 6.14 us  [call(): pl.pallas_call(kernel, out_shape=out_shape, in_specs=[pl.BlockSpec(memory...]
  transfers between devices with their start and end apart: 2 -> 2, of which waited for: 2 -> 2; matrix products, arithmetic and copies ran while one was open for 0% -> 0% of each run, Pallas kernels for 1% -> 0%
where the time goes in v2:
time: 77.2 us; the launch traced here: 76.9 us
  blocking collectives  30.6 us (40%)
  waiting for transfers between devices  23.5 us (30%)
  starting transfers between devices  15.2 us (20%)
  Pallas kernels  6.14 us (8%)
    all_to_all x1, blocking collectives, on_device(): shares = lax.all_to_all(everyone, 'tp_near', 0, 0, tiled=True)  22.1 us
    all_to_all x1, waiting for transfers between devices, on_device(): lax.all_to_all(packed.reshape(ctx * 3, 4, LANES), CTX, 0, 0, tiled=True)  11.8 us
    all_to_all x1, waiting for transfers between devices, on_device(): lax.all_to_all(results.reshape(ctx * 3, 4, LANES), CTX, 0, 0, tiled=True)  11.7 us
    all_to_all x1, starting transfers between devices, on_device(): lax.all_to_all(packed.reshape(ctx * 3, 4, LANES), CTX, 0, 0, tiled=True)  11.4 us
    all_gather x1, blocking collectives, on_device(): pair = lax.all_gather(corr, 'tp_far')  6.45 us
    pallas_call x4, Pallas kernels, call(): pl.pallas_call(kernel, out_shape=out_shape, in_specs=[pl.BlockSpec(memory...  6.14 us
    all_to_all x1, starting transfers between devices, on_device(): lax.all_to_all(results.reshape(ctx * 3, 4, LANES), CTX, 0, 0, tiled=True)  3.86 us
    all_gather x1, blocking collectives, on_device(): lax.all_gather(spread, 'core', tiled=True).reshape(ctx * 24, LANES)  2.08 us
  transfers between devices with their start and end apart: 2, of which 2 were waited for; matrix products, arithmetic and copies ran while one was open for 0% of the time, Pallas kernels for 0%

profile of v2, /device:TPU:4, one launch (start us, length us, event | category | flops | bytes accessed | tf_op | source)
XLA Modules:
  0.0 76.9 jit_solution(270940685375831138)
XLA Ops:
  0.6 2.2 %shard_map.85 = (f32[384,128]{1,0:T(8,128)}, bf16[2,1536,256]{2,1,0:T(8,128)(2,1)S(1)}, f32[272,256]{1,0:T(8,128)S(1)}) custom-call(bf16[16,1024]{1,0:T(8,128)(2,1)} %signal_ref.1, bf16[16,1024]{1,0:T(8,128)(2,1)} %grad_ref.1, f32[16,1024]{1,0:T(8,128)} %filter_hbm.1, bf16[2,1536,256]{2,1,0:T(8,128)(2,1)} %constant.12.clone.table_hbm, ...), custom_call_target="tpu_custom_call" | custom-call | tf_op jit(solution)/shard_map/pallas_call | solution.py:207
  2.9 11.4 %all-to-all-start = ((f32[96,4,128]{2,1,0:T(4,128)}), f32[96,4,128]{2,1,0:T(4,128)S(1)}, u32[]{:S(2)}, u32[]{:S(2)}) async-start(f32[96,4,128]{2,1,0:T(4,128)} %bitcast.1), calls=%async_computation | async-start | bytes 393216 | tf_op jit(solution)/shard_map/all_to_all | solution.py:242
  14.2 0.0 copy-start.2
  14.2 11.8 %all-to-all-done = f32[96,4,128]{2,1,0:T(4,128)S(1)} async-done(((f32[96,4,128]{2,1,0:T(4,128)}), f32[96,4,128]{2,1,0:T(4,128)S(1)}, u32[]{:S(2)}, u32[]{:S(2)}) %all-to-all-start) | async-done | bytes 196640 | tf_op jit(solution)/shard_map/all_to_all | solution.py:242
  26.0 2.1 %all_gather.9 = f32[192,4,128]{2,1,0:T(4,128)S(1)} all-gather(f32[96,4,128]{2,1,0:T(4,128)S(1)} %all-to-all-done), channel_id=1, replica_groups=mesh['chip'=16,'core'=2,'tp_far'=2,'tp_near'=8] {'core'}, dimensions={0}, use_global_device_ids=true | all-gather | bytes 589824 | tf_op jit(solution)/shard_map/all_gather | solution.py:243
  28.1 0.0 copy-start
  28.1 0.0 copy-start.1
  28.1 3.2 %shard_map.86 = f32[384,128]{1,0:T(8,128)} custom-call(s32[1]{0:T(128)} %bitcast.core_ref, f32[768,128]{1,0:T(8,128)S(1)} %bitcast.9, bf16[2,1536,256]{2,1,0:T(8,128)(2,1)S(1)} %get-tuple-element.10.table, f32[272,256]{1,0:T(8,128)S(1)} %get-tuple-element.11.twist), custom_call_target="tpu_custom_call" | custom-call | tf_op jit(solution)/shard_map/pallas_call | solution.py:207
  31.3 3.9 %all-to-all-start.1 = ((f32[96,4,128]{2,1,0:T(4,128)}), f32[96,4,128]{2,1,0:T(4,128)S(1)}, u32[]{:S(2)}, u32[]{:S(2)}) async-start(f32[96,4,128]{2,1,0:T(4,128)} %bitcast.3), calls=%async_computation.1 | async-start | bytes 393216 | tf_op jit(solution)/shard_map/all_to_all | solution.py:255
  35.2 0.0 copy-done.2
  35.2 0.1 copy.10.gain_ref
  35.3 11.7 %all-to-all-done.1 = f32[96,4,128]{2,1,0:T(4,128)S(1)} async-done(((f32[96,4,128]{2,1,0:T(4,128)}), f32[96,4,128]{2,1,0:T(4,128)S(1)}, u32[]{:S(2)}, u32[]{:S(2)}) %all-to-all-start.1) | async-done | bytes 196640 | tf_op jit(solution)/shard_map/all_to_all | solution.py:255
  47.0 6.4 %all-gather = f32[32,1024]{1,0:T(8,128)S(1)} all-gather(f32[16,1024]{1,0:T(8,128)S(1)} %shard_map.87), channel_id=2, replica_groups=mesh['chip'=16,'core'=2,'tp_far'=2,'tp_near'=8] {'tp_far'}, dimensions={0}, use_global_device_ids=true | all-gather | bytes 196608 | tf_op jit(solution)/shard_map/all_gather | solution.py:258
  53.5 0.0 copy-done
  53.5 0.0 copy-done.1
  53.5 0.7 shard_map.88
  54.2 22.1 %all_to_all.15 = f32[8,16,1024]{2,1,0:T(8,128)S(1)} all-to-all(f32[8,16,1024]{2,1,0:T(8,128)S(1)} %get-tuple-element.14), channel_id=1, replica_groups=mesh['chip'=16,'core'=2,'tp_far'=2,'tp_near'=8] {'tp_near'}, dimensions={0} | all-to-all | bytes 1048576 | tf_op jit(solution)/shard_map/all_to_all | solution.py:269
  76.2 0.7 reduce_sum.9
  (1 shorter events, 0.0 us)
Async XLA Ops:
  2.9 23.2 %all-to-all-start = ((f32[96,4,128]{2,1,0:T(4,128)}), f32[96,4,128]{2,1,0:T(4,128)S(1)}, u32[]{:S(2)}, u32[]{:S(2)}) async-start(f32[96,4,128]{2,1,0:T(4,128)} %bitcast.1), calls=%async_computation | async-start | bytes 393216 | tf_op jit(solution)/shard_map/all_to_all | solution.py:242
  14.2 21.0 %copy-start.2 = (f32[16]{0:T(128)S(1)}, f32[16]{0:T(128)}, u32[]{:S(2)}) copy-start(f32[16]{0:T(128)} %param.8) | copy-start | bytes 196
  28.1 25.4 %copy-start = (bf16[16,1024]{1,0:T(8,128)(2,1)S(1)}, bf16[16,1024]{1,0:T(8,128)(2,1)}, u32[]{:S(2)}) copy-start(bf16[16,1024]{1,0:T(8,128)(2,1)} %signal_ref.1) | copy-start | bytes 98308
  28.1 25.4 %copy-start.1 = (bf16[16,1024]{1,0:T(8,128)(2,1)S(1)}, bf16[16,1024]{1,0:T(8,128)(2,1)}, u32[]{:S(2)}) copy-start(bf16[16,1024]{1,0:T(8,128)(2,1)} %grad_ref.1) | copy-start | bytes 98308
  31.3 15.7 %all-to-all-start.1 = ((f32[96,4,128]{2,1,0:T(4,128)}), f32[96,4,128]{2,1,0:T(4,128)S(1)}, u32[]{:S(2)}, u32[]{:S(2)}) async-start(f32[96,4,128]{2,1,0:T(4,128)} %bitcast.3), calls=%async_computation.1 | async-start | bytes 393216 | tf_op jit(solution)/shard_map/all_to_all | solution.py:255

commit v3 on v1

--- a/solution.py
+++ b/solution.py
@@ -27,7 +27,8 @@
     period = 2 * rows
     padded = period * LANES
     place = np.arange(rows)
-    a = place % blocks * SUBLANES + place // blocks
+    block = place // SUBLANES % (blocks // 2) * 2 + place // (rows // 2)
+    a = block * SUBLANES + place % SUBLANES
     f1 = np.arange(rows)
     turn = 2.0 * np.pi * (np.outer(f1, a) % period) / period
     cosines = np.cos(turn)
@@ -77,40 +78,29 @@
     for copy in copies:
         copy.start()
     channels = signal_ref.shape[0]
-
-    def put(core, w, chunk, array):
-        out_ref[pl.ds(core * 12 + w, channels, stride=24), :] = array[:, chunk * LANES : (chunk + 1) * LANES]
-
-    for core, ref in enumerate((signal_ref, grad_ref)):
-        copies[core].wait()
+    for number, ref in enumerate((signal_ref, grad_ref, filter_ref)):
+        copies[number].wait()
         array = ref[...].astype(jnp.float32)
         for chunk in range(SUBLANES):
-            put(core, chunk, chunk, array)
-    copies[2].wait()
-    taps = filter_ref[...]
-    for chunk in range(SUBLANES):
-        put(chunk // 4, 8 + chunk % 4, chunk, taps)
+            out_ref[pl.ds(number * 8 + chunk, channels, stride=24), :] = array[:, chunk * LANES : (chunk + 1) * LANES]
     for copy in copies[3:]:
         copy.wait()
 
 
 def convolve_kernel(core_ref, in_ref, table, twist, out_ref, a_ref, u_h, u_l):
-    blocks = in_ref.shape[0] // 24
-    rows = blocks * SUBLANES
-    on_second = core_ref[0] == 1
-    sign = jnp.where(on_second, -1.0, 1.0)
+    chips = out_ref.shape[0]
+    half = chips * SUBLANES
+    rows = 2 * half
+    core = core_ref[0]
 
     def part(number, start, count):
         return table[number, start : start + count, :]
 
-    def chunk(core, w):
-        return in_ref[pl.ds(core * blocks * 12 + w, blocks, stride=12), :]
-
-    signal = jnp.concatenate([chunk(0, w) for w in range(8)], axis=0)
-    grad = jnp.concatenate([chunk(1, w) for w in range(8)], axis=0)
-    taps = jnp.concatenate([chunk(core, 8 + w) for core in range(2) for w in range(4)], axis=0)
-    both = jnp.concatenate([signal, grad], axis=1).astype(jnp.bfloat16)
-    taps_h, taps_l = split(taps)
+    def sequence(number):
+        return in_ref[:, number * 8 : number * 8 + 8, :].reshape(rows, LANES)
+
+    both = jnp.concatenate([sequence(0), sequence(1)], axis=1).astype(jnp.bfloat16)
+    taps_h, taps_l = split(sequence(2))
     outer_h, outer_l = part(0, 0, 2 * rows), part(1, 0, 2 * rows)
     a_ref[:, : 2 * LANES] = dot(outer_h, both) + dot(outer_l, both)
     turned = dot(outer_h, jnp.concatenate([taps_h, taps_l], axis=1))
@@ -144,13 +134,13 @@
         spec = dot(z_h, there_h) + dot(z_l, there_h) + dot(z_h, there_l)
         sr, si = spec[:count, :LANES], spec[:count, LANES:]
         gr, gi = spec[count : 2 * count, :LANES], spec[count : 2 * count, LANES:]
-        hr, hi = spec[2 * count :, :LANES], spec[2 * count :, LANES:] * sign
-        mr, mi = jnp.where(on_second, gr, sr), jnp.where(on_second, gi, si)
-        conv = jnp.concatenate([mr * hr - mi * hi, mr * hi + mi * hr], axis=1)
+        hr, hi = spec[2 * count :, :LANES], spec[2 * count :, LANES:]
+        conv = jnp.concatenate([sr * hr - si * hi, sr * hi + si * hr], axis=1)
+        back = jnp.concatenate([gr * hr + gi * hi, gi * hr - gr * hi], axis=1)
         corr = jnp.concatenate([gr * sr + gi * si, gi * sr - gr * si], axis=1)
-        p_h, p_l = split(jnp.concatenate([conv, corr], axis=0))
+        p_h, p_l = split(jnp.concatenate([conv, back, corr], axis=0))
         v = dot(p_h, back_h) + dot(p_l, back_h) + dot(p_h, back_l)
-        for number in range(2):
+        for number in range(3):
             vr = v[number * count : (number + 1) * count, :LANES]
             vi = v[number * count : (number + 1) * count, LANES:]
             lanes = slice(number * LANES, (number + 1) * LANES)
@@ -165,25 +155,21 @@
             u_h[rows + start : rows + start + count, lanes] = imag_h
             u_l[rows + start : rows + start + count, lanes] = imag_l
 
-    y = jnp.zeros((rows, 2 * LANES), jnp.float32)
+    y = jnp.zeros((half, 3 * LANES), jnp.float32)
     for inner in range(0, 2 * rows, 2 * LANES):
         here = slice(inner, inner + 2 * LANES)
-        columns_h, columns_l = part(0, at, rows), part(1, at, rows)
+        mine = pl.ds(pl.multiple_of(at + core * half, half), half)
+        columns_h, columns_l = table[0, mine, :], table[1, mine, :]
         y += dot(columns_h, u_h[here, :]) + dot(columns_h, u_l[here, :]) + dot(columns_l, u_h[here, :])
         at += rows
-    half = rows // 2
-    corr = jnp.where(on_second, y[half:, LANES:], y[:half, LANES:])
-    for w in range(8):
-        out_ref[pl.ds(w, blocks, stride=12), :] = y[w * blocks : (w + 1) * blocks, :LANES]
-    for w in range(4):
-        out_ref[pl.ds(8 + w, blocks, stride=12), :] = corr[w * blocks : (w + 1) * blocks]
+    for number in range(3):
+        out_ref[:, number * 8 : number * 8 + 8, :] = y[:, number * LANES : (number + 1) * LANES].reshape(chips, SUBLANES, LANES)
 
 
 def collect_kernel(in_ref, corr_ref):
     channels = corr_ref.shape[0]
     for chunk in range(SUBLANES):
-        start = chunk // 4 * 12 + 8 + chunk % 4
-        corr_ref[:, chunk * LANES : (chunk + 1) * LANES] = in_ref[pl.ds(start, channels, stride=24), :]
+        corr_ref[:, chunk * LANES : (chunk + 1) * LANES] = in_ref[pl.ds(16 + chunk, channels, stride=24), :]
 
 
 def add_kernel(in_ref, out_ref):
@@ -197,8 +183,8 @@
     gains = gain_ref[...]
     for chunk in range(SUBLANES):
         lanes = slice(chunk * LANES, (chunk + 1) * LANES)
-        for core, (own, result) in enumerate(((signal_ref, out_ref), (grad_ref, back_ref))):
-            conv = in_ref[pl.ds(core * 12 + chunk, channels, stride=24), :]
+        for number, (own, result) in enumerate(((signal_ref, out_ref), (grad_ref, back_ref))):
+            conv = in_ref[pl.ds(number * 8 + chunk, channels, stride=24), :]
             result[:, lanes] = (conv + gains * own[:, lanes].astype(jnp.float32)).astype(jnp.bfloat16)
 
 
@@ -217,7 +203,9 @@
 
 def on_device(signal, filter_taps, skip_gain, grad_out):
     channels, tokens = signal.shape
-    ctx = lax.axis_size(CTX)
+    chips = lax.axis_size("chip")
+    ctx = 2 * chips
+    assert channels == chips and tokens == SUBLANES * LANES
     length = tokens * ctx
     rows = length // LANES
     table, twist = make_tables(rows, ctx, 1.0 / math.sqrt(length))
@@ -227,7 +215,7 @@
     packed, table, twist = call(
         pack_kernel,
         (
-            pltpu.VMEM((ctx * 12, LANES), jnp.float32),
+            pltpu.VMEM((chips * 24, LANES), jnp.float32),
             pltpu.VMEM(table.shape, table.dtype),
             pltpu.VMEM(twist.shape, twist.dtype),
         ),
@@ -240,21 +228,20 @@
         ),
         spaces=[pltpu.HBM] * 5,
     )
-    spread = lax.all_to_all(packed.reshape(ctx * 3, 4, LANES), CTX, 0, 0, tiled=True)
-    sequences = lax.all_gather(spread, "core", tiled=True).reshape(ctx * 24, LANES)
+    spread = lax.all_to_all(packed.reshape(chips, 24, LANES), "chip", 0, 0, tiled=True)
+    sequences = lax.all_gather(spread, "core", tiled=True)
     results = call(
         convolve_kernel,
-        jax.ShapeDtypeStruct((ctx * 12, LANES), jnp.float32),
+        jax.ShapeDtypeStruct((chips, 24, LANES), jnp.float32),
         (core, sequences, table, twist),
         scratch=(
             pltpu.VMEM((2 * rows, 3 * LANES), jnp.float32),
-            pltpu.VMEM((2 * rows, 2 * LANES), jnp.bfloat16),
-            pltpu.VMEM((2 * rows, 2 * LANES), jnp.bfloat16),
+            pltpu.VMEM((2 * rows, 3 * LANES), jnp.bfloat16),
+            pltpu.VMEM((2 * rows, 3 * LANES), jnp.bfloat16),
         ),
         spaces=[pltpu.SMEM] + [pltpu.VMEM] * 3,
     )
-    returned = lax.all_to_all(results.reshape(ctx * 3, 4, LANES), CTX, 0, 0, tiled=True)
-    returned = returned.reshape(ctx * 12, LANES)
+    returned = lax.all_to_all(results, "chip", 0, 0, tiled=True).reshape(chips * 24, LANES)
     corr = call(collect_kernel, jax.ShapeDtypeStruct((channels, tokens), jnp.float32), (returned,))
     pair = lax.all_gather(corr, "tp_far")
     near = lax.axis_size("tp_near")

time: 76.2 us -> 71.2 us (0.934)
  the two profiles are of different devices: /device:TPU:4 before, /device:TPU:66 now
where the time goes in v3:
time: 71.2 us; the launch traced here: 70.8 us
  waiting for transfers between devices  23.7 us (33%)
  blocking collectives  22 us (31%)
  starting transfers between devices  18 us (25%)
  Pallas kernels  5.71 us (8%)
    all_to_all x1, waiting for transfers between devices, on_device(): shares = lax.all_to_all(everyone, 'tp_near', 0, 0, tiled=True)  15 us
    all_to_all x1, blocking collectives, on_device(): lax.all_to_all(results, 'chip', 0, 0, tiled=True).reshape(chips * 24, LANES)  13.4 us
    all_to_all x1, starting transfers between devices, on_device(): lax.all_to_all(packed.reshape(chips, 24, LANES), 'chip', 0, 0, tiled=True)  10.9 us
    all_to_all x1, waiting for transfers between devices, on_device(): lax.all_to_all(packed.reshape(chips, 24, LANES), 'chip', 0, 0, tiled=True)  8.67 us
    all_to_all x1, starting transfers between devices, on_device(): shares = lax.all_to_all(everyone, 'tp_near', 0, 0, tiled=True)  7.1 us
    all_gather x1, blocking collectives, on_device(): pair = lax.all_gather(corr, 'tp_far')  6.45 us
    pallas_call x5, Pallas kernels, call(): pl.pallas_call(kernel, out_shape=out_shape, in_specs=[pl.BlockSpec(memory...  5.71 us
    all_gather x1, blocking collectives, on_device(): sequences = lax.all_gather(spread, 'core', tiled=True)  2.08 us
  transfers between devices with their start and end apart: 2, of which 2 were waited for; matrix products, arithmetic and copies ran while one was open for 0% of the time, Pallas kernels for 1%

profile of v3, /device:TPU:66, one launch (start us, length us, event | category | flops | bytes accessed | tf_op | source)
XLA Modules:
  0.0 70.8 jit_solution(11559694961903834512)
XLA Ops:
  0.6 2.2 %shard_map.85 = (f32[384,128]{1,0:T(8,128)}, bf16[2,1536,256]{2,1,0:T(8,128)(2,1)S(1)}, f32[272,256]{1,0:T(8,128)S(1)}) custom-call(bf16[16,1024]{1,0:T(8,128)(2,1)} %signal_ref.1, bf16[16,1024]{1,0:T(8,128)(2,1)} %grad_ref.1, f32[16,1024]{1,0:T(8,128)} %filter_hbm.1, bf16[2,1536,256]{2,1,0:T(8,128)(2,1)} %constant.12.clone.table_hbm, ...), custom_call_target="tpu_custom_call" | custom-call | tf_op jit(solution)/shard_map/pallas_call | solution.py:194
  2.9 10.9 %all-to-all-start = ((f32[16,24,128]{2,1,0:T(8,128)}), f32[16,24,128]{2,1,0:T(8,128)S(1)}, u32[]{:S(2)}, u32[]{:S(2)}) async-start(f32[16,24,128]{2,1,0:T(8,128)} %bitcast.1), calls=%async_computation | async-start | bytes 393216 | tf_op jit(solution)/shard_map/all_to_all | solution.py:231
  13.8 8.7 %all-to-all-done = f32[16,24,128]{2,1,0:T(8,128)S(1)} async-done(((f32[16,24,128]{2,1,0:T(8,128)}), f32[16,24,128]{2,1,0:T(8,128)S(1)}, u32[]{:S(2)}, u32[]{:S(2)}) %all-to-all-start) | async-done | bytes 196640 | tf_op jit(solution)/shard_map/all_to_all | solution.py:231
  22.4 2.1 %all_gather.9.in_ref = f32[32,24,128]{2,1,0:T(8,128)S(1)} all-gather(f32[16,24,128]{2,1,0:T(8,128)S(1)} %all-to-all-done), channel_id=1, replica_groups=mesh['chip'=16,'core'=2,'tp_far'=2,'tp_near'=8] {'core'}, dimensions={0}, use_global_device_ids=true | all-gather | bytes 589824 | tf_op jit(solution)/shard_map/all_gather | solution.py:232
  24.5 1.9 %shard_map.86 = f32[16,24,128]{2,1,0:T(8,128)S(1)} custom-call(s32[1]{0:T(128)} %bitcast.core_ref, f32[32,24,128]{2,1,0:T(8,128)S(1)} %all_gather.9.in_ref, bf16[2,1536,256]{2,1,0:T(8,128)(2,1)S(1)} %get-tuple-element.9.table, f32[272,256]{1,0:T(8,128)S(1)} %get-tuple-element.10.twist), custom_call_target="tpu_custom_call" | custom-call | tf_op jit(solution)/shard_map/pallas_call | solution.py:194
  26.4 0.0 copy-start.2
  26.4 0.0 copy-start
  26.5 0.0 copy-start.1
  26.5 13.4 %all_to_all.15 = f32[16,24,128]{2,1,0:T(8,128)S(1)} all-to-all(f32[16,24,128]{2,1,0:T(8,128)S(1)} %shard_map.86), channel_id=1, replica_groups=mesh['chip'=16,'core'=2,'tp_far'=2,'tp_near'=8] {'chip'}, dimensions={0} | all-to-all | bytes 393216 | tf_op jit(solution)/shard_map/all_to_all | solution.py:244
  39.9 6.4 %all-gather = f32[32,1024]{1,0:T(8,128)S(1)} all-gather(f32[16,1024]{1,0:T(8,128)S(1)} %shard_map.88), channel_id=2, replica_groups=mesh['chip'=16,'core'=2,'tp_far'=2,'tp_near'=8] {'tp_far'}, dimensions={0}, use_global_device_ids=true | all-gather | bytes 196608 | tf_op jit(solution)/shard_map/all_gather | solution.py:246
  46.4 0.8 %shard_map.89 = f32[8,16,1024]{2,1,0:T(8,128)} custom-call(f32[2,16,1024]{2,1,0:T(8,128)S(1)} %bitcast.7), custom_call_target="tpu_custom_call" | custom-call | tf_op jit(solution)/shard_map/pallas_call | solution.py:194
  47.2 7.1 %all-to-all-start.2 = ((f32[8,16,1024]{2,1,0:T(8,128)}), f32[8,16,1024]{2,1,0:T(8,128)S(1)}, u32[]{:S(2)}, u32[]{:S(2)}) async-start(f32[8,16,1024]{2,1,0:T(8,128)} %shard_map.89), calls=%async_computation.2 | async-start | bytes 1048576 | tf_op jit(solution)/shard_map/all_to_all | solution.py:249
  54.3 0.0 copy-done.2
  54.3 0.1 copy.10.gain_ref
  54.4 0.0 copy-done
  54.4 0.0 copy-done.1
  54.4 0.7 %shard_map.87 = (bf16[16,1024]{1,0:T(8,128)(2,1)}, bf16[16,1024]{1,0:T(8,128)(2,1)}) custom-call(f32[384,128]{1,0:T(8,128)S(1)} %bitcast.6, f32[16,1]{1,0:T(8,128)S(1)} %copy.10.gain_ref, bf16[16,1024]{1,0:T(8,128)(2,1)S(1)} %copy-done, bf16[16,1024]{1,0:T(8,128)(2,1)S(1)} %copy-done.1), custom_call_target="tpu_custom_call" | custom-call | tf_op jit(solution)/shard_map/pallas_call | solution.py:194
  55.1 15.0 %all-to-all-done.2 = f32[8,16,1024]{2,1,0:T(8,128)S(1)} async-done(((f32[8,16,1024]{2,1,0:T(8,128)}), f32[8,16,1024]{2,1,0:T(8,128)S(1)}, u32[]{:S(2)}, u32[]{:S(2)}) %all-to-all-start.2) | async-done | bytes 524320 | tf_op jit(solution)/shard_map/all_to_all | solution.py:249
  70.1 0.7 reduce_sum.9
  (1 shorter events, 0.0 us)
Async XLA Ops:
  2.9 19.6 %all-to-all-start = ((f32[16,24,128]{2,1,0:T(8,128)}), f32[16,24,128]{2,1,0:T(8,128)S(1)}, u32[]{:S(2)}, u32[]{:S(2)}) async-start(f32[16,24,128]{2,1,0:T(8,128)} %bitcast.1), calls=%async_computation | async-start | bytes 393216 | tf_op jit(solution)/shard_map/all_to_all | solution.py:231
  26.4 27.9 %copy-start.2 = (f32[16]{0:T(128)S(1)}, f32[16]{0:T(128)}, u32[]{:S(2)}) copy-start(f32[16]{0:T(128)} %param.8) | copy-start | bytes 196
  26.4 28.0 %copy-start = (bf16[16,1024]{1,0:T(8,128)(2,1)S(1)}, bf16[16,1024]{1,0:T(8,128)(2,1)}, u32[]{:S(2)}) copy-start(bf16[16,1024]{1,0:T(8,128)(2,1)} %signal_ref.1) | copy-start | bytes 98308
  26.5 28.0 %copy-start.1 = (bf16[16,1024]{1,0:T(8,128)(2,1)S(1)}, bf16[16,1024]{1,0:T(8,128)(2,1)}, u32[]{:S(2)}) copy-start(bf16[16,1024]{1,0:T(8,128)(2,1)} %grad_ref.1) | copy-start | bytes 98308
  47.2 22.9 %all-to-all-start.2 = ((f32[8,16,1024]{2,1,0:T(8,128)}), f32[8,16,1024]{2,1,0:T(8,128)S(1)}, u32[]{:S(2)}, u32[]{:S(2)}) async-start(f32[8,16,1024]{2,1,0:T(8,128)} %shard_map.89), calls=%async_computation.2 | async-start | bytes 1048576 | tf_op jit(solution)/shard_map/all_to_all | solution.py:249

commit v4 on v3

--- a/solution.py
+++ b/solution.py
@@ -65,12 +65,15 @@
 
 
 def pack_kernel(
-    signal_hbm, grad_hbm, filter_hbm, table_hbm, twist_hbm, out_ref, table_ref, twist_ref, signal_ref, grad_ref, filter_ref, sems
+    signal_hbm, grad_hbm, filter_hbm, gain_hbm, table_hbm, twist_hbm,
+    out_ref, skip_ref, table_ref, twist_ref,
+    signal_ref, grad_ref, filter_ref, gain_ref, sems,
 ):
     pairs = (
         (signal_hbm, signal_ref),
         (grad_hbm, grad_ref),
         (filter_hbm, filter_ref),
+        (gain_hbm, gain_ref),
         (table_hbm, table_ref),
         (twist_hbm, twist_ref),
     )
@@ -78,20 +81,29 @@
     for copy in copies:
         copy.start()
     channels = signal_ref.shape[0]
+    arrays = []
     for number, ref in enumerate((signal_ref, grad_ref, filter_ref)):
         copies[number].wait()
-        array = ref[...].astype(jnp.float32)
+        arrays.append(ref[...].astype(jnp.float32))
         for chunk in range(SUBLANES):
-            out_ref[pl.ds(number * 8 + chunk, channels, stride=24), :] = array[:, chunk * LANES : (chunk + 1) * LANES]
-    for copy in copies[3:]:
+            lanes = slice(chunk * LANES, (chunk + 1) * LANES)
+            out_ref[pl.ds(number * 8 + chunk, channels, stride=24), :] = arrays[number][:, lanes]
+    copies[3].wait()
+    row = lax.broadcasted_iota(jnp.int32, (channels, 1), 0)
+    gains = jnp.zeros((channels, 1), jnp.float32)
+    for channel in range(channels):
+        gains = jnp.where(row == channel, gain_ref[channel], gains)
+    skip_ref[0] = gains * arrays[0]
+    skip_ref[1] = gains * arrays[1]
+    for copy in copies[4:]:
         copy.wait()
 
 
-def convolve_kernel(core_ref, in_ref, table, twist, out_ref, a_ref, u_h, u_l):
+def convolve_kernel(in_ref, table, twist, out_ref, a_ref, u_h, u_l):
     chips = out_ref.shape[0]
     half = chips * SUBLANES
     rows = 2 * half
-    core = core_ref[0]
+    core = lax.axis_index("core")
 
     def part(number, start, count):
         return table[number, start : start + count, :]
@@ -173,19 +185,24 @@
 
 
 def add_kernel(in_ref, out_ref):
-    total = in_ref[0] + in_ref[1]
+    total = in_ref[0]
+    for place in range(1, in_ref.shape[0]):
+        total += in_ref[place]
     for place in range(out_ref.shape[0]):
         out_ref[place] = total
 
 
-def finish_kernel(in_ref, gain_ref, signal_ref, grad_ref, out_ref, back_ref):
-    channels = signal_ref.shape[0]
-    gains = gain_ref[...]
+def finish_kernel(in_ref, skip_ref, shares_ref, out_ref, back_ref, corr_ref):
+    channels = corr_ref.shape[0]
     for chunk in range(SUBLANES):
         lanes = slice(chunk * LANES, (chunk + 1) * LANES)
-        for number, (own, result) in enumerate(((signal_ref, out_ref), (grad_ref, back_ref))):
+        for number, result in enumerate((out_ref, back_ref)):
             conv = in_ref[pl.ds(number * 8 + chunk, channels, stride=24), :]
-            result[:, lanes] = (conv + gains * own[:, lanes].astype(jnp.float32)).astype(jnp.bfloat16)
+            result[:, lanes] = (conv + skip_ref[number, :, lanes]).astype(jnp.bfloat16)
+    total = shares_ref[0]
+    for place in range(1, shares_ref.shape[0]):
+        total += shares_ref[place]
+    corr_ref[...] = total
 
 
 def call(kernel, out_shape, operands, scratch=(), spaces=None):
@@ -209,13 +226,16 @@
     length = tokens * ctx
     rows = length // LANES
     table, twist = make_tables(rows, ctx, 1.0 / math.sqrt(length))
-    core = lax.axis_index("core").astype(jnp.int32).reshape(1)
-
-    in_hbm = [pltpu.with_memory_space_constraint(x, pltpu.HBM) for x in (signal, grad_out, filter_taps, table, twist)]
-    packed, table, twist = call(
+
+    in_hbm = [
+        pltpu.with_memory_space_constraint(x, pltpu.HBM)
+        for x in (signal, grad_out, filter_taps, skip_gain, table, twist)
+    ]
+    packed, skip, table, twist = call(
         pack_kernel,
         (
             pltpu.VMEM((chips * 24, LANES), jnp.float32),
+            pltpu.VMEM((2, channels, tokens), jnp.float32),
             pltpu.VMEM(table.shape, table.dtype),
             pltpu.VMEM(twist.shape, twist.dtype),
         ),
@@ -224,22 +244,22 @@
             pltpu.VMEM(signal.shape, signal.dtype),
             pltpu.VMEM(grad_out.shape, grad_out.dtype),
             pltpu.VMEM(filter_taps.shape, filter_taps.dtype),
-            pltpu.SemaphoreType.DMA((5,)),
-        ),
-        spaces=[pltpu.HBM] * 5,
+            pltpu.SMEM(skip_gain.shape, skip_gain.dtype),
+            pltpu.SemaphoreType.DMA((6,)),
+        ),
+        spaces=[pltpu.HBM] * 6,
     )
     spread = lax.all_to_all(packed.reshape(chips, 24, LANES), "chip", 0, 0, tiled=True)
     sequences = lax.all_gather(spread, "core", tiled=True)
     results = call(
         convolve_kernel,
         jax.ShapeDtypeStruct((chips, 24, LANES), jnp.float32),
-        (core, sequences, table, twist),
+        (sequences, table, twist),
         scratch=(
             pltpu.VMEM((2 * rows, 3 * LANES), jnp.float32),
             pltpu.VMEM((2 * rows, 3 * LANES), jnp.bfloat16),
             pltpu.VMEM((2 * rows, 3 * LANES), jnp.bfloat16),
         ),
-        spaces=[pltpu.SMEM] + [pltpu.VMEM] * 3,
     )
     returned = lax.all_to_all(results, "chip", 0, 0, tiled=True).reshape(chips * 24, LANES)
     corr = call(collect_kernel, jax.ShapeDtypeStruct((channels, tokens), jnp.float32), (returned,))
@@ -247,14 +267,14 @@
     near = lax.axis_size("tp_near")
     everyone = call(add_kernel, jax.ShapeDtypeStruct((near, channels, tokens), jnp.float32), (pair,))
     shares = lax.all_to_all(everyone, "tp_near", 0, 0, tiled=True)
-    grad_filter = jnp.sum(shares, axis=0)
-    output, grad_signal = call(
+    output, grad_signal, grad_filter = call(
         finish_kernel,
         (
             jax.ShapeDtypeStruct((channels, tokens), jnp.bfloat16),
             jax.ShapeDtypeStruct((channels, tokens), jnp.bfloat16),
-        ),
-        (returned, skip_gain[:, None], signal, grad_out),
+            jax.ShapeDtypeStruct((channels, tokens), jnp.float32),
+        ),
+        (returned, skip, shares),
     )
     return (output, grad_signal, grad_filter)
 

time: 71.2 us -> 69 us (0.969)
  the two profiles are of different devices: /device:TPU:66 before, /device:TPU:70 now
where the time goes in v4:
time: 69 us; the launch traced here: 68.8 us
  blocking collectives  63.9 us (93%)
  Pallas kernels  4.25 us (6%)
    all_to_all x1, blocking collectives, on_device(): shares = lax.all_to_all(everyone, 'tp_near', 0, 0, tiled=True)  22.7 us
    all_to_all x1, blocking collectives, on_device(): lax.all_to_all(packed.reshape(chips, 24, LANES), 'chip', 0, 0, tiled=True)  19.3 us
    all_to_all x1, blocking collectives, on_device(): lax.all_to_all(results, 'chip', 0, 0, tiled=True).reshape(chips * 24, LANES)  13.3 us
    all_gather x1, blocking collectives, on_device(): pair = lax.all_gather(corr, 'tp_far')  6.45 us
    pallas_call x5, Pallas kernels, call(): pl.pallas_call(kernel, out_shape=out_shape, in_specs=[pl.BlockSpec(memory...  4.25 us
    all_gather x1, blocking collectives, on_device(): sequences = lax.all_gather(spread, 'core', tiled=True)  2.08 us

profile of v4, /device:TPU:70, one launch (start us, length us, event | category | flops | bytes accessed | tf_op | source)
XLA Modules:
  0.0 68.8 jit_solution(7284504427961270266)
XLA Ops:
  0.6 1.6 %shard_map.85 = (f32[384,128]{1,0:T(8,128)S(1)}, f32[2,16,1024]{2,1,0:T(8,128)S(1)}, bf16[2,1536,256]{2,1,0:T(8,128)(2,1)S(1)}, f32[272,256]{1,0:T(8,128)S(1)}) custom-call(bf16[16,1024]{1,0:T(8,128)(2,1)} %signal_hbm.1, bf16[16,1024]{1,0:T(8,128)(2,1)} %grad_hbm.1, f32[16,1024]{1,0:T(8,128)} %filter_hbm.1, f32[16]{0:T(128)} %gain_hbm.1, ...), custom_call_target="tpu_custom_call" | custom-call | tf_op jit(solution)/shard_map/pallas_call | solution.py:211
  2.2 19.3 %all_to_all.15 = f32[16,24,128]{2,1,0:T(8,128)S(1)} all-to-all(f32[16,24,128]{2,1,0:T(8,128)S(1)} %bitcast.6), channel_id=1, replica_groups=mesh['chip'=16,'core'=2,'tp_far'=2,'tp_near'=8] {'chip'}, dimensions={0} | all-to-all | bytes 393216 | tf_op jit(solution)/shard_map/all_to_all | solution.py:252
  21.5 2.1 %all_gather.9.in_ref = f32[32,24,128]{2,1,0:T(8,128)S(1)} all-gather(f32[16,24,128]{2,1,0:T(8,128)S(1)} %all_to_all.15), channel_id=1, replica_groups=mesh['chip'=16,'core'=2,'tp_far'=2,'tp_near'=8] {'core'}, dimensions={0}, use_global_device_ids=true | all-gather | bytes 589824 | tf_op jit(solution)/shard_map/all_gather | solution.py:253
  23.6 1.9 %shard_map.86 = f32[16,24,128]{2,1,0:T(8,128)S(1)} custom-call(f32[32,24,128]{2,1,0:T(8,128)S(1)} %all_gather.9.in_ref, bf16[2,1536,256]{2,1,0:T(8,128)(2,1)S(1)} %get-tuple-element.8.table, f32[272,256]{1,0:T(8,128)S(1)} %get-tuple-element.9.twist), custom_call_target="tpu_custom_call" | custom-call | tf_op jit(solution)/shard_map/pallas_call | solution.py:211
  25.6 13.3 %all_to_all.16 = f32[16,24,128]{2,1,0:T(8,128)S(1)} all-to-all(f32[16,24,128]{2,1,0:T(8,128)S(1)} %shard_map.86), channel_id=1, replica_groups=mesh['chip'=16,'core'=2,'tp_far'=2,'tp_near'=8] {'chip'}, dimensions={0} | all-to-all | bytes 393216 | tf_op jit(solution)/shard_map/all_to_all | solution.py:264
  38.9 6.4 %all-gather = f32[32,1024]{1,0:T(8,128)S(1)} all-gather(f32[16,1024]{1,0:T(8,128)S(1)} %shard_map.87), channel_id=2, replica_groups=mesh['chip'=16,'core'=2,'tp_far'=2,'tp_near'=8] {'tp_far'}, dimensions={0}, use_global_device_ids=true | all-gather | bytes 196608 | tf_op jit(solution)/shard_map/all_gather | solution.py:266
  45.4 22.7 %all_to_all.17.shares_ref = f32[8,16,1024]{2,1,0:T(8,128)S(1)} all-to-all(f32[8,16,1024]{2,1,0:T(8,128)S(1)} %shard_map.88), channel_id=1, replica_groups=mesh['chip'=16,'core'=2,'tp_far'=2,'tp_near'=8] {'tp_near'}, dimensions={0} | all-to-all | bytes 1048576 | tf_op jit(solution)/shard_map/all_to_all | solution.py:269
  68.1 0.7 %shard_map.89 = (bf16[16,1024]{1,0:T(8,128)(2,1)}, bf16[16,1024]{1,0:T(8,128)(2,1)}, f32[16,1024]{1,0:T(8,128)}) custom-call(f32[384,128]{1,0:T(8,128)S(1)} %bitcast.4, f32[2,16,1024]{2,1,0:T(8,128)S(1)} %get-tuple-element.10.skip_ref, f32[8,16,1024]{2,1,0:T(8,128)S(1)} %all_to_all.17.shares_ref), custom_call_target="tpu_custom_call" | custom-call | tf_op jit(solution)/shard_map/pallas_call | solution.py:211
  (2 shorter events, 0.1 us)

commit v5 on v4

--- a/solution.py
+++ b/solution.py
@@ -179,9 +179,7 @@
 
 
 def collect_kernel(in_ref, corr_ref):
-    channels = corr_ref.shape[0]
-    for chunk in range(SUBLANES):
-        corr_ref[:, chunk * LANES : (chunk + 1) * LANES] = in_ref[pl.ds(16 + chunk, channels, stride=24), :]
+    corr_ref[...] = in_ref[:, 16:, :]
 
 
 def add_kernel(in_ref, out_ref):
@@ -192,17 +190,18 @@
         out_ref[place] = total
 
 
-def finish_kernel(in_ref, skip_ref, shares_ref, out_ref, back_ref, corr_ref):
+def finish_kernel(in_ref, skip_ref, shares_ref, out_ref, back_ref, corr_ref, total_ref):
     channels = corr_ref.shape[0]
+    total = shares_ref[0]
+    for place in range(1, shares_ref.shape[0]):
+        total += shares_ref[place]
+    total_ref[...] = total
     for chunk in range(SUBLANES):
         lanes = slice(chunk * LANES, (chunk + 1) * LANES)
+        corr_ref[:, lanes] = total_ref[pl.ds(chunk, channels, stride=SUBLANES), :]
         for number, result in enumerate((out_ref, back_ref)):
             conv = in_ref[pl.ds(number * 8 + chunk, channels, stride=24), :]
             result[:, lanes] = (conv + skip_ref[number, :, lanes]).astype(jnp.bfloat16)
-    total = shares_ref[0]
-    for place in range(1, shares_ref.shape[0]):
-        total += shares_ref[place]
-    corr_ref[...] = total
 
 
 def call(kernel, out_shape, operands, scratch=(), spaces=None):
@@ -261,11 +260,12 @@
             pltpu.VMEM((2 * rows, 3 * LANES), jnp.bfloat16),
         ),
     )
-    returned = lax.all_to_all(results, "chip", 0, 0, tiled=True).reshape(chips * 24, LANES)
-    corr = call(collect_kernel, jax.ShapeDtypeStruct((channels, tokens), jnp.float32), (returned,))
+    returned = lax.all_to_all(results, "chip", 0, 0, tiled=True)
+    corr = call(collect_kernel, jax.ShapeDtypeStruct((channels, SUBLANES, LANES), jnp.float32), (returned,))
+    corr = corr.reshape(channels * SUBLANES, LANES)
     pair = lax.all_gather(corr, "tp_far")
     near = lax.axis_size("tp_near")
-    everyone = call(add_kernel, jax.ShapeDtypeStruct((near, channels, tokens), jnp.float32), (pair,))
+    everyone = call(add_kernel, jax.ShapeDtypeStruct((near, *corr.shape), jnp.float32), (pair,))
     shares = lax.all_to_all(everyone, "tp_near", 0, 0, tiled=True)
     output, grad_signal, grad_filter = call(
         finish_kernel,
@@ -274,7 +274,8 @@
             jax.ShapeDtypeStruct((channels, tokens), jnp.bfloat16),
             jax.ShapeDtypeStruct((channels, tokens), jnp.float32),
         ),
-        (returned, skip, shares),
+        (returned.reshape(chips * 24, LANES), skip, shares),
+        scratch=(pltpu.VMEM(corr.shape, corr.dtype),),
     )
     return (output, grad_signal, grad_filter)
 

time: 69 us -> 69 us (level)
  no operation moved by 1% of the time
where the time goes in v5:
time: 69 us; the launch traced here: 68.8 us
  blocking collectives  63.9 us (93%)
  Pallas kernels  4.24 us (6%)
    all_to_all x1, blocking collectives, on_device(): shares = lax.all_to_all(everyone, 'tp_near', 0, 0, tiled=True)  22.7 us
    all_to_all x1, blocking collectives, on_device(): lax.all_to_all(packed.reshape(chips, 24, LANES), 'chip', 0, 0, tiled=True)  19.3 us
    all_to_all x1, blocking collectives, on_device(): returned = lax.all_to_all(results, 'chip', 0, 0, tiled=True)  13.3 us
    all_gather x1, blocking collectives, on_device(): pair = lax.all_gather(corr, 'tp_far')  6.43 us
    pallas_call x5, Pallas kernels, call(): pl.pallas_call(kernel, out_shape=out_shape, in_specs=[pl.BlockSpec(memory...  4.24 us
    all_gather x1, blocking collectives, on_device(): sequences = lax.all_gather(spread, 'core', tiled=True)  2.08 us

profile of v5, /device:TPU:70, one launch (start us, length us, event | category | flops | bytes accessed | tf_op | source)
XLA Modules:
  0.0 68.8 jit_solution(12703280149777868457)
XLA Ops:
  0.6 1.6 %shard_map.85 = (f32[384,128]{1,0:T(8,128)S(1)}, f32[2,16,1024]{2,1,0:T(8,128)S(1)}, bf16[2,1536,256]{2,1,0:T(8,128)(2,1)S(1)}, f32[272,256]{1,0:T(8,128)S(1)}) custom-call(bf16[16,1024]{1,0:T(8,128)(2,1)} %signal_hbm.1, bf16[16,1024]{1,0:T(8,128)(2,1)} %grad_hbm.1, f32[16,1024]{1,0:T(8,128)} %filter_hbm.1, f32[16]{0:T(128)} %gain_hbm.1, ...), custom_call_target="tpu_custom_call" | custom-call | tf_op jit(solution)/shard_map/pallas_call | solution.py:210
  2.2 19.3 %all_to_all.15 = f32[16,24,128]{2,1,0:T(8,128)S(1)} all-to-all(f32[16,24,128]{2,1,0:T(8,128)S(1)} %bitcast.5), channel_id=1, replica_groups=mesh['chip'=16,'core'=2,'tp_far'=2,'tp_near'=8] {'chip'}, dimensions={0} | all-to-all | bytes 393216 | tf_op jit(solution)/shard_map/all_to_all | solution.py:251
  21.5 2.1 %all_gather.6.in_ref = f32[32,24,128]{2,1,0:T(8,128)S(1)} all-gather(f32[16,24,128]{2,1,0:T(8,128)S(1)} %all_to_all.15), channel_id=1, replica_groups=mesh['chip'=16,'core'=2,'tp_far'=2,'tp_near'=8] {'core'}, dimensions={0}, use_global_device_ids=true | all-gather | bytes 589824 | tf_op jit(solution)/shard_map/all_gather | solution.py:252
  23.6 1.9 %shard_map.86 = f32[16,24,128]{2,1,0:T(8,128)S(1)} custom-call(f32[32,24,128]{2,1,0:T(8,128)S(1)} %all_gather.6.in_ref, bf16[2,1536,256]{2,1,0:T(8,128)(2,1)S(1)} %get-tuple-element.8.table, f32[272,256]{1,0:T(8,128)S(1)} %get-tuple-element.9.twist), custom_call_target="tpu_custom_call" | custom-call | tf_op jit(solution)/shard_map/pallas_call | solution.py:210
  25.6 13.3 %all_to_all.16.in_ref = f32[16,24,128]{2,1,0:T(8,128)S(1)} all-to-all(f32[16,24,128]{2,1,0:T(8,128)S(1)} %shard_map.86), channel_id=1, replica_groups=mesh['chip'=16,'core'=2,'tp_far'=2,'tp_near'=8] {'chip'}, dimensions={0} | all-to-all | bytes 393216 | tf_op jit(solution)/shard_map/all_to_all | solution.py:263
  38.9 6.4 %all_gather.7.in_ref = f32[2,128,128]{2,1,0:T(8,128)S(1)} all-gather(f32[1,128,128]{2,1,0:T(8,128)S(1)} %bitcast.4), channel_id=1, replica_groups=mesh['chip'=16,'core'=2,'tp_far'=2,'tp_near'=8] {'tp_far'}, dimensions={0}, use_global_device_ids=true | all-gather | bytes 196608 | tf_op jit(solution)/shard_map/all_gather | solution.py:266
  45.4 22.7 %all_to_all.17.shares_ref = f32[8,128,128]{2,1,0:T(8,128)S(1)} all-to-all(f32[8,128,128]{2,1,0:T(8,128)S(1)} %shard_map.88), channel_id=1, replica_groups=mesh['chip'=16,'core'=2,'tp_far'=2,'tp_near'=8] {'tp_near'}, dimensions={0} | all-to-all | bytes 1048576 | tf_op jit(solution)/shard_map/all_to_all | solution.py:269
  68.1 0.7 %shard_map.89 = (bf16[16,1024]{1,0:T(8,128)(2,1)}, bf16[16,1024]{1,0:T(8,128)(2,1)}, f32[16,1024]{1,0:T(8,128)}) custom-call(f32[384,128]{1,0:T(8,128)S(1)} %bitcast.3, f32[2,16,1024]{2,1,0:T(8,128)S(1)} %get-tuple-element.10.skip_ref, f32[8,128,128]{2,1,0:T(8,128)S(1)} %all_to_all.17.shares_ref), custom_call_target="tpu_custom_call" | custom-call | tf_op jit(solution)/shard_map/pallas_call | solution.py:210
  (2 shorter events, 0.0 us)

commit v6 on v5

--- a/solution.py
+++ b/solution.py
@@ -175,32 +175,34 @@
         y += dot(columns_h, u_h[here, :]) + dot(columns_h, u_l[here, :]) + dot(columns_l, u_h[here, :])
         at += rows
     for number in range(3):
-        out_ref[:, number * 8 : number * 8 + 8, :] = y[:, number * LANES : (number + 1) * LANES].reshape(chips, SUBLANES, LANES)
-
-
-def collect_kernel(in_ref, corr_ref):
-    corr_ref[...] = in_ref[:, 16:, :]
-
-
-def add_kernel(in_ref, out_ref):
-    total = in_ref[0]
-    for place in range(1, in_ref.shape[0]):
-        total += in_ref[place]
-    for place in range(out_ref.shape[0]):
-        out_ref[place] = total
-
-
-def finish_kernel(in_ref, skip_ref, shares_ref, out_ref, back_ref, corr_ref, total_ref):
+        piece = y[:, number * LANES : (number + 1) * LANES].reshape(chips, SUBLANES, LANES)
+        for far in range(out_ref.shape[1]):
+            out_ref[:, far, number * 8 : number * 8 + 8, :] = piece
+
+
+def collect_kernel(in_ref, everyone_ref):
+    channels, chunks, lanes = in_ref.shape[0], SUBLANES, in_ref.shape[3]
+    total = in_ref[:, 0, 16:, :]
+    for far in range(1, in_ref.shape[1]):
+        total += in_ref[:, far, 16:, :]
+    total = total.reshape(channels * chunks, lanes)
+    for place in range(everyone_ref.shape[0]):
+        everyone_ref[place] = total
+
+
+def finish_kernel(in_ref, skip_ref, shares_ref, out_ref, back_ref, corr_ref, own_ref, total_ref):
     channels = corr_ref.shape[0]
     total = shares_ref[0]
     for place in range(1, shares_ref.shape[0]):
         total += shares_ref[place]
     total_ref[...] = total
+    own = in_ref[:, pl.ds(lax.axis_index("tp_far"), 1), :16, :]
+    own_ref[...] = own.reshape(own_ref.shape)
     for chunk in range(SUBLANES):
         lanes = slice(chunk * LANES, (chunk + 1) * LANES)
         corr_ref[:, lanes] = total_ref[pl.ds(chunk, channels, stride=SUBLANES), :]
         for number, result in enumerate((out_ref, back_ref)):
-            conv = in_ref[pl.ds(number * 8 + chunk, channels, stride=24), :]
+            conv = own_ref[pl.ds(number * 8 + chunk, channels, stride=16), :]
             result[:, lanes] = (conv + skip_ref[number, :, lanes]).astype(jnp.bfloat16)
 
 
@@ -220,6 +222,7 @@
 def on_device(signal, filter_taps, skip_gain, grad_out):
     channels, tokens = signal.shape
     chips = lax.axis_size("chip")
+    far = lax.axis_size("tp_far")
     ctx = 2 * chips
     assert channels == chips and tokens == SUBLANES * LANES
     length = tokens * ctx
@@ -252,7 +255,7 @@
     sequences = lax.all_gather(spread, "core", tiled=True)
     results = call(
         convolve_kernel,
-        jax.ShapeDtypeStruct((chips, 24, LANES), jnp.float32),
+        jax.ShapeDtypeStruct((chips, far, 24, LANES), jnp.float32),
         (sequences, table, twist),
         scratch=(
             pltpu.VMEM((2 * rows, 3 * LANES), jnp.float32),
@@ -260,12 +263,12 @@
             pltpu.VMEM((2 * rows, 3 * LANES), jnp.bfloat16),
         ),
     )
-    returned = lax.all_to_all(results, "chip", 0, 0, tiled=True)
-    corr = call(collect_kernel, jax.ShapeDtypeStruct((channels, SUBLANES, LANES), jnp.float32), (returned,))
-    corr = corr.reshape(channels * SUBLANES, LANES)
-    pair = lax.all_gather(corr, "tp_far")
+    results = results.reshape(chips * far, 24, LANES)
+    returned = lax.all_to_all(results, ("chip", "tp_far"), 0, 0, tiled=True).reshape(chips, far, 24, LANES)
     near = lax.axis_size("tp_near")
-    everyone = call(add_kernel, jax.ShapeDtypeStruct((near, *corr.shape), jnp.float32), (pair,))
+    everyone = call(
+        collect_kernel, jax.ShapeDtypeStruct((near, channels * SUBLANES, LANES), jnp.float32), (returned,)
+    )
     shares = lax.all_to_all(everyone, "tp_near", 0, 0, tiled=True)
     output, grad_signal, grad_filter = call(
         finish_kernel,
@@ -274,8 +277,11 @@
             jax.ShapeDtypeStruct((channels, tokens), jnp.bfloat16),
             jax.ShapeDtypeStruct((channels, tokens), jnp.float32),
         ),
-        (returned.reshape(chips * 24, LANES), skip, shares),
-        scratch=(pltpu.VMEM(corr.shape, corr.dtype),),
+        (returned, skip, shares),
+        scratch=(
+            pltpu.VMEM((channels * 16, LANES), jnp.float32),
+            pltpu.VMEM((channels * SUBLANES, LANES), jnp.float32),
+        ),
     )
     return (output, grad_signal, grad_filter)
 

time: 69 us -> 70.9 us (1.028)
  the two profiles are of different devices: /device:TPU:70 before, /device:TPU:8 now
where the time goes in v6:
time: 70.9 us; the launch traced here: 70.6 us
  blocking collectives  65.7 us (93%)
  Pallas kernels  4.26 us (6%)
    all_to_all x1, blocking collectives, on_device(): shares = lax.all_to_all(everyone, 'tp_near', 0, 0, tiled=True)  21.7 us
    all_to_all x1, blocking collectives, on_device(): lax.all_to_all(results, ('chip', 'tp_far'), 0, 0, tiled=True)  21.7 us
    all_to_all x1, blocking collectives, on_device(): lax.all_to_all(packed.reshape(chips, 24, LANES), 'chip', 0, 0, tiled=True)  20.2 us
    pallas_call x4, Pallas kernels, call(): pl.pallas_call(kernel, out_shape=out_shape, in_specs=[pl.BlockSpec(memory...  4.26 us
    all_gather x1, blocking collectives, on_device(): sequences = lax.all_gather(spread, 'core', tiled=True)  2.08 us

profile of v6, /device:TPU:8, one launch (start us, length us, event | category | flops | bytes accessed | tf_op | source)
XLA Modules:
  0.0 70.6 jit_solution(5250935792478271705)
XLA Ops:
  0.6 1.6 %shard_map.85 = (f32[384,128]{1,0:T(8,128)S(1)}, f32[2,16,1024]{2,1,0:T(8,128)S(1)}, bf16[2,1536,256]{2,1,0:T(8,128)(2,1)S(1)}, f32[272,256]{1,0:T(8,128)S(1)}) custom-call(bf16[16,1024]{1,0:T(8,128)(2,1)} %signal_hbm.1, bf16[16,1024]{1,0:T(8,128)(2,1)} %grad_hbm.1, f32[16,1024]{1,0:T(8,128)} %filter_hbm.1, f32[16]{0:T(128)} %gain_hbm.1, ...), custom_call_target="tpu_custom_call" | custom-call | tf_op jit(solution)/shard_map/pallas_call | solution.py:212
  2.2 20.2 %all_to_all.15 = f32[16,24,128]{2,1,0:T(8,128)S(1)} all-to-all(f32[16,24,128]{2,1,0:T(8,128)S(1)} %bitcast.6), channel_id=1, replica_groups=mesh['chip'=16,'core'=2,'tp_far'=2,'tp_near'=8] {'chip'}, dimensions={0} | all-to-all | bytes 393216 | tf_op jit(solution)/shard_map/all_to_all | solution.py:254
  22.4 2.1 %all_gather.3.in_ref = f32[32,24,128]{2,1,0:T(8,128)S(1)} all-gather(f32[16,24,128]{2,1,0:T(8,128)S(1)} %all_to_all.15), channel_id=1, replica_groups=mesh['chip'=16,'core'=2,'tp_far'=2,'tp_near'=8] {'core'}, dimensions={0}, use_global_device_ids=true | all-gather | bytes 589824 | tf_op jit(solution)/shard_map/all_gather | solution.py:255
  24.5 1.9 %shard_map.86 = f32[16,2,24,128]{3,2,1,0:T(8,128)S(1)} custom-call(f32[32,24,128]{2,1,0:T(8,128)S(1)} %all_gather.3.in_ref, bf16[2,1536,256]{2,1,0:T(8,128)(2,1)S(1)} %get-tuple-element.8.table, f32[272,256]{1,0:T(8,128)S(1)} %get-tuple-element.9.twist), custom_call_target="tpu_custom_call" | custom-call | tf_op jit(solution)/shard_map/pallas_call | solution.py:212
  26.4 21.7 %all_to_all.16 = f32[32,24,128]{2,1,0:T(8,128)S(1)} all-to-all(f32[32,24,128]{2,1,0:T(8,128)S(1)} %bitcast.5), channel_id=1, replica_groups=mesh['chip'=16,'core'=2,'tp_far'=2,'tp_near'=8] {'chip','tp_far'}, dimensions={0} | all-to-all | bytes 786432 | tf_op jit(solution)/shard_map/all_to_all | solution.py:267
  48.2 21.7 %all_to_all.17.shares_ref = f32[8,128,128]{2,1,0:T(8,128)S(1)} all-to-all(f32[8,128,128]{2,1,0:T(8,128)S(1)} %shard_map.87), channel_id=1, replica_groups=mesh['chip'=16,'core'=2,'tp_far'=2,'tp_near'=8] {'tp_near'}, dimensions={0} | all-to-all | bytes 1048576 | tf_op jit(solution)/shard_map/all_to_all | solution.py:272
  69.9 0.7 %shard_map.88 = (bf16[16,1024]{1,0:T(8,128)(2,1)}, bf16[16,1024]{1,0:T(8,128)(2,1)}, f32[16,1024]{1,0:T(8,128)}) custom-call(f32[16,2,24,128]{3,2,1,0:T(8,128)S(1)} %bitcast.4, f32[2,16,1024]{2,1,0:T(8,128)S(1)} %get-tuple-element.10.skip_ref, f32[8,128,128]{2,1,0:T(8,128)S(1)} %all_to_all.17.shares_ref), custom_call_target="tpu_custom_call" | custom-call | tf_op jit(solution)/shard_map/pallas_call | solution.py:212
  (1 shorter events, 0.0 us)

commit v7 on v5

--- a/solution.py
+++ b/solution.py
@@ -13,7 +13,9 @@
 LANES = 128
 SUBLANES = 8
 CTX = ("chip", "core")
-TP = ("tp_far", "tp_near")
+TP = ("tp_far", "tp_even", "tp_next")
+TP_FIRST = ("tp_far", "tp_next")
+TP_SECOND = ("tp_even",)
 VMEM_BYTES = 24 * 1024 * 1024
 
 
@@ -178,8 +180,10 @@
         out_ref[:, number * 8 : number * 8 + 8, :] = y[:, number * LANES : (number + 1) * LANES].reshape(chips, SUBLANES, LANES)
 
 
-def collect_kernel(in_ref, corr_ref):
-    corr_ref[...] = in_ref[:, 16:, :]
+def collect_kernel(in_ref, out_ref):
+    mine = in_ref[:, 16:, :].reshape(out_ref.shape[1:])
+    for place in range(out_ref.shape[0]):
+        out_ref[place] = mine
 
 
 def add_kernel(in_ref, out_ref):
@@ -261,12 +265,12 @@
         ),
     )
     returned = lax.all_to_all(results, "chip", 0, 0, tiled=True)
-    corr = call(collect_kernel, jax.ShapeDtypeStruct((channels, SUBLANES, LANES), jnp.float32), (returned,))
-    corr = corr.reshape(channels * SUBLANES, LANES)
-    pair = lax.all_gather(corr, "tp_far")
-    near = lax.axis_size("tp_near")
-    everyone = call(add_kernel, jax.ShapeDtypeStruct((near, *corr.shape), jnp.float32), (pair,))
-    shares = lax.all_to_all(everyone, "tp_near", 0, 0, tiled=True)
+    shape = (channels * SUBLANES, LANES)
+    first, second = lax.axis_size(TP_FIRST), lax.axis_size(TP_SECOND)
+    everyone = call(collect_kernel, jax.ShapeDtypeStruct((first, *shape), jnp.float32), (returned,))
+    shares = lax.all_to_all(everyone, TP_FIRST, 0, 0, tiled=True)
+    everyone = call(add_kernel, jax.ShapeDtypeStruct((second, *shape), jnp.float32), (shares,))
+    shares = lax.all_to_all(everyone, TP_SECOND, 0, 0, tiled=True)
     output, grad_signal, grad_filter = call(
         finish_kernel,
         (
@@ -275,15 +279,14 @@
             jax.ShapeDtypeStruct((channels, tokens), jnp.float32),
         ),
         (returned.reshape(chips * 24, LANES), skip, shares),
-        scratch=(pltpu.VMEM(corr.shape, corr.dtype),),
+        scratch=(pltpu.VMEM(shape, jnp.float32),),
     )
     return (output, grad_signal, grad_filter)
 
 
 def solution(mesh):
     ctx, tp = mesh.shape["ctx"], mesh.shape["tp"]
-    far = 2 if tp % 2 == 0 else 1
-    parted = Mesh(mesh.devices.reshape(ctx // 2, 2, far, tp // far), ("chip", "core", "tp_far", "tp_near"))
+    parted = Mesh(mesh.devices.reshape(ctx // 2, 2, 2, tp // 4, 2), (*CTX, *TP))
     in_specs = (P(TP, CTX), P(None, CTX), P(TP), P(TP, CTX))
     out_specs = (P(TP, CTX), P(TP, CTX), P(None, CTX))
     return jax.shard_map(

time: 69 us -> 68 us (0.986)
  the two profiles are of different devices: /device:TPU:70 before, /device:TPU:8 now
where the time goes in v7:
time: 68 us; the launch traced here: 67.7 us
  blocking collectives  62.9 us (92%)
  Pallas kernels  4.23 us (6%)
    all_to_all x1, blocking collectives, on_device(): lax.all_to_all(packed.reshape(chips, 24, LANES), 'chip', 0, 0, tiled=True)  20.2 us
    all_to_all x1, blocking collectives, on_device(): shares = lax.all_to_all(everyone, TP_SECOND, 0, 0, tiled=True)  16.2 us
    all_to_all x1, blocking collectives, on_device(): returned = lax.all_to_all(results, 'chip', 0, 0, tiled=True)  13 us
    all_to_all x1, blocking collectives, on_device(): shares = lax.all_to_all(everyone, TP_FIRST, 0, 0, tiled=True)  11.4 us
    pallas_call x5, Pallas kernels, call(): pl.pallas_call(kernel, out_shape=out_shape, in_specs=[pl.BlockSpec(memory...  4.23 us
    all_gather x1, blocking collectives, on_device(): sequences = lax.all_gather(spread, 'core', tiled=True)  2.08 us

profile of v7, /device:TPU:8, one launch (start us, length us, event | category | flops | bytes accessed | tf_op | source)
XLA Modules:
  0.0 67.7 jit_solution(16172747234512423685)
XLA Ops:
  0.6 1.6 %shard_map.85 = (f32[384,128]{1,0:T(8,128)S(1)}, f32[2,16,1024]{2,1,0:T(8,128)S(1)}, bf16[2,1536,256]{2,1,0:T(8,128)(2,1)S(1)}, f32[272,256]{1,0:T(8,128)S(1)}) custom-call(bf16[16,1024]{1,0:T(8,128)(2,1)} %signal_hbm.1, bf16[16,1024]{1,0:T(8,128)(2,1)} %grad_hbm.1, f32[16,1024]{1,0:T(8,128)} %filter_hbm.1, f32[16]{0:T(128)} %gain_hbm.1, ...), custom_call_target="tpu_custom_call" | custom-call | tf_op jit(solution)/shard_map/pallas_call | solution.py:214
  2.2 20.2 %all_to_all.20 = f32[16,24,128]{2,1,0:T(8,128)S(1)} all-to-all(f32[16,24,128]{2,1,0:T(8,128)S(1)} %bitcast.3), channel_id=1, replica_groups=mesh['chip'=16,'core'=2,'tp_far'=2,'tp_even'=4,'tp_next'=2] {'chip'}, dimensions={0} | all-to-all | bytes 393216 | tf_op jit(solution)/shard_map/all_to_all | solution.py:255
  22.4 2.1 %all_gather.3.in_ref = f32[32,24,128]{2,1,0:T(8,128)S(1)} all-gather(f32[16,24,128]{2,1,0:T(8,128)S(1)} %all_to_all.20), channel_id=1, replica_groups=mesh['chip'=16,'core'=2,'tp_far'=2,'tp_even'=4,'tp_next'=2] {'core'}, dimensions={0}, use_global_device_ids=true | all-gather | bytes 589824 | tf_op jit(solution)/shard_map/all_gather | solution.py:256
  24.5 1.9 %shard_map.86 = f32[16,24,128]{2,1,0:T(8,128)S(1)} custom-call(f32[32,24,128]{2,1,0:T(8,128)S(1)} %all_gather.3.in_ref, bf16[2,1536,256]{2,1,0:T(8,128)(2,1)S(1)} %get-tuple-element.8.table, f32[272,256]{1,0:T(8,128)S(1)} %get-tuple-element.9.twist), custom_call_target="tpu_custom_call" | custom-call | tf_op jit(solution)/shard_map/pallas_call | solution.py:214
  26.4 13.0 %all_to_all.21.in_ref = f32[16,24,128]{2,1,0:T(8,128)S(1)} all-to-all(f32[16,24,128]{2,1,0:T(8,128)S(1)} %shard_map.86), channel_id=1, replica_groups=mesh['chip'=16,'core'=2,'tp_far'=2,'tp_even'=4,'tp_next'=2] {'chip'}, dimensions={0} | all-to-all | bytes 393216 | tf_op jit(solution)/shard_map/all_to_all | solution.py:267
  39.4 11.4 %all_to_all.22.in_ref = f32[4,128,128]{2,1,0:T(8,128)S(1)} all-to-all(f32[4,128,128]{2,1,0:T(8,128)S(1)} %shard_map.87), channel_id=1, replica_groups=mesh['chip'=16,'core'=2,'tp_far'=2,'tp_even'=4,'tp_next'=2] {'tp_far','t..., dimensions={0} | all-to-all | bytes 524288 | tf_op jit(solution)/shard_map/all_to_all | solution.py:271
  50.8 16.2 %all_to_all.23.shares_ref = f32[4,128,128]{2,1,0:T(8,128)S(1)} all-to-all(f32[4,128,128]{2,1,0:T(8,128)S(1)} %shard_map.88), channel_id=1, replica_groups=mesh['chip'=16,'core'=2,'tp_far'=2,'tp_even'=4,'tp_next'=2] {'tp_even'}, dimensions={0} | all-to-all | bytes 524288 | tf_op jit(solution)/shard_map/all_to_all | solution.py:273
  67.0 0.7 %shard_map.89 = (bf16[16,1024]{1,0:T(8,128)(2,1)}, bf16[16,1024]{1,0:T(8,128)(2,1)}, f32[16,1024]{1,0:T(8,128)}) custom-call(f32[384,128]{1,0:T(8,128)S(1)} %bitcast.2, f32[2,16,1024]{2,1,0:T(8,128)S(1)} %get-tuple-element.10.skip_ref, f32[4,128,128]{2,1,0:T(8,128)S(1)} %all_to_all.23.shares_ref), custom_call_target="tpu_custom_call" | custom-call | tf_op jit(solution)/shard_map/pallas_call | solution.py:214
  (2 shorter events, 0.0 us)

commit v8 on v7

--- a/solution.py
+++ b/solution.py
@@ -51,9 +51,8 @@
     inner_there = np.block([[c, -s], [s, c]])
     inner_back = np.block([[c, s], [-s, c]])
     back_columns = np.concatenate(np.split(outer_back, 2 * rows // (2 * LANES), axis=1), axis=0)
-    stacked = np.concatenate([outer, inner_there, inner_back, back_columns], axis=0)
-    high, low = split_table(stacked)
-    return np.stack([high, low]), twist.astype(np.float32)
+    parts = [np.stack(split_table(part)) for part in (outer, inner_there, inner_back, *np.split(back_columns, 2))]
+    return (*parts, twist.astype(np.float32))
 
 
 def split(x):
@@ -67,8 +66,8 @@
 
 
 def pack_kernel(
-    signal_hbm, grad_hbm, filter_hbm, gain_hbm, table_hbm, twist_hbm,
-    out_ref, skip_ref, table_ref, twist_ref,
+    signal_hbm, grad_hbm, filter_hbm, gain_hbm, table_hbm,
+    out_ref, skip_ref, table_ref,
     signal_ref, grad_ref, filter_ref, gain_ref, sems,
 ):
     pairs = (
@@ -77,7 +76,6 @@
         (filter_hbm, filter_ref),
         (gain_hbm, gain_ref),
         (table_hbm, table_ref),
-        (twist_hbm, twist_ref),
     )
     copies = [pltpu.make_async_copy(source, target, sems.at[k]) for k, (source, target) in enumerate(pairs)]
     for copy in copies:
@@ -101,34 +99,28 @@
         copy.wait()
 
 
-def convolve_kernel(in_ref, table, twist, out_ref, a_ref, u_h, u_l):
+def convolve_kernel(in_ref, outer, there, back, first_back, second_back, twist, out_ref, a_ref, u_h, u_l):
     chips = out_ref.shape[0]
     half = chips * SUBLANES
     rows = 2 * half
     core = lax.axis_index("core")
 
-    def part(number, start, count):
-        return table[number, start : start + count, :]
-
     def sequence(number):
         return in_ref[:, number * 8 : number * 8 + 8, :].reshape(rows, LANES)
 
     both = jnp.concatenate([sequence(0), sequence(1)], axis=1).astype(jnp.bfloat16)
     taps_h, taps_l = split(sequence(2))
-    outer_h, outer_l = part(0, 0, 2 * rows), part(1, 0, 2 * rows)
+    outer_h, outer_l = outer[0], outer[1]
     a_ref[:, : 2 * LANES] = dot(outer_h, both) + dot(outer_l, both)
     turned = dot(outer_h, jnp.concatenate([taps_h, taps_l], axis=1))
     a_ref[:, 2 * LANES :] = turned[:, :LANES] + turned[:, LANES:] + dot(outer_l, taps_h)
-    at = 2 * rows
-    there_h, there_l = part(0, at, 2 * LANES), part(1, at, 2 * LANES)
-    at += 2 * LANES
-    back_h, back_l = part(0, at, 2 * LANES), part(1, at, 2 * LANES)
-    at += 2 * LANES
+    there_h, there_l = there[0], there[1]
+    back_h, back_l = back[0], back[1]
 
     last = a_ref[rows : rows + 1, :]
     first_row = lax.broadcasted_iota(jnp.int32, (16, 1), 0) == 0
 
-    for start, count in ((0, rows // 2), (rows // 2, rows // 2), (rows, 16)):
+    for start, count in [(k, 64) for k in range(0, rows, 64)] + [(rows, 16)]:
         tr = twist[start : start + count, :LANES]
         ti = twist[start : start + count, LANES:]
         pieces = []
@@ -170,12 +162,11 @@
             u_l[rows + start : rows + start + count, lanes] = imag_l
 
     y = jnp.zeros((half, 3 * LANES), jnp.float32)
-    for inner in range(0, 2 * rows, 2 * LANES):
-        here = slice(inner, inner + 2 * LANES)
-        mine = pl.ds(pl.multiple_of(at + core * half, half), half)
-        columns_h, columns_l = table[0, mine, :], table[1, mine, :]
+    mine = pl.ds(pl.multiple_of(core * half, half), half)
+    for number, columns in enumerate((first_back, second_back)):
+        here = slice(number * rows, (number + 1) * rows)
+        columns_h, columns_l = columns[0, mine, :], columns[1, mine, :]
         y += dot(columns_h, u_h[here, :]) + dot(columns_h, u_l[here, :]) + dot(columns_l, u_h[here, :])
-        at += rows
     for number in range(3):
         out_ref[:, number * 8 : number * 8 + 8, :] = y[:, number * LANES : (number + 1) * LANES].reshape(chips, SUBLANES, LANES)
 
@@ -228,19 +219,18 @@
     assert channels == chips and tokens == SUBLANES * LANES
     length = tokens * ctx
     rows = length // LANES
-    table, twist = make_tables(rows, ctx, 1.0 / math.sqrt(length))
+    outer, *tables = make_tables(rows, ctx, 1.0 / math.sqrt(length))
 
     in_hbm = [
         pltpu.with_memory_space_constraint(x, pltpu.HBM)
-        for x in (signal, grad_out, filter_taps, skip_gain, table, twist)
+        for x in (signal, grad_out, filter_taps, skip_gain, outer)
     ]
-    packed, skip, table, twist = call(
+    packed, skip, outer = call(
         pack_kernel,
         (
             pltpu.VMEM((chips * 24, LANES), jnp.float32),
             pltpu.VMEM((2, channels, tokens), jnp.float32),
-            pltpu.VMEM(table.shape, table.dtype),
-            pltpu.VMEM(twist.shape, twist.dtype),
+            pltpu.VMEM(outer.shape, outer.dtype),
         ),
         in_hbm,
         scratch=(
@@ -248,16 +238,16 @@
             pltpu.VMEM(grad_out.shape, grad_out.dtype),
             pltpu.VMEM(filter_taps.shape, filter_taps.dtype),
             pltpu.SMEM(skip_gain.shape, skip_gain.dtype),
-            pltpu.SemaphoreType.DMA((6,)),
-        ),
-        spaces=[pltpu.HBM] * 6,
+            pltpu.SemaphoreType.DMA((5,)),
+        ),
+        spaces=[pltpu.HBM] * 5,
     )
     spread = lax.all_to_all(packed.reshape(chips, 24, LANES), "chip", 0, 0, tiled=True)
     sequences = lax.all_gather(spread, "core", tiled=True)
     results = call(
         convolve_kernel,
         jax.ShapeDtypeStruct((chips, 24, LANES), jnp.float32),
-        (sequences, table, twist),
+        (sequences, outer, *tables),
         scratch=(
             pltpu.VMEM((2 * rows, 3 * LANES), jnp.float32),
             pltpu.VMEM((2 * rows, 3 * LANES), jnp.bfloat16),

time: 68 us -> 67.8 us (level)
  no operation moved by 1% of the time
where the time goes in v8:
time: 67.8 us; the launch traced here: 67.6 us
  blocking collectives  63.1 us (93%)
  Pallas kernels  3.7 us (5%)
  between operations  0.7 us (1%)
    all_to_all x1, blocking collectives, on_device(): lax.all_to_all(packed.reshape(chips, 24, LANES), 'chip', 0, 0, tiled=True)  20.3 us
    all_to_all x1, blocking collectives, on_device(): shares = lax.all_to_all(everyone, TP_SECOND, 0, 0, tiled=True)  16.2 us
    all_to_all x1, blocking collectives, on_device(): returned = lax.all_to_all(results, 'chip', 0, 0, tiled=True)  13 us
    all_to_all x1, blocking collectives, on_device(): shares = lax.all_to_all(everyone, TP_FIRST, 0, 0, tiled=True)  11.4 us
    pallas_call x5, Pallas kernels, call(): pl.pallas_call(kernel, out_shape=out_shape, in_specs=[pl.BlockSpec(memory...  3.7 us
    all_gather x1, blocking collectives, on_device(): sequences = lax.all_gather(spread, 'core', tiled=True)  2.21 us

profile of v8, /device:TPU:8, one launch (start us, length us, event | category | flops | bytes accessed | tf_op | source)
XLA Modules:
  0.0 67.6 jit_solution(6983735227755021319)
XLA Ops:
  0.6 0.0 copy-start.3
  0.6 0.0 copy-start.4
  0.7 1.2 %shard_map.121 = (f32[384,128]{1,0:T(8,128)S(1)}, f32[2,16,1024]{2,1,0:T(8,128)S(1)}, bf16[2,512,256]{2,1,0:T(8,128)(2,1)S(1)}) custom-call(bf16[16,1024]{1,0:T(8,128)(2,1)} %signal_hbm.1, bf16[16,1024]{1,0:T(8,128)(2,1)} %grad_hbm.1, f32[16,1024]{1,0:T(8,128)} %filter_hbm.1, f32[16]{0:T(128)} %gain_hbm.1, bf16[2,512,256]{2,1,0:T(8,128)(2,1)} %constant.12.clone.table_hbm), custom_call_target="tpu_custom_call" | custom-call | tf_op jit(solution)/shard_map/pallas_call | solution.py:205
  1.9 0.0 copy-start.2
  1.9 20.3 %all_to_all.20 = f32[16,24,128]{2,1,0:T(8,128)S(1)} all-to-all(f32[16,24,128]{2,1,0:T(8,128)S(1)} %bitcast.3), channel_id=1, replica_groups=mesh['chip'=16,'core'=2,'tp_far'=2,'tp_even'=4,'tp_next'=2] {'chip'}, dimensions={0} | all-to-all | bytes 393216 | tf_op jit(solution)/shard_map/all_to_all | solution.py:245
  22.2 0.0 copy-start
  22.2 0.0 copy-start.1
  22.2 2.2 %all_gather.3.in_ref = f32[32,24,128]{2,1,0:T(8,128)S(1)} all-gather(f32[16,24,128]{2,1,0:T(8,128)S(1)} %all_to_all.20), channel_id=1, replica_groups=mesh['chip'=16,'core'=2,'tp_far'=2,'tp_even'=4,'tp_next'=2] {'core'}, dimensions={0}, use_global_device_ids=true | all-gather | bytes 589824 | tf_op jit(solution)/shard_map/all_gather | solution.py:246
  24.4 0.0 copy-done.3
  24.4 0.0 copy-done.4
  24.4 0.0 copy-done.2
  24.4 0.0 copy-done
  24.5 0.0 copy-done.1
  24.5 1.8 %shard_map.122 = f32[16,24,128]{2,1,0:T(8,128)S(1)} custom-call(f32[32,24,128]{2,1,0:T(8,128)S(1)} %all_gather.3.in_ref, bf16[2,512,256]{2,1,0:T(8,128)(2,1)S(1)} %get-tuple-element.7.outer, bf16[2,256,256]{2,1,0:T(8,128)(2,1)S(1)} %copy-done.4, bf16[2,256,256]{2,1,0:T(8,128)(2,1)S(1)} %copy-done.3, bf16[2,256,256]{2,1,0:T(8,128)(2,1)S(1)} %copy-done.2, ...), custom_call_target="tpu_custom_call" | custom-call | tf_op jit(solution)/shard_map/pallas_call | solution.py:205
  26.2 13.0 %all_to_all.21.in_ref = f32[16,24,128]{2,1,0:T(8,128)S(1)} all-to-all(f32[16,24,128]{2,1,0:T(8,128)S(1)} %shard_map.122), channel_id=1, replica_groups=mesh['chip'=16,'core'=2,'tp_far'=2,'tp_even'=4,'tp_next'=2] {'chip'}, dimensions={0} | all-to-all | bytes 393216 | tf_op jit(solution)/shard_map/all_to_all | solution.py:257
  39.2 11.4 %all_to_all.22.in_ref = f32[4,128,128]{2,1,0:T(8,128)S(1)} all-to-all(f32[4,128,128]{2,1,0:T(8,128)S(1)} %shard_map.123), channel_id=1, replica_groups=mesh['chip'=16,'core'=2,'tp_far'=2,'tp_even'=4,'tp_next'=2] {'tp_far','t..., dimensions={0} | all-to-all | bytes 524288 | tf_op jit(solution)/shard_map/all_to_all | solution.py:261
  50.6 16.2 %all_to_all.23.shares_ref = f32[4,128,128]{2,1,0:T(8,128)S(1)} all-to-all(f32[4,128,128]{2,1,0:T(8,128)S(1)} %shard_map.124), channel_id=1, replica_groups=mesh['chip'=16,'core'=2,'tp_far'=2,'tp_even'=4,'tp_next'=2] {'tp_even'}, dimensions={0} | all-to-all | bytes 524288 | tf_op jit(solution)/shard_map/all_to_all | solution.py:263
  66.9 0.7 %shard_map.125 = (bf16[16,1024]{1,0:T(8,128)(2,1)}, bf16[16,1024]{1,0:T(8,128)(2,1)}, f32[16,1024]{1,0:T(8,128)}) custom-call(f32[384,128]{1,0:T(8,128)S(1)} %bitcast.2, f32[2,16,1024]{2,1,0:T(8,128)S(1)} %get-tuple-element.8.skip_ref, f32[4,128,128]{2,1,0:T(8,128)S(1)} %all_to_all.23.shares_ref), custom_call_target="tpu_custom_call" | custom-call | tf_op jit(solution)/shard_map/pallas_call | solution.py:205
  (2 shorter events, 0.0 us)
Async XLA Ops:
  0.6 23.8 %copy-start.3 = (bf16[2,256,256]{2,1,0:T(8,128)(2,1)S(1)}, bf16[2,256,256]{2,1,0:T(8,128)(2,1)}, u32[]{:S(2)}) copy-start(bf16[2,256,256]{2,1,0:T(8,128)(2,1)} %constant.14.clone.back) | copy-start | bytes 786436
  0.6 23.8 %copy-start.4 = (bf16[2,256,256]{2,1,0:T(8,128)(2,1)S(1)}, bf16[2,256,256]{2,1,0:T(8,128)(2,1)}, u32[]{:S(2)}) copy-start(bf16[2,256,256]{2,1,0:T(8,128)(2,1)} %constant.13.clone.there) | copy-start | bytes 786436
  1.9 22.6 %copy-start.2 = (bf16[2,256,256]{2,1,0:T(8,128)(2,1)S(1)}, bf16[2,256,256]{2,1,0:T(8,128)(2,1)}, u32[]{:S(2)}) copy-start(bf16[2,256,256]{2,1,0:T(8,128)(2,1)} %constant.15.clone.first_back) | copy-start | bytes 786436
  22.2 2.2 %copy-start = (f32[272,256]{1,0:T(8,128)S(1)}, f32[272,256]{1,0:T(8,128)}, u32[]{:S(2)}) copy-start(f32[272,256]{1,0:T(8,128)} %constant.17.clone.twist) | copy-start | bytes 835588
  22.2 2.2 %copy-start.1 = (bf16[2,256,256]{2,1,0:T(8,128)(2,1)S(1)}, bf16[2,256,256]{2,1,0:T(8,128)(2,1)}, u32[]{:S(2)}) copy-start(bf16[2,256,256]{2,1,0:T(8,128)(2,1)} %constant.16.clone.second_back) | copy-start | bytes 786436

commit v9 on v8

--- a/solution.py
+++ b/solution.py
@@ -99,7 +99,7 @@
         copy.wait()
 
 
-def convolve_kernel(in_ref, outer, there, back, first_back, second_back, twist, out_ref, a_ref, u_h, u_l):
+def convolve_kernel(in_ref, outer, there, back, first_back, second_back, twist, out_ref, everyone_ref, a_ref, u_h, u_l):
     chips = out_ref.shape[0]
     half = chips * SUBLANES
     rows = 2 * half
@@ -167,33 +167,35 @@
         here = slice(number * rows, (number + 1) * rows)
         columns_h, columns_l = columns[0, mine, :], columns[1, mine, :]
         y += dot(columns_h, u_h[here, :]) + dot(columns_h, u_l[here, :]) + dot(columns_l, u_h[here, :])
-    for number in range(3):
+    for number in range(2):
         out_ref[:, number * 8 : number * 8 + 8, :] = y[:, number * LANES : (number + 1) * LANES].reshape(chips, SUBLANES, LANES)
-
-
-def collect_kernel(in_ref, out_ref):
-    mine = in_ref[:, 16:, :].reshape(out_ref.shape[1:])
-    for place in range(out_ref.shape[0]):
-        out_ref[place] = mine
-
-
-def add_kernel(in_ref, out_ref):
+    for place in range(everyone_ref.shape[0]):
+        everyone_ref[place] = y[:, 2 * LANES :]
+
+
+def sum_of(in_ref):
     total = in_ref[0]
     for place in range(1, in_ref.shape[0]):
         total += in_ref[place]
+    return total
+
+
+def add_kernel(in_ref, out_ref):
+    total = sum_of(in_ref)
     for place in range(out_ref.shape[0]):
         out_ref[place] = total
 
 
-def finish_kernel(in_ref, skip_ref, shares_ref, out_ref, back_ref, corr_ref, total_ref):
+def join_kernel(in_ref, shares_ref, out_ref):
+    out_ref[:, :16, :] = in_ref[...]
+    out_ref[:, 16:, :] = sum_of(shares_ref).reshape(out_ref.shape[0], SUBLANES, LANES)
+
+
+def finish_kernel(in_ref, skip_ref, out_ref, back_ref, corr_ref):
     channels = corr_ref.shape[0]
-    total = shares_ref[0]
-    for place in range(1, shares_ref.shape[0]):
-        total += shares_ref[place]
-    total_ref[...] = total
     for chunk in range(SUBLANES):
         lanes = slice(chunk * LANES, (chunk + 1) * LANES)
-        corr_ref[:, lanes] = total_ref[pl.ds(chunk, channels, stride=SUBLANES), :]
+        corr_ref[:, lanes] = in_ref[pl.ds(16 + chunk, channels, stride=24), :]
         for number, result in enumerate((out_ref, back_ref)):
             conv = in_ref[pl.ds(number * 8 + chunk, channels, stride=24), :]
             result[:, lanes] = (conv + skip_ref[number, :, lanes]).astype(jnp.bfloat16)
@@ -244,9 +246,13 @@
     )
     spread = lax.all_to_all(packed.reshape(chips, 24, LANES), "chip", 0, 0, tiled=True)
     sequences = lax.all_gather(spread, "core", tiled=True)
-    results = call(
+    first, second = lax.axis_size(TP_FIRST), lax.axis_size(TP_SECOND)
+    results, everyone = call(
         convolve_kernel,
-        jax.ShapeDtypeStruct((chips, 24, LANES), jnp.float32),
+        (
+            pltpu.VMEM((chips, 16, LANES), jnp.float32),
+            pltpu.VMEM((first, rows // 2, LANES), jnp.float32),
+        ),
         (sequences, outer, *tables),
         scratch=(
             pltpu.VMEM((2 * rows, 3 * LANES), jnp.float32),
@@ -254,13 +260,11 @@
             pltpu.VMEM((2 * rows, 3 * LANES), jnp.bfloat16),
         ),
     )
-    returned = lax.all_to_all(results, "chip", 0, 0, tiled=True)
-    shape = (channels * SUBLANES, LANES)
-    first, second = lax.axis_size(TP_FIRST), lax.axis_size(TP_SECOND)
-    everyone = call(collect_kernel, jax.ShapeDtypeStruct((first, *shape), jnp.float32), (returned,))
     shares = lax.all_to_all(everyone, TP_FIRST, 0, 0, tiled=True)
-    everyone = call(add_kernel, jax.ShapeDtypeStruct((second, *shape), jnp.float32), (shares,))
+    everyone = call(add_kernel, jax.ShapeDtypeStruct((second, rows // 2, LANES), jnp.float32), (shares,))
     shares = lax.all_to_all(everyone, TP_SECOND, 0, 0, tiled=True)
+    joined = call(join_kernel, jax.ShapeDtypeStruct((chips, 24, LANES), jnp.float32), (results, shares))
+    returned = lax.all_to_all(joined, "chip", 0, 0, tiled=True)
     output, grad_signal, grad_filter = call(
         finish_kernel,
         (
@@ -268,8 +272,7 @@
             jax.ShapeDtypeStruct((channels, tokens), jnp.bfloat16),
             jax.ShapeDtypeStruct((channels, tokens), jnp.float32),
         ),
-        (returned.reshape(chips * 24, LANES), skip, shares),
-        scratch=(pltpu.VMEM(shape, jnp.float32),),
+        (returned.reshape(chips * 24, LANES), skip),
     )
     return (output, grad_signal, grad_filter)
 

time: 67.8 us -> 68.4 us (level)
  the two profiles are of different devices: /device:TPU:8 before, /device:TPU:2 now
where the time goes in v9:
time: 68.4 us; the launch traced here: 68.1 us
  blocking collectives  63.6 us (93%)
  Pallas kernels  3.71 us (5%)
  between operations  0.7 us (1%)
    all_to_all x1, blocking collectives, on_device(): lax.all_to_all(packed.reshape(chips, 24, LANES), 'chip', 0, 0, tiled=True)  20.2 us
    all_to_all x1, blocking collectives, on_device(): shares = lax.all_to_all(everyone, TP_SECOND, 0, 0, tiled=True)  16.7 us
    all_to_all x1, blocking collectives, on_device(): returned = lax.all_to_all(joined, 'chip', 0, 0, tiled=True)  12.8 us
    all_to_all x1, blocking collectives, on_device(): shares = lax.all_to_all(everyone, TP_FIRST, 0, 0, tiled=True)  11.7 us
    pallas_call x5, Pallas kernels, call(): pl.pallas_call(kernel, out_shape=out_shape, in_specs=[pl.BlockSpec(memory...  3.71 us
    all_gather x1, blocking collectives, on_device(): sequences = lax.all_gather(spread, 'core', tiled=True)  2.21 us

profile of v9, /device:TPU:2, one launch (start us, length us, event | category | flops | bytes accessed | tf_op | source)
XLA Modules:
  0.0 68.1 jit_solution(10627205642544503731)
XLA Ops:
  0.6 0.0 copy-start.3
  0.6 0.0 copy-start.4
  0.7 1.2 %shard_map.121 = (f32[384,128]{1,0:T(8,128)S(1)}, f32[2,16,1024]{2,1,0:T(8,128)S(1)}, bf16[2,512,256]{2,1,0:T(8,128)(2,1)S(1)}) custom-call(bf16[16,1024]{1,0:T(8,128)(2,1)} %signal_hbm.1, bf16[16,1024]{1,0:T(8,128)(2,1)} %grad_hbm.1, f32[16,1024]{1,0:T(8,128)} %filter_hbm.1, f32[16]{0:T(128)} %gain_hbm.1, bf16[2,512,256]{2,1,0:T(8,128)(2,1)} %constant.12.clone.table_hbm), custom_call_target="tpu_custom_call" | custom-call | tf_op jit(solution)/shard_map/pallas_call | solution.py:207
  1.9 0.0 copy-start.2
  1.9 20.2 %all_to_all.20 = f32[16,24,128]{2,1,0:T(8,128)S(1)} all-to-all(f32[16,24,128]{2,1,0:T(8,128)S(1)} %bitcast.3), channel_id=1, replica_groups=mesh['chip'=16,'core'=2,'tp_far'=2,'tp_even'=4,'tp_next'=2] {'chip'}, dimensions={0} | all-to-all | bytes 393216 | tf_op jit(solution)/shard_map/all_to_all | solution.py:247
  22.1 0.0 copy-start
  22.1 0.0 copy-start.1
  22.1 2.2 %all_gather.3.in_ref = f32[32,24,128]{2,1,0:T(8,128)S(1)} all-gather(f32[16,24,128]{2,1,0:T(8,128)S(1)} %all_to_all.20), channel_id=1, replica_groups=mesh['chip'=16,'core'=2,'tp_far'=2,'tp_even'=4,'tp_next'=2] {'core'}, dimensions={0}, use_global_device_ids=true | all-gather | bytes 589824 | tf_op jit(solution)/shard_map/all_gather | solution.py:248
  24.3 0.0 copy-done.3
  24.3 0.0 copy-done.4
  24.3 0.0 copy-done.2
  24.3 0.0 copy-done
  24.4 0.0 copy-done.1
  24.4 1.8 %shard_map.122 = (f32[16,16,128]{2,1,0:T(8,128)S(1)}, f32[4,128,128]{2,1,0:T(8,128)S(1)}) custom-call(f32[32,24,128]{2,1,0:T(8,128)S(1)} %all_gather.3.in_ref, bf16[2,512,256]{2,1,0:T(8,128)(2,1)S(1)} %get-tuple-element.9.outer, bf16[2,256,256]{2,1,0:T(8,128)(2,1)S(1)} %copy-done.4, bf16[2,256,256]{2,1,0:T(8,128)(2,1)S(1)} %copy-done.3, ...), custom_call_target="tpu_custom_call" | custom-call | tf_op jit(solution)/shard_map/pallas_call | solution.py:207
  26.1 11.7 %all_to_all.21.in_ref = f32[4,128,128]{2,1,0:T(8,128)S(1)} all-to-all(f32[4,128,128]{2,1,0:T(8,128)S(1)} %get-tuple-element.11), channel_id=1, replica_groups=mesh['chip'=16,'core'=2,'tp_far'=2,'tp_even'=4,'tp_next'=2] {'tp_far','t..., dimensions={0} | all-to-all | bytes 524288 | tf_op jit(solution)/shard_map/all_to_all | solution.py:263
  37.9 16.7 %all_to_all.22.shares_ref = f32[4,128,128]{2,1,0:T(8,128)S(1)} all-to-all(f32[4,128,128]{2,1,0:T(8,128)S(1)} %shard_map.123), channel_id=1, replica_groups=mesh['chip'=16,'core'=2,'tp_far'=2,'tp_even'=4,'tp_next'=2] {'tp_even'}, dimensions={0} | all-to-all | bytes 524288 | tf_op jit(solution)/shard_map/all_to_all | solution.py:265
  54.6 12.8 %all_to_all.23 = f32[16,24,128]{2,1,0:T(8,128)S(1)} all-to-all(f32[16,24,128]{2,1,0:T(8,128)S(1)} %shard_map.124), channel_id=1, replica_groups=mesh['chip'=16,'core'=2,'tp_far'=2,'tp_even'=4,'tp_next'=2] {'chip'}, dimensions={0} | all-to-all | bytes 393216 | tf_op jit(solution)/shard_map/all_to_all | solution.py:267
  67.4 0.7 %shard_map.125 = (bf16[16,1024]{1,0:T(8,128)(2,1)}, bf16[16,1024]{1,0:T(8,128)(2,1)}, f32[16,1024]{1,0:T(8,128)}) custom-call(f32[384,128]{1,0:T(8,128)S(1)} %bitcast.2, f32[2,16,1024]{2,1,0:T(8,128)S(1)} %get-tuple-element.12.skip_ref), custom_call_target="tpu_custom_call" | custom-call | tf_op jit(solution)/shard_map/pallas_call | solution.py:207
  (2 shorter events, 0.0 us)
Async XLA Ops:
  0.6 23.7 %copy-start.3 = (bf16[2,256,256]{2,1,0:T(8,128)(2,1)S(1)}, bf16[2,256,256]{2,1,0:T(8,128)(2,1)}, u32[]{:S(2)}) copy-start(bf16[2,256,256]{2,1,0:T(8,128)(2,1)} %constant.14.clone.back) | copy-start | bytes 786436
  0.6 23.7 %copy-start.4 = (bf16[2,256,256]{2,1,0:T(8,128)(2,1)S(1)}, bf16[2,256,256]{2,1,0:T(8,128)(2,1)}, u32[]{:S(2)}) copy-start(bf16[2,256,256]{2,1,0:T(8,128)(2,1)} %constant.13.clone.there) | copy-start | bytes 786436
  1.9 22.5 %copy-start.2 = (bf16[2,256,256]{2,1,0:T(8,128)(2,1)S(1)}, bf16[2,256,256]{2,1,0:T(8,128)(2,1)}, u32[]{:S(2)}) copy-start(bf16[2,256,256]{2,1,0:T(8,128)(2,1)} %constant.15.clone.first_back) | copy-start | bytes 786436
  22.1 2.2 %copy-start = (f32[272,256]{1,0:T(8,128)S(1)}, f32[272,256]{1,0:T(8,128)}, u32[]{:S(2)}) copy-start(f32[272,256]{1,0:T(8,128)} %constant.17.clone.twist) | copy-start | bytes 835588
  22.1 2.2 %copy-start.1 = (bf16[2,256,256]{2,1,0:T(8,128)(2,1)S(1)}, bf16[2,256,256]{2,1,0:T(8,128)(2,1)}, u32[]{:S(2)}) copy-start(bf16[2,256,256]{2,1,0:T(8,128)(2,1)} %constant.16.clone.second_back) | copy-start | bytes 786436

commit v10 on v8

--- a/solution.py
+++ b/solution.py
@@ -14,8 +14,8 @@
 SUBLANES = 8
 CTX = ("chip", "core")
 TP = ("tp_far", "tp_even", "tp_next")
-TP_FIRST = ("tp_far", "tp_next")
-TP_SECOND = ("tp_even",)
+TP_FIRST = ("tp_even",)
+TP_SECOND = ("tp_far", "tp_next")
 VMEM_BYTES = 24 * 1024 * 1024
 
 

time: 67.8 us -> 68.8 us (1.015)
  the two profiles are of different devices: /device:TPU:8 before, /device:TPU:64 now
where the time goes in v10:
time: 68.8 us; the launch traced here: 68.6 us
  blocking collectives  64.1 us (93%)
  Pallas kernels  3.71 us (5%)
  between operations  0.7 us (1%)
    all_to_all x1, blocking collectives, on_device(): lax.all_to_all(packed.reshape(chips, 24, LANES), 'chip', 0, 0, tiled=True)  20 us
    all_to_all x1, blocking collectives, on_device(): shares = lax.all_to_all(everyone, TP_FIRST, 0, 0, tiled=True)  16.7 us
    all_to_all x1, blocking collectives, on_device(): returned = lax.all_to_all(results, 'chip', 0, 0, tiled=True)  13 us
    all_to_all x1, blocking collectives, on_device(): shares = lax.all_to_all(everyone, TP_SECOND, 0, 0, tiled=True)  12.2 us
    pallas_call x5, Pallas kernels, call(): pl.pallas_call(kernel, out_shape=out_shape, in_specs=[pl.BlockSpec(memory...  3.71 us
    all_gather x1, blocking collectives, on_device(): sequences = lax.all_gather(spread, 'core', tiled=True)  2.21 us

profile of v10, /device:TPU:64, one launch (start us, length us, event | category | flops | bytes accessed | tf_op | source)
XLA Modules:
  0.0 68.6 jit_solution(9596831797551587217)
XLA Ops:
  0.6 0.0 copy-start.3
  0.6 0.0 copy-start.4
  0.7 1.2 %shard_map.121 = (f32[384,128]{1,0:T(8,128)S(1)}, f32[2,16,1024]{2,1,0:T(8,128)S(1)}, bf16[2,512,256]{2,1,0:T(8,128)(2,1)S(1)}) custom-call(bf16[16,1024]{1,0:T(8,128)(2,1)} %signal_hbm.1, bf16[16,1024]{1,0:T(8,128)(2,1)} %grad_hbm.1, f32[16,1024]{1,0:T(8,128)} %filter_hbm.1, f32[16]{0:T(128)} %gain_hbm.1, bf16[2,512,256]{2,1,0:T(8,128)(2,1)} %constant.12.clone.table_hbm), custom_call_target="tpu_custom_call" | custom-call | tf_op jit(solution)/shard_map/pallas_call | solution.py:205
  1.9 0.0 copy-start.2
  1.9 20.0 %all_to_all.20 = f32[16,24,128]{2,1,0:T(8,128)S(1)} all-to-all(f32[16,24,128]{2,1,0:T(8,128)S(1)} %bitcast.3), channel_id=1, replica_groups=mesh['chip'=16,'core'=2,'tp_far'=2,'tp_even'=4,'tp_next'=2] {'chip'}, dimensions={0} | all-to-all | bytes 393216 | tf_op jit(solution)/shard_map/all_to_all | solution.py:245
  21.9 0.0 copy-start
  21.9 0.0 copy-start.1
  21.9 2.2 %all_gather.3.in_ref = f32[32,24,128]{2,1,0:T(8,128)S(1)} all-gather(f32[16,24,128]{2,1,0:T(8,128)S(1)} %all_to_all.20), channel_id=1, replica_groups=mesh['chip'=16,'core'=2,'tp_far'=2,'tp_even'=4,'tp_next'=2] {'core'}, dimensions={0}, use_global_device_ids=true | all-gather | bytes 589824 | tf_op jit(solution)/shard_map/all_gather | solution.py:246
  24.1 0.0 copy-done.3
  24.1 0.0 copy-done.4
  24.1 0.0 copy-done.2
  24.1 0.0 copy-done
  24.2 0.0 copy-done.1
  24.2 1.8 %shard_map.122 = f32[16,24,128]{2,1,0:T(8,128)S(1)} custom-call(f32[32,24,128]{2,1,0:T(8,128)S(1)} %all_gather.3.in_ref, bf16[2,512,256]{2,1,0:T(8,128)(2,1)S(1)} %get-tuple-element.7.outer, bf16[2,256,256]{2,1,0:T(8,128)(2,1)S(1)} %copy-done.4, bf16[2,256,256]{2,1,0:T(8,128)(2,1)S(1)} %copy-done.3, bf16[2,256,256]{2,1,0:T(8,128)(2,1)S(1)} %copy-done.2, ...), custom_call_target="tpu_custom_call" | custom-call | tf_op jit(solution)/shard_map/pallas_call | solution.py:205
  25.9 13.0 %all_to_all.21.in_ref = f32[16,24,128]{2,1,0:T(8,128)S(1)} all-to-all(f32[16,24,128]{2,1,0:T(8,128)S(1)} %shard_map.122), channel_id=1, replica_groups=mesh['chip'=16,'core'=2,'tp_far'=2,'tp_even'=4,'tp_next'=2] {'chip'}, dimensions={0} | all-to-all | bytes 393216 | tf_op jit(solution)/shard_map/all_to_all | solution.py:257
  39.0 16.7 %all_to_all.22.in_ref = f32[4,128,128]{2,1,0:T(8,128)S(1)} all-to-all(f32[4,128,128]{2,1,0:T(8,128)S(1)} %shard_map.123), channel_id=1, replica_groups=mesh['chip'=16,'core'=2,'tp_far'=2,'tp_even'=4,'tp_next'=2] {'tp_even'}, dimensions={0} | all-to-all | bytes 524288 | tf_op jit(solution)/shard_map/all_to_all | solution.py:261
  55.7 12.2 %all_to_all.23.shares_ref = f32[4,128,128]{2,1,0:T(8,128)S(1)} all-to-all(f32[4,128,128]{2,1,0:T(8,128)S(1)} %shard_map.124), channel_id=1, replica_groups=mesh['chip'=16,'core'=2,'tp_far'=2,'tp_even'=4,'tp_next'=2] {'tp_far','t..., dimensions={0} | all-to-all | bytes 524288 | tf_op jit(solution)/shard_map/all_to_all | solution.py:263
  67.9 0.7 %shard_map.125 = (bf16[16,1024]{1,0:T(8,128)(2,1)}, bf16[16,1024]{1,0:T(8,128)(2,1)}, f32[16,1024]{1,0:T(8,128)}) custom-call(f32[384,128]{1,0:T(8,128)S(1)} %bitcast.2, f32[2,16,1024]{2,1,0:T(8,128)S(1)} %get-tuple-element.8.skip_ref, f32[4,128,128]{2,1,0:T(8,128)S(1)} %all_to_all.23.shares_ref), custom_call_target="tpu_custom_call" | custom-call | tf_op jit(solution)/shard_map/pallas_call | solution.py:205
  (2 shorter events, 0.0 us)
Async XLA Ops:
  0.6 23.5 %copy-start.3 = (bf16[2,256,256]{2,1,0:T(8,128)(2,1)S(1)}, bf16[2,256,256]{2,1,0:T(8,128)(2,1)}, u32[]{:S(2)}) copy-start(bf16[2,256,256]{2,1,0:T(8,128)(2,1)} %constant.14.clone.back) | copy-start | bytes 786436
  0.6 23.5 %copy-start.4 = (bf16[2,256,256]{2,1,0:T(8,128)(2,1)S(1)}, bf16[2,256,256]{2,1,0:T(8,128)(2,1)}, u32[]{:S(2)}) copy-start(bf16[2,256,256]{2,1,0:T(8,128)(2,1)} %constant.13.clone.there) | copy-start | bytes 786436
  1.9 22.3 %copy-start.2 = (bf16[2,256,256]{2,1,0:T(8,128)(2,1)S(1)}, bf16[2,256,256]{2,1,0:T(8,128)(2,1)}, u32[]{:S(2)}) copy-start(bf16[2,256,256]{2,1,0:T(8,128)(2,1)} %constant.15.clone.first_back) | copy-start | bytes 786436
  21.9 2.2 %copy-start = (f32[272,256]{1,0:T(8,128)S(1)}, f32[272,256]{1,0:T(8,128)}, u32[]{:S(2)}) copy-start(f32[272,256]{1,0:T(8,128)} %constant.17.clone.twist) | copy-start | bytes 835588
  21.9 2.2 %copy-start.1 = (bf16[2,256,256]{2,1,0:T(8,128)(2,1)S(1)}, bf16[2,256,256]{2,1,0:T(8,128)(2,1)}, u32[]{:S(2)}) copy-start(bf16[2,256,256]{2,1,0:T(8,128)(2,1)} %constant.16.clone.second_back) | copy-start | bytes 786436

commit v11 on v9

--- a/solution.py
+++ b/solution.py
@@ -180,10 +180,10 @@
     return total
 
 
-def add_kernel(in_ref, out_ref):
-    total = sum_of(in_ref)
+def collect_kernel(in_ref, out_ref):
+    mine = in_ref[:, 16:, :].reshape(out_ref.shape[1:])
     for place in range(out_ref.shape[0]):
-        out_ref[place] = total
+        out_ref[place] = mine
 
 
 def join_kernel(in_ref, shares_ref, out_ref):
@@ -191,11 +191,15 @@
     out_ref[:, 16:, :] = sum_of(shares_ref).reshape(out_ref.shape[0], SUBLANES, LANES)
 
 
-def finish_kernel(in_ref, skip_ref, out_ref, back_ref, corr_ref):
+def finish_kernel(in_ref, skip_ref, shares_ref, out_ref, back_ref, corr_ref, total_ref):
     channels = corr_ref.shape[0]
+    total = shares_ref[0]
+    for place in range(1, shares_ref.shape[0]):
+        total += shares_ref[place]
+    total_ref[...] = total
     for chunk in range(SUBLANES):
         lanes = slice(chunk * LANES, (chunk + 1) * LANES)
-        corr_ref[:, lanes] = in_ref[pl.ds(16 + chunk, channels, stride=24), :]
+        corr_ref[:, lanes] = total_ref[pl.ds(chunk, channels, stride=SUBLANES), :]
         for number, result in enumerate((out_ref, back_ref)):
             conv = in_ref[pl.ds(number * 8 + chunk, channels, stride=24), :]
             result[:, lanes] = (conv + skip_ref[number, :, lanes]).astype(jnp.bfloat16)
@@ -261,10 +265,11 @@
         ),
     )
     shares = lax.all_to_all(everyone, TP_FIRST, 0, 0, tiled=True)
-    everyone = call(add_kernel, jax.ShapeDtypeStruct((second, rows // 2, LANES), jnp.float32), (shares,))
-    shares = lax.all_to_all(everyone, TP_SECOND, 0, 0, tiled=True)
     joined = call(join_kernel, jax.ShapeDtypeStruct((chips, 24, LANES), jnp.float32), (results, shares))
     returned = lax.all_to_all(joined, "chip", 0, 0, tiled=True)
+    shape = (channels * SUBLANES, LANES)
+    everyone = call(collect_kernel, jax.ShapeDtypeStruct((second, *shape), jnp.float32), (returned,))
+    shares = lax.all_to_all(everyone, TP_SECOND, 0, 0, tiled=True)
     output, grad_signal, grad_filter = call(
         finish_kernel,
         (
@@ -272,7 +277,8 @@
             jax.ShapeDtypeStruct((channels, tokens), jnp.bfloat16),
             jax.ShapeDtypeStruct((channels, tokens), jnp.float32),
         ),
-        (returned.reshape(chips * 24, LANES), skip),
+        (returned.reshape(chips * 24, LANES), skip, shares),
+        scratch=(pltpu.VMEM(shape, jnp.float32),),
     )
     return (output, grad_signal, grad_filter)
 

time: 68.4 us -> 67.9 us (level)
  the two profiles are of different devices: /device:TPU:2 before, /device:TPU:8 now
where the time goes in v11:
time: 67.9 us; the launch traced here: 67.6 us
  blocking collectives  63.2 us (93%)
  Pallas kernels  3.71 us (5%)
  between operations  0.7 us (1%)
    all_to_all x1, blocking collectives, on_device(): lax.all_to_all(packed.reshape(chips, 24, LANES), 'chip', 0, 0, tiled=True)  20.3 us
    all_to_all x1, blocking collectives, on_device(): shares = lax.all_to_all(everyone, TP_SECOND, 0, 0, tiled=True)  16.5 us
    all_to_all x1, blocking collectives, on_device(): returned = lax.all_to_all(joined, 'chip', 0, 0, tiled=True)  12.5 us
    all_to_all x1, blocking collectives, on_device(): shares = lax.all_to_all(everyone, TP_FIRST, 0, 0, tiled=True)  11.7 us
    pallas_call x5, Pallas kernels, call(): pl.pallas_call(kernel, out_shape=out_shape, in_specs=[pl.BlockSpec(memory...  3.71 us
    all_gather x1, blocking collectives, on_device(): sequences = lax.all_gather(spread, 'core', tiled=True)  2.21 us

profile of v11, /device:TPU:8, one launch (start us, length us, event | category | flops | bytes accessed | tf_op | source)
XLA Modules:
  0.0 67.6 jit_solution(962716003149846673)
XLA Ops:
  0.6 0.0 copy-start.3
  0.6 0.0 copy-start.4
  0.7 1.2 %shard_map.121 = (f32[384,128]{1,0:T(8,128)S(1)}, f32[2,16,1024]{2,1,0:T(8,128)S(1)}, bf16[2,512,256]{2,1,0:T(8,128)(2,1)S(1)}) custom-call(bf16[16,1024]{1,0:T(8,128)(2,1)} %signal_hbm.1, bf16[16,1024]{1,0:T(8,128)(2,1)} %grad_hbm.1, f32[16,1024]{1,0:T(8,128)} %filter_hbm.1, f32[16]{0:T(128)} %gain_hbm.1, bf16[2,512,256]{2,1,0:T(8,128)(2,1)} %constant.12.clone.table_hbm), custom_call_target="tpu_custom_call" | custom-call | tf_op jit(solution)/shard_map/pallas_call | solution.py:211
  1.9 0.0 copy-start.2
  1.9 20.3 %all_to_all.20 = f32[16,24,128]{2,1,0:T(8,128)S(1)} all-to-all(f32[16,24,128]{2,1,0:T(8,128)S(1)} %bitcast.3), channel_id=1, replica_groups=mesh['chip'=16,'core'=2,'tp_far'=2,'tp_even'=4,'tp_next'=2] {'chip'}, dimensions={0} | all-to-all | bytes 393216 | tf_op jit(solution)/shard_map/all_to_all | solution.py:251
  22.2 0.0 copy-start
  22.2 0.0 copy-start.1
  22.2 2.2 %all_gather.3.in_ref = f32[32,24,128]{2,1,0:T(8,128)S(1)} all-gather(f32[16,24,128]{2,1,0:T(8,128)S(1)} %all_to_all.20), channel_id=1, replica_groups=mesh['chip'=16,'core'=2,'tp_far'=2,'tp_even'=4,'tp_next'=2] {'core'}, dimensions={0}, use_global_device_ids=true | all-gather | bytes 589824 | tf_op jit(solution)/shard_map/all_gather | solution.py:252
  24.4 0.0 copy-done.3
  24.4 0.0 copy-done.4
  24.4 0.0 copy-done.2
  24.4 0.0 copy-done
  24.5 0.0 copy-done.1
  24.5 1.8 %shard_map.122 = (f32[16,16,128]{2,1,0:T(8,128)S(1)}, f32[4,128,128]{2,1,0:T(8,128)S(1)}) custom-call(f32[32,24,128]{2,1,0:T(8,128)S(1)} %all_gather.3.in_ref, bf16[2,512,256]{2,1,0:T(8,128)(2,1)S(1)} %get-tuple-element.9.outer, bf16[2,256,256]{2,1,0:T(8,128)(2,1)S(1)} %copy-done.4, bf16[2,256,256]{2,1,0:T(8,128)(2,1)S(1)} %copy-done.3, ...), custom_call_target="tpu_custom_call" | custom-call | tf_op jit(solution)/shard_map/pallas_call | solution.py:211
  26.2 11.7 %all_to_all.21.shares_ref = f32[4,128,128]{2,1,0:T(8,128)S(1)} all-to-all(f32[4,128,128]{2,1,0:T(8,128)S(1)} %get-tuple-element.11), channel_id=1, replica_groups=mesh['chip'=16,'core'=2,'tp_far'=2,'tp_even'=4,'tp_next'=2] {'tp_far','t..., dimensions={0} | all-to-all | bytes 524288 | tf_op jit(solution)/shard_map/all_to_all | solution.py:267
  37.9 12.5 %all_to_all.22.in_ref = f32[16,24,128]{2,1,0:T(8,128)S(1)} all-to-all(f32[16,24,128]{2,1,0:T(8,128)S(1)} %shard_map.123), channel_id=1, replica_groups=mesh['chip'=16,'core'=2,'tp_far'=2,'tp_even'=4,'tp_next'=2] {'chip'}, dimensions={0} | all-to-all | bytes 393216 | tf_op jit(solution)/shard_map/all_to_all | solution.py:269
  50.4 16.5 %all_to_all.23.shares_ref = f32[4,128,128]{2,1,0:T(8,128)S(1)} all-to-all(f32[4,128,128]{2,1,0:T(8,128)S(1)} %shard_map.124), channel_id=1, replica_groups=mesh['chip'=16,'core'=2,'tp_far'=2,'tp_even'=4,'tp_next'=2] {'tp_even'}, dimensions={0} | all-to-all | bytes 524288 | tf_op jit(solution)/shard_map/all_to_all | solution.py:272
  66.9 0.7 %shard_map.125 = (bf16[16,1024]{1,0:T(8,128)(2,1)}, bf16[16,1024]{1,0:T(8,128)(2,1)}, f32[16,1024]{1,0:T(8,128)}) custom-call(f32[384,128]{1,0:T(8,128)S(1)} %bitcast.2, f32[2,16,1024]{2,1,0:T(8,128)S(1)} %get-tuple-element.12.skip_ref, f32[4,128,128]{2,1,0:T(8,128)S(1)} %all_to_all.23.shares_ref), custom_call_target="tpu_custom_call" | custom-call | tf_op jit(solution)/shard_map/pallas_call | solution.py:211
  (2 shorter events, 0.0 us)
Async XLA Ops:
  0.6 23.8 %copy-start.3 = (bf16[2,256,256]{2,1,0:T(8,128)(2,1)S(1)}, bf16[2,256,256]{2,1,0:T(8,128)(2,1)}, u32[]{:S(2)}) copy-start(bf16[2,256,256]{2,1,0:T(8,128)(2,1)} %constant.14.clone.back) | copy-start | bytes 786436
  0.6 23.8 %copy-start.4 = (bf16[2,256,256]{2,1,0:T(8,128)(2,1)S(1)}, bf16[2,256,256]{2,1,0:T(8,128)(2,1)}, u32[]{:S(2)}) copy-start(bf16[2,256,256]{2,1,0:T(8,128)(2,1)} %constant.13.clone.there) | copy-start | bytes 786436
  1.9 22.6 %copy-start.2 = (bf16[2,256,256]{2,1,0:T(8,128)(2,1)S(1)}, bf16[2,256,256]{2,1,0:T(8,128)(2,1)}, u32[]{:S(2)}) copy-start(bf16[2,256,256]{2,1,0:T(8,128)(2,1)} %constant.15.clone.first_back) | copy-start | bytes 786436
  22.2 2.2 %copy-start = (f32[272,256]{1,0:T(8,128)S(1)}, f32[272,256]{1,0:T(8,128)}, u32[]{:S(2)}) copy-start(f32[272,256]{1,0:T(8,128)} %constant.17.clone.twist) | copy-start | bytes 835588
  22.2 2.2 %copy-start.1 = (bf16[2,256,256]{2,1,0:T(8,128)(2,1)S(1)}, bf16[2,256,256]{2,1,0:T(8,128)(2,1)}, u32[]{:S(2)}) copy-start(bf16[2,256,256]{2,1,0:T(8,128)(2,1)} %constant.16.clone.second_back) | copy-start | bytes 786436

commit v12 on v8

--- a/solution.py
+++ b/solution.py
@@ -1,3 +1,4 @@
+import functools
 import math
 
 import jax
@@ -25,7 +26,7 @@
     return high, low
 
 
-def make_tables(rows, blocks, scale):
+def make_tables(rows, blocks):
     period = 2 * rows
     padded = period * LANES
     place = np.arange(rows)
@@ -37,9 +38,6 @@
     sines = -np.sin(turn)
     sines[0] = np.where(a % 2 == 0, 1.0, -1.0)
     outer = np.concatenate([cosines, sines], axis=0)
-    weights = np.full((rows,), 2.0)
-    weights[0] = 1.0
-    outer_back = (outer * np.concatenate([weights, weights])[:, None]).T * (scale / padded)
     b = np.arange(LANES)
     kept = np.arange(rows + 1)
     angle = 2.0 * np.pi * (np.outer(kept, b) % padded) / padded
@@ -49,10 +47,10 @@
     inner = 2.0 * np.pi * (np.outer(b, b) % LANES) / LANES
     c, s = np.cos(inner), np.sin(inner)
     inner_there = np.block([[c, -s], [s, c]])
-    inner_back = np.block([[c, s], [-s, c]])
-    back_columns = np.concatenate(np.split(outer_back, 2 * rows // (2 * LANES), axis=1), axis=0)
-    parts = [np.stack(split_table(part)) for part in (outer, inner_there, inner_back, *np.split(back_columns, 2))]
-    return (*parts, twist.astype(np.float32))
+    inner_back = inner_there.T
+    return (
+        *split_table(outer), np.stack(split_table(inner_there)), np.stack(split_table(inner_back)), twist.astype(np.float32)
+    )
 
 
 def split(x):
@@ -61,8 +59,8 @@
     return high, low
 
 
-def dot(x, y):
-    return jnp.dot(x, y, preferred_element_type=jnp.float32)
+def dot(x, y, over=(1, 0)):
+    return lax.dot_general(x, y, (((over[0],), (over[1],)), ((), ())), preferred_element_type=jnp.float32)
 
 
 def pack_kernel(
@@ -95,11 +93,10 @@
         gains = jnp.where(row == channel, gain_ref[channel], gains)
     skip_ref[0] = gains * arrays[0]
     skip_ref[1] = gains * arrays[1]
-    for copy in copies[4:]:
-        copy.wait()
-
-
-def convolve_kernel(in_ref, outer, there, back, first_back, second_back, twist, out_ref, a_ref, u_h, u_l):
+    copies[4].wait()
+
+
+def convolve_kernel(in_ref, outer_ref_h, outer_ref_l, there, back, twist, out_ref, a_ref, u_h, u_l, *, scale):
     chips = out_ref.shape[0]
     half = chips * SUBLANES
     rows = 2 * half
@@ -110,7 +107,7 @@
 
     both = jnp.concatenate([sequence(0), sequence(1)], axis=1).astype(jnp.bfloat16)
     taps_h, taps_l = split(sequence(2))
-    outer_h, outer_l = outer[0], outer[1]
+    outer_h, outer_l = outer_ref_h[...], outer_ref_l[...]
     a_ref[:, : 2 * LANES] = dot(outer_h, both) + dot(outer_l, both)
     turned = dot(outer_h, jnp.concatenate([taps_h, taps_l], axis=1))
     a_ref[:, 2 * LANES :] = turned[:, :LANES] + turned[:, LANES:] + dot(outer_l, taps_h)
@@ -146,6 +143,9 @@
         corr = jnp.concatenate([gr * sr + gi * si, gi * sr - gr * si], axis=1)
         p_h, p_l = split(jnp.concatenate([conv, back, corr], axis=0))
         v = dot(p_h, back_h) + dot(p_l, back_h) + dot(p_h, back_l)
+        if start in (0, rows):
+            weight = jnp.where(lax.broadcasted_iota(jnp.int32, (count, 1), 0) == 0, 0.5, 1.0)
+            tr, ti = tr * weight, ti * weight
         for number in range(3):
             vr = v[number * count : (number + 1) * count, :LANES]
             vi = v[number * count : (number + 1) * count, LANES:]
@@ -161,12 +161,10 @@
             u_h[rows + start : rows + start + count, lanes] = imag_h
             u_l[rows + start : rows + start + count, lanes] = imag_l
 
-    y = jnp.zeros((half, 3 * LANES), jnp.float32)
     mine = pl.ds(pl.multiple_of(core * half, half), half)
-    for number, columns in enumerate((first_back, second_back)):
-        here = slice(number * rows, (number + 1) * rows)
-        columns_h, columns_l = columns[0, mine, :], columns[1, mine, :]
-        y += dot(columns_h, u_h[here, :]) + dot(columns_h, u_l[here, :]) + dot(columns_l, u_h[here, :])
+    columns_h, columns_l = outer_ref_h[:, mine], outer_ref_l[:, mine]
+    y = dot(columns_h, u_h[...], (0, 0)) + dot(columns_h, u_l[...], (0, 0)) + dot(columns_l, u_h[...], (0, 0))
+    y *= scale
     for number in range(3):
         out_ref[:, number * 8 : number * 8 + 8, :] = y[:, number * LANES : (number + 1) * LANES].reshape(chips, SUBLANES, LANES)
 
@@ -219,18 +217,18 @@
     assert channels == chips and tokens == SUBLANES * LANES
     length = tokens * ctx
     rows = length // LANES
-    outer, *tables = make_tables(rows, ctx, 1.0 / math.sqrt(length))
+    outer_h, outer_l, there, back, twist = make_tables(rows, ctx)
 
     in_hbm = [
         pltpu.with_memory_space_constraint(x, pltpu.HBM)
-        for x in (signal, grad_out, filter_taps, skip_gain, outer)
+        for x in (signal, grad_out, filter_taps, skip_gain, there)
     ]
-    packed, skip, outer = call(
+    packed, skip, there = call(
         pack_kernel,
         (
             pltpu.VMEM((chips * 24, LANES), jnp.float32),
             pltpu.VMEM((2, channels, tokens), jnp.float32),
-            pltpu.VMEM(outer.shape, outer.dtype),
+            pltpu.VMEM(there.shape, there.dtype),
         ),
         in_hbm,
         scratch=(
@@ -245,9 +243,9 @@
     spread = lax.all_to_all(packed.reshape(chips, 24, LANES), "chip", 0, 0, tiled=True)
     sequences = lax.all_gather(spread, "core", tiled=True)
     results = call(
-        convolve_kernel,
+        functools.partial(convolve_kernel, scale=2.0 / (2 * length * math.sqrt(length))),
         jax.ShapeDtypeStruct((chips, 24, LANES), jnp.float32),
-        (sequences, outer, *tables),
+        (sequences, outer_h, outer_l, there, back, twist),
         scratch=(
             pltpu.VMEM((2 * rows, 3 * LANES), jnp.float32),
             pltpu.VMEM((2 * rows, 3 * LANES), jnp.bfloat16),

time: 67.8 us -> 67.8 us (level)
  no operation moved by 1% of the time
where the time goes in v12:
time: 67.8 us; the launch traced here: 67.5 us
  blocking collectives  63.1 us (93%)
  Pallas kernels  3.67 us (5%)
  between operations  0.68 us (1%)
    all_to_all x1, blocking collectives, on_device(): lax.all_to_all(packed.reshape(chips, 24, LANES), 'chip', 0, 0, tiled=True)  20.3 us
    all_to_all x1, blocking collectives, on_device(): shares = lax.all_to_all(everyone, TP_SECOND, 0, 0, tiled=True)  16.2 us
    all_to_all x1, blocking collectives, on_device(): returned = lax.all_to_all(results, 'chip', 0, 0, tiled=True)  13 us
    all_to_all x1, blocking collectives, on_device(): shares = lax.all_to_all(everyone, TP_FIRST, 0, 0, tiled=True)  11.4 us
    pallas_call x5, Pallas kernels, call(): pl.pallas_call(kernel, out_shape=out_shape, in_specs=[pl.BlockSpec(memory...  3.67 us
    all_gather x1, blocking collectives, on_device(): sequences = lax.all_gather(spread, 'core', tiled=True)  2.21 us

profile of v12, /device:TPU:8, one launch (start us, length us, event | category | flops | bytes accessed | tf_op | source)
XLA Modules:
  0.0 67.5 jit_solution(10262546592994905125)
XLA Ops:
  0.6 0.0 copy-start.3
  0.6 1.1 %shard_map.112 = (f32[384,128]{1,0:T(8,128)S(1)}, f32[2,16,1024]{2,1,0:T(8,128)S(1)}, bf16[2,256,256]{2,1,0:T(8,128)(2,1)S(1)}) custom-call(bf16[16,1024]{1,0:T(8,128)(2,1)} %signal_hbm.1, bf16[16,1024]{1,0:T(8,128)(2,1)} %grad_hbm.1, f32[16,1024]{1,0:T(8,128)} %filter_hbm.1, f32[16]{0:T(128)} %gain_hbm.1, bf16[2,256,256]{2,1,0:T(8,128)(2,1)} %constant.10.clone.table_hbm), custom_call_target="tpu_custom_call" | custom-call | tf_op jit(solution)/shard_map/pallas_call | solution.py:203
  1.8 0.0 copy-start.2
  1.8 20.3 %all_to_all.20 = f32[16,24,128]{2,1,0:T(8,128)S(1)} all-to-all(f32[16,24,128]{2,1,0:T(8,128)S(1)} %bitcast.3), channel_id=1, replica_groups=mesh['chip'=16,'core'=2,'tp_far'=2,'tp_even'=4,'tp_next'=2] {'chip'}, dimensions={0} | all-to-all | bytes 393216 | tf_op jit(solution)/shard_map/all_to_all | solution.py:243
  22.1 0.0 copy-start
  22.1 0.0 copy-start.1
  22.1 2.2 %all_gather.3.in_ref = f32[32,24,128]{2,1,0:T(8,128)S(1)} all-gather(f32[16,24,128]{2,1,0:T(8,128)S(1)} %all_to_all.20), channel_id=1, replica_groups=mesh['chip'=16,'core'=2,'tp_far'=2,'tp_even'=4,'tp_next'=2] {'core'}, dimensions={0}, use_global_device_ids=true | all-gather | bytes 589824 | tf_op jit(solution)/shard_map/all_gather | solution.py:244
  24.3 0.0 copy-done.3
  24.3 0.0 copy-done.2
  24.3 0.0 copy-done
  24.3 0.0 copy-done.1
  24.3 1.8 %shard_map.113 = f32[16,24,128]{2,1,0:T(8,128)S(1)} custom-call(f32[32,24,128]{2,1,0:T(8,128)S(1)} %all_gather.3.in_ref, bf16[512,256]{1,0:T(8,128)(2,1)S(1)} %copy-done.3, bf16[512,256]{1,0:T(8,128)(2,1)S(1)} %copy-done.2, bf16[2,256,256]{2,1,0:T(8,128)(2,1)S(1)} %get-tuple-element.7.there, bf16[2,256,256]{2,1,0:T(8,128)(2,1)S(1)} %copy-done.1, ...), custom_call_target="tpu_custom_call" | custom-call | tf_op jit(solution)/shard_map/pallas_call | solution.py:203
  26.2 13.0 %all_to_all.21.in_ref = f32[16,24,128]{2,1,0:T(8,128)S(1)} all-to-all(f32[16,24,128]{2,1,0:T(8,128)S(1)} %shard_map.113), channel_id=1, replica_groups=mesh['chip'=16,'core'=2,'tp_far'=2,'tp_even'=4,'tp_next'=2] {'chip'}, dimensions={0} | all-to-all | bytes 393216 | tf_op jit(solution)/shard_map/all_to_all | solution.py:255
  39.2 11.4 %all_to_all.22.in_ref = f32[4,128,128]{2,1,0:T(8,128)S(1)} all-to-all(f32[4,128,128]{2,1,0:T(8,128)S(1)} %shard_map.114), channel_id=1, replica_groups=mesh['chip'=16,'core'=2,'tp_far'=2,'tp_even'=4,'tp_next'=2] {'tp_far','t..., dimensions={0} | all-to-all | bytes 524288 | tf_op jit(solution)/shard_map/all_to_all | solution.py:259
  50.6 16.2 %all_to_all.23.shares_ref = f32[4,128,128]{2,1,0:T(8,128)S(1)} all-to-all(f32[4,128,128]{2,1,0:T(8,128)S(1)} %shard_map.115), channel_id=1, replica_groups=mesh['chip'=16,'core'=2,'tp_far'=2,'tp_even'=4,'tp_next'=2] {'tp_even'}, dimensions={0} | all-to-all | bytes 524288 | tf_op jit(solution)/shard_map/all_to_all | solution.py:261
  66.8 0.7 %shard_map.116 = (bf16[16,1024]{1,0:T(8,128)(2,1)}, bf16[16,1024]{1,0:T(8,128)(2,1)}, f32[16,1024]{1,0:T(8,128)}) custom-call(f32[384,128]{1,0:T(8,128)S(1)} %bitcast.2, f32[2,16,1024]{2,1,0:T(8,128)S(1)} %get-tuple-element.8.skip_ref, f32[4,128,128]{2,1,0:T(8,128)S(1)} %all_to_all.23.shares_ref), custom_call_target="tpu_custom_call" | custom-call | tf_op jit(solution)/shard_map/pallas_call | solution.py:203
  (2 shorter events, 0.0 us)
Async XLA Ops:
  0.6 23.7 %copy-start.3 = (bf16[512,256]{1,0:T(8,128)(2,1)S(1)}, bf16[512,256]{1,0:T(8,128)(2,1)}, u32[]{:S(2)}) copy-start(bf16[512,256]{1,0:T(8,128)(2,1)} %constant.11.clone.outer_ref_h) | copy-start | bytes 786436
  1.8 22.6 %copy-start.2 = (bf16[512,256]{1,0:T(8,128)(2,1)S(1)}, bf16[512,256]{1,0:T(8,128)(2,1)}, u32[]{:S(2)}) copy-start(bf16[512,256]{1,0:T(8,128)(2,1)} %constant.12.clone.outer_ref_l) | copy-start | bytes 786436
  22.1 2.2 %copy-start = (f32[272,256]{1,0:T(8,128)S(1)}, f32[272,256]{1,0:T(8,128)}, u32[]{:S(2)}) copy-start(f32[272,256]{1,0:T(8,128)} %constant.14.clone.twist) | copy-start | bytes 835588
  22.1 2.2 %copy-start.1 = (bf16[2,256,256]{2,1,0:T(8,128)(2,1)S(1)}, bf16[2,256,256]{2,1,0:T(8,128)(2,1)}, u32[]{:S(2)}) copy-start(bf16[2,256,256]{2,1,0:T(8,128)(2,1)} %constant.13.clone.back) | copy-start | bytes 786436

commit v13 on v12

--- a/solution.py
+++ b/solution.py
@@ -96,7 +96,7 @@
     copies[4].wait()
 
 
-def convolve_kernel(in_ref, outer_ref_h, outer_ref_l, there, back, twist, out_ref, a_ref, u_h, u_l, *, scale):
+def convolve_kernel(in_ref, outer_ref_h, outer_ref_l, there, back, twist, out_ref, everyone_ref, a_ref, u_h, u_l, *, scale):
     chips = out_ref.shape[0]
     half = chips * SUBLANES
     rows = 2 * half
@@ -165,8 +165,17 @@
     columns_h, columns_l = outer_ref_h[:, mine], outer_ref_l[:, mine]
     y = dot(columns_h, u_h[...], (0, 0)) + dot(columns_h, u_l[...], (0, 0)) + dot(columns_l, u_h[...], (0, 0))
     y *= scale
-    for number in range(3):
+    for number in range(2):
         out_ref[:, number * 8 : number * 8 + 8, :] = y[:, number * LANES : (number + 1) * LANES].reshape(chips, SUBLANES, LANES)
+    for place in range(everyone_ref.shape[0]):
+        everyone_ref[place] = y[:, 2 * LANES :]
+
+
+def sum_of(in_ref):
+    total = in_ref[0]
+    for place in range(1, in_ref.shape[0]):
+        total += in_ref[place]
+    return total
 
 
 def collect_kernel(in_ref, out_ref):
@@ -175,12 +184,9 @@
         out_ref[place] = mine
 
 
-def add_kernel(in_ref, out_ref):
-    total = in_ref[0]
-    for place in range(1, in_ref.shape[0]):
-        total += in_ref[place]
-    for place in range(out_ref.shape[0]):
-        out_ref[place] = total
+def join_kernel(in_ref, shares_ref, out_ref):
+    out_ref[:, :16, :] = in_ref[...]
+    out_ref[:, 16:, :] = sum_of(shares_ref).reshape(out_ref.shape[0], SUBLANES, LANES)
 
 
 def finish_kernel(in_ref, skip_ref, shares_ref, out_ref, back_ref, corr_ref, total_ref):
@@ -242,9 +248,13 @@
     )
     spread = lax.all_to_all(packed.reshape(chips, 24, LANES), "chip", 0, 0, tiled=True)
     sequences = lax.all_gather(spread, "core", tiled=True)
-    results = call(
+    first, second = lax.axis_size(TP_FIRST), lax.axis_size(TP_SECOND)
+    results, everyone = call(
         functools.partial(convolve_kernel, scale=2.0 / (2 * length * math.sqrt(length))),
-        jax.ShapeDtypeStruct((chips, 24, LANES), jnp.float32),
+        (
+            pltpu.VMEM((chips, 16, LANES), jnp.float32),
+            pltpu.VMEM((first, rows // 2, LANES), jnp.float32),
+        ),
         (sequences, outer_h, outer_l, there, back, twist),
         scratch=(
             pltpu.VMEM((2 * rows, 3 * LANES), jnp.float32),
@@ -252,12 +262,11 @@
             pltpu.VMEM((2 * rows, 3 * LANES), jnp.bfloat16),
         ),
     )
-    returned = lax.all_to_all(results, "chip", 0, 0, tiled=True)
+    shares = lax.all_to_all(everyone, TP_FIRST, 0, 0, tiled=True)
+    joined = call(join_kernel, jax.ShapeDtypeStruct((chips, 24, LANES), jnp.float32), (results, shares))
+    returned = lax.all_to_all(joined, "chip", 0, 0, tiled=True)
     shape = (channels * SUBLANES, LANES)
-    first, second = lax.axis_size(TP_FIRST), lax.axis_size(TP_SECOND)
-    everyone = call(collect_kernel, jax.ShapeDtypeStruct((first, *shape), jnp.float32), (returned,))
-    shares = lax.all_to_all(everyone, TP_FIRST, 0, 0, tiled=True)
-    everyone = call(add_kernel, jax.ShapeDtypeStruct((second, *shape), jnp.float32), (shares,))
+    everyone = call(collect_kernel, jax.ShapeDtypeStruct((second, *shape), jnp.float32), (returned,))
     shares = lax.all_to_all(everyone, TP_SECOND, 0, 0, tiled=True)
     output, grad_signal, grad_filter = call(
         finish_kernel,

time: 67.8 us -> 67.8 us (level)
  no operation moved by 1% of the time
where the time goes in v13:
time: 67.8 us; the launch traced here: 67.5 us
  blocking collectives  63.2 us (93%)
  Pallas kernels  3.67 us (5%)
  between operations  0.68 us (1%)
    all_to_all x1, blocking collectives, on_device(): lax.all_to_all(packed.reshape(chips, 24, LANES), 'chip', 0, 0, tiled=True)  20.3 us
    all_to_all x1, blocking collectives, on_device(): shares = lax.all_to_all(everyone, TP_SECOND, 0, 0, tiled=True)  16.5 us
    all_to_all x1, blocking collectives, on_device(): returned = lax.all_to_all(joined, 'chip', 0, 0, tiled=True)  12.5 us
    all_to_all x1, blocking collectives, on_device(): shares = lax.all_to_all(everyone, TP_FIRST, 0, 0, tiled=True)  11.7 us
    pallas_call x5, Pallas kernels, call(): pl.pallas_call(kernel, out_shape=out_shape, in_specs=[pl.BlockSpec(memory...  3.67 us
    all_gather x1, blocking collectives, on_device(): sequences = lax.all_gather(spread, 'core', tiled=True)  2.21 us

profile of v13, /device:TPU:8, one launch (start us, length us, event | category | flops | bytes accessed | tf_op | source)
XLA Modules:
  0.0 67.5 jit_solution(6421070369989829859)
XLA Ops:
  0.6 0.0 copy-start.3
  0.6 1.1 %shard_map.112 = (f32[384,128]{1,0:T(8,128)S(1)}, f32[2,16,1024]{2,1,0:T(8,128)S(1)}, bf16[2,256,256]{2,1,0:T(8,128)(2,1)S(1)}) custom-call(bf16[16,1024]{1,0:T(8,128)(2,1)} %signal_hbm.1, bf16[16,1024]{1,0:T(8,128)(2,1)} %grad_hbm.1, f32[16,1024]{1,0:T(8,128)} %filter_hbm.1, f32[16]{0:T(128)} %gain_hbm.1, bf16[2,256,256]{2,1,0:T(8,128)(2,1)} %constant.10.clone.table_hbm), custom_call_target="tpu_custom_call" | custom-call | tf_op jit(solution)/shard_map/pallas_call | solution.py:209
  1.8 0.0 copy-start.2
  1.8 20.3 %all_to_all.20 = f32[16,24,128]{2,1,0:T(8,128)S(1)} all-to-all(f32[16,24,128]{2,1,0:T(8,128)S(1)} %bitcast.3), channel_id=1, replica_groups=mesh['chip'=16,'core'=2,'tp_far'=2,'tp_even'=4,'tp_next'=2] {'chip'}, dimensions={0} | all-to-all | bytes 393216 | tf_op jit(solution)/shard_map/all_to_all | solution.py:249
  22.1 0.0 copy-start
  22.1 0.0 copy-start.1
  22.1 2.2 %all_gather.3.in_ref = f32[32,24,128]{2,1,0:T(8,128)S(1)} all-gather(f32[16,24,128]{2,1,0:T(8,128)S(1)} %all_to_all.20), channel_id=1, replica_groups=mesh['chip'=16,'core'=2,'tp_far'=2,'tp_even'=4,'tp_next'=2] {'core'}, dimensions={0}, use_global_device_ids=true | all-gather | bytes 589824 | tf_op jit(solution)/shard_map/all_gather | solution.py:250
  24.3 0.0 copy-done.3
  24.3 0.0 copy-done.2
  24.3 0.0 copy-done
  24.3 0.0 copy-done.1
  24.3 1.8 %shard_map.113 = (f32[16,16,128]{2,1,0:T(8,128)S(1)}, f32[4,128,128]{2,1,0:T(8,128)S(1)}) custom-call(f32[32,24,128]{2,1,0:T(8,128)S(1)} %all_gather.3.in_ref, bf16[512,256]{1,0:T(8,128)(2,1)S(1)} %copy-done.3, bf16[512,256]{1,0:T(8,128)(2,1)S(1)} %copy-done.2, bf16[2,256,256]{2,1,0:T(8,128)(2,1)S(1)} %get-tuple-element.9.there, ...), custom_call_target="tpu_custom_call" | custom-call | tf_op jit(solution)/shard_map/pallas_call | solution.py:209
  26.2 11.7 %all_to_all.21.shares_ref = f32[4,128,128]{2,1,0:T(8,128)S(1)} all-to-all(f32[4,128,128]{2,1,0:T(8,128)S(1)} %get-tuple-element.11), channel_id=1, replica_groups=mesh['chip'=16,'core'=2,'tp_far'=2,'tp_even'=4,'tp_next'=2] {'tp_far','t..., dimensions={0} | all-to-all | bytes 524288 | tf_op jit(solution)/shard_map/all_to_all | solution.py:265
  37.9 12.5 %all_to_all.22.in_ref = f32[16,24,128]{2,1,0:T(8,128)S(1)} all-to-all(f32[16,24,128]{2,1,0:T(8,128)S(1)} %shard_map.114), channel_id=1, replica_groups=mesh['chip'=16,'core'=2,'tp_far'=2,'tp_even'=4,'tp_next'=2] {'chip'}, dimensions={0} | all-to-all | bytes 393216 | tf_op jit(solution)/shard_map/all_to_all | solution.py:267
  50.4 16.5 %all_to_all.23.shares_ref = f32[4,128,128]{2,1,0:T(8,128)S(1)} all-to-all(f32[4,128,128]{2,1,0:T(8,128)S(1)} %shard_map.115), channel_id=1, replica_groups=mesh['chip'=16,'core'=2,'tp_far'=2,'tp_even'=4,'tp_next'=2] {'tp_even'}, dimensions={0} | all-to-all | bytes 524288 | tf_op jit(solution)/shard_map/all_to_all | solution.py:270
  66.8 0.7 %shard_map.116 = (bf16[16,1024]{1,0:T(8,128)(2,1)}, bf16[16,1024]{1,0:T(8,128)(2,1)}, f32[16,1024]{1,0:T(8,128)}) custom-call(f32[384,128]{1,0:T(8,128)S(1)} %bitcast.2, f32[2,16,1024]{2,1,0:T(8,128)S(1)} %get-tuple-element.12.skip_ref, f32[4,128,128]{2,1,0:T(8,128)S(1)} %all_to_all.23.shares_ref), custom_call_target="tpu_custom_call" | custom-call | tf_op jit(solution)/shard_map/pallas_call | solution.py:209
  (2 shorter events, 0.0 us)
Async XLA Ops:
  0.6 23.7 %copy-start.3 = (bf16[512,256]{1,0:T(8,128)(2,1)S(1)}, bf16[512,256]{1,0:T(8,128)(2,1)}, u32[]{:S(2)}) copy-start(bf16[512,256]{1,0:T(8,128)(2,1)} %constant.11.clone.outer_ref_h) | copy-start | bytes 786436
  1.8 22.6 %copy-start.2 = (bf16[512,256]{1,0:T(8,128)(2,1)S(1)}, bf16[512,256]{1,0:T(8,128)(2,1)}, u32[]{:S(2)}) copy-start(bf16[512,256]{1,0:T(8,128)(2,1)} %constant.12.clone.outer_ref_l) | copy-start | bytes 786436
  22.1 2.2 %copy-start = (f32[272,256]{1,0:T(8,128)S(1)}, f32[272,256]{1,0:T(8,128)}, u32[]{:S(2)}) copy-start(f32[272,256]{1,0:T(8,128)} %constant.14.clone.twist) | copy-start | bytes 835588
  22.1 2.2 %copy-start.1 = (bf16[2,256,256]{2,1,0:T(8,128)(2,1)S(1)}, bf16[2,256,256]{2,1,0:T(8,128)(2,1)}, u32[]{:S(2)}) copy-start(bf16[2,256,256]{2,1,0:T(8,128)(2,1)} %constant.13.clone.back) | copy-start | bytes 786436

commit v14 on v12

--- a/solution.py
+++ b/solution.py
@@ -13,7 +13,8 @@
 
 LANES = 128
 SUBLANES = 8
-CTX = ("chip", "core")
+CTX = ("x_lo", "z", "core")
+CHIPS = ("z", "x_lo")
 TP = ("tp_far", "tp_even", "tp_next")
 TP_FIRST = ("tp_far", "tp_next")
 TP_SECOND = ("tp_even",)
@@ -30,7 +31,9 @@
     period = 2 * rows
     padded = period * LANES
     place = np.arange(rows)
-    block = place // SUBLANES % (blocks // 2) * 2 + place // (rows // 2)
+    member = place // SUBLANES % (blocks // 2)
+    chip = member % 2 * (blocks // 4) + member // 2
+    block = chip * 2 + place // (rows // 2)
     a = block * SUBLANES + place % SUBLANES
     f1 = np.arange(rows)
     turn = 2.0 * np.pi * (np.outer(f1, a) % period) / period
@@ -212,7 +215,7 @@
 
 def on_device(signal, filter_taps, skip_gain, grad_out):
     channels, tokens = signal.shape
-    chips = lax.axis_size("chip")
+    chips = lax.axis_size(CHIPS)
     ctx = 2 * chips
     assert channels == chips and tokens == SUBLANES * LANES
     length = tokens * ctx
@@ -240,7 +243,7 @@
         ),
         spaces=[pltpu.HBM] * 5,
     )
-    spread = lax.all_to_all(packed.reshape(chips, 24, LANES), "chip", 0, 0, tiled=True)
+    spread = lax.all_to_all(packed.reshape(chips, 24, LANES), CHIPS, 0, 0, tiled=True)
     sequences = lax.all_gather(spread, "core", tiled=True)
     results = call(
         functools.partial(convolve_kernel, scale=2.0 / (2 * length * math.sqrt(length))),
@@ -252,7 +255,7 @@
             pltpu.VMEM((2 * rows, 3 * LANES), jnp.bfloat16),
         ),
     )
-    returned = lax.all_to_all(results, "chip", 0, 0, tiled=True)
+    returned = lax.all_to_all(results, CHIPS, 0, 0, tiled=True)
     shape = (channels * SUBLANES, LANES)
     first, second = lax.axis_size(TP_FIRST), lax.axis_size(TP_SECOND)
     everyone = call(collect_kernel, jax.ShapeDtypeStruct((first, *shape), jnp.float32), (returned,))
@@ -274,7 +277,7 @@
 
 def solution(mesh):
     ctx, tp = mesh.shape["ctx"], mesh.shape["tp"]
-    parted = Mesh(mesh.devices.reshape(ctx // 2, 2, 2, tp // 4, 2), (*CTX, *TP))
+    parted = Mesh(mesh.devices.reshape(2, ctx // 4, 2, 2, tp // 4, 2), (*CTX, *TP))
     in_specs = (P(TP, CTX), P(None, CTX), P(TP), P(TP, CTX))
     out_specs = (P(TP, CTX), P(TP, CTX), P(None, CTX))
     return jax.shard_map(

time: 67.8 us -> 70.9 us (1.046)
  blocking collectives: 63.1 us -> 66.3 us
    all_to_all x2, blocking collectives: 33.3 us -> 36.4 us  [the longest x1 22.2 us: on_device(): lax.all_to_all(packed.reshape(chips, 24, LANES), CHIPS, 0, 0, tiled=True)]
where the time goes in v14:
time: 70.9 us; the launch traced here: 70.6 us
  blocking collectives  66.3 us (94%)
  Pallas kernels  3.67 us (5%)
    all_to_all x1, blocking collectives, on_device(): lax.all_to_all(packed.reshape(chips, 24, LANES), CHIPS, 0, 0, tiled=True)  22.2 us
    all_to_all x1, blocking collectives, on_device(): shares = lax.all_to_all(everyone, TP_SECOND, 0, 0, tiled=True)  16.2 us
    all_to_all x1, blocking collectives, on_device(): returned = lax.all_to_all(results, CHIPS, 0, 0, tiled=True)  14.3 us
    all_to_all x1, blocking collectives, on_device(): shares = lax.all_to_all(everyone, TP_FIRST, 0, 0, tiled=True)  11.4 us
    pallas_call x5, Pallas kernels, call(): pl.pallas_call(kernel, out_shape=out_shape, in_specs=[pl.BlockSpec(memory...  3.67 us
    all_gather x1, blocking collectives, on_device(): sequences = lax.all_gather(spread, 'core', tiled=True)  2.21 us

profile of v14, /device:TPU:8, one launch (start us, length us, event | category | flops | bytes accessed | tf_op | source)
XLA Modules:
  0.0 70.6 jit_solution(2206188272746860534)
XLA Ops:
  0.6 0.0 copy-start.3
  0.6 1.1 %shard_map.112 = (f32[384,128]{1,0:T(8,128)S(1)}, f32[2,16,1024]{2,1,0:T(8,128)S(1)}, bf16[2,256,256]{2,1,0:T(8,128)(2,1)S(1)}) custom-call(bf16[16,1024]{1,0:T(8,128)(2,1)} %signal_hbm.1, bf16[16,1024]{1,0:T(8,128)(2,1)} %grad_hbm.1, f32[16,1024]{1,0:T(8,128)} %filter_hbm.1, f32[16]{0:T(128)} %gain_hbm.1, bf16[2,256,256]{2,1,0:T(8,128)(2,1)} %constant.10.clone.table_hbm), custom_call_target="tpu_custom_call" | custom-call | tf_op jit(solution)/shard_map/pallas_call | solution.py:206
  1.8 0.0 copy-start.2
  1.8 22.2 %all_to_all.20 = f32[16,24,128]{2,1,0:T(8,128)S(1)} all-to-all(f32[16,24,128]{2,1,0:T(8,128)S(1)} %bitcast.3), channel_id=1, replica_groups=mesh['x_lo'=2,'z'=8,'core'=2,'tp_far'=2,'tp_even'=4,'tp_next'=2] {'z','x..., dimensions={0} | all-to-all | bytes 393216 | tf_op jit(solution)/shard_map/all_to_all | solution.py:246
  23.9 0.0 copy-start
  23.9 0.0 copy-start.1
  23.9 2.2 %all_gather.3.in_ref = f32[32,24,128]{2,1,0:T(8,128)S(1)} all-gather(f32[16,24,128]{2,1,0:T(8,128)S(1)} %all_to_all.20), channel_id=1, replica_groups=mesh['x_lo'=2,'z'=8,'core'=2,'tp_far'=2,'tp_even'=4,'tp_next'=2] {'core'}, dimensions={0}, use_global_device_ids=true | all-gather | bytes 589824 | tf_op jit(solution)/shard_map/all_gather | solution.py:247
  26.1 0.0 copy-done.3
  26.1 0.0 copy-done.2
  26.1 0.0 copy-done
  26.2 0.0 copy-done.1
  26.2 1.8 %shard_map.113 = f32[16,24,128]{2,1,0:T(8,128)S(1)} custom-call(f32[32,24,128]{2,1,0:T(8,128)S(1)} %all_gather.3.in_ref, bf16[512,256]{1,0:T(8,128)(2,1)S(1)} %copy-done.3, bf16[512,256]{1,0:T(8,128)(2,1)S(1)} %copy-done.2, bf16[2,256,256]{2,1,0:T(8,128)(2,1)S(1)} %get-tuple-element.7.there, bf16[2,256,256]{2,1,0:T(8,128)(2,1)S(1)} %copy-done.1, ...), custom_call_target="tpu_custom_call" | custom-call | tf_op jit(solution)/shard_map/pallas_call | solution.py:206
  28.0 14.3 %all_to_all.21.in_ref = f32[16,24,128]{2,1,0:T(8,128)S(1)} all-to-all(f32[16,24,128]{2,1,0:T(8,128)S(1)} %shard_map.113), channel_id=1, replica_groups=mesh['x_lo'=2,'z'=8,'core'=2,'tp_far'=2,'tp_even'=4,'tp_next'=2] {'z','x..., dimensions={0} | all-to-all | bytes 393216 | tf_op jit(solution)/shard_map/all_to_all | solution.py:258
  42.3 11.4 %all_to_all.22.in_ref = f32[4,128,128]{2,1,0:T(8,128)S(1)} all-to-all(f32[4,128,128]{2,1,0:T(8,128)S(1)} %shard_map.114), channel_id=1, replica_groups=mesh['x_lo'=2,'z'=8,'core'=2,'tp_far'=2,'tp_even'=4,'tp_next'=2] {'tp_fa..., dimensions={0} | all-to-all | bytes 524288 | tf_op jit(solution)/shard_map/all_to_all | solution.py:262
  53.7 16.2 %all_to_all.23.shares_ref = f32[4,128,128]{2,1,0:T(8,128)S(1)} all-to-all(f32[4,128,128]{2,1,0:T(8,128)S(1)} %shard_map.115), channel_id=1, replica_groups=mesh['x_lo'=2,'z'=8,'core'=2,'tp_far'=2,'tp_even'=4,'tp_next'=2] {'tp_ev..., dimensions={0} | all-to-all | bytes 524288 | tf_op jit(solution)/shard_map/all_to_all | solution.py:264
  69.9 0.7 shard_map.116
  (2 shorter events, 0.0 us)
Async XLA Ops:
  0.6 25.5 %copy-start.3 = (bf16[512,256]{1,0:T(8,128)(2,1)S(1)}, bf16[512,256]{1,0:T(8,128)(2,1)}, u32[]{:S(2)}) copy-start(bf16[512,256]{1,0:T(8,128)(2,1)} %constant.11.clone.outer_ref_h) | copy-start | bytes 786436
  1.8 24.4 %copy-start.2 = (bf16[512,256]{1,0:T(8,128)(2,1)S(1)}, bf16[512,256]{1,0:T(8,128)(2,1)}, u32[]{:S(2)}) copy-start(bf16[512,256]{1,0:T(8,128)(2,1)} %constant.12.clone.outer_ref_l) | copy-start | bytes 786436
  23.9 2.2 %copy-start = (f32[272,256]{1,0:T(8,128)S(1)}, f32[272,256]{1,0:T(8,128)}, u32[]{:S(2)}) copy-start(f32[272,256]{1,0:T(8,128)} %constant.14.clone.twist) | copy-start | bytes 835588
  23.9 2.2 %copy-start.1 = (bf16[2,256,256]{2,1,0:T(8,128)(2,1)S(1)}, bf16[2,256,256]{2,1,0:T(8,128)(2,1)}, u32[]{:S(2)}) copy-start(bf16[2,256,256]{2,1,0:T(8,128)(2,1)} %constant.13.clone.back) | copy-start | bytes 786436

commit v15 on v12

--- a/solution.py
+++ b/solution.py
@@ -15,7 +15,7 @@
 SUBLANES = 8
 CTX = ("chip", "core")
 TP = ("tp_far", "tp_even", "tp_next")
-TP_FIRST = ("tp_far", "tp_next")
+TP_FIRST = ("tp_next", "tp_far")
 TP_SECOND = ("tp_even",)
 VMEM_BYTES = 24 * 1024 * 1024
 

time: 67.8 us -> 67.8 us (level)
  no operation moved by 1% of the time
where the time goes in v15:
time: 67.8 us; the launch traced here: 67.5 us
  blocking collectives  63.1 us (93%)
  Pallas kernels  3.67 us (5%)
  between operations  0.68 us (1%)
    all_to_all x1, blocking collectives, on_device(): lax.all_to_all(packed.reshape(chips, 24, LANES), 'chip', 0, 0, tiled=True)  20.3 us
    all_to_all x1, blocking collectives, on_device(): shares = lax.all_to_all(everyone, TP_SECOND, 0, 0, tiled=True)  16.2 us
    all_to_all x1, blocking collectives, on_device(): returned = lax.all_to_all(results, 'chip', 0, 0, tiled=True)  13 us
    all_to_all x1, blocking collectives, on_device(): shares = lax.all_to_all(everyone, TP_FIRST, 0, 0, tiled=True)  11.4 us
    pallas_call x5, Pallas kernels, call(): pl.pallas_call(kernel, out_shape=out_shape, in_specs=[pl.BlockSpec(memory...  3.67 us
    all_gather x1, blocking collectives, on_device(): sequences = lax.all_gather(spread, 'core', tiled=True)  2.21 us

profile of v15, /device:TPU:8, one launch (start us, length us, event | category | flops | bytes accessed | tf_op | source)
XLA Modules:
  0.0 67.5 jit_solution(11920535083875035166)
XLA Ops:
  0.6 0.0 copy-start.3
  0.6 1.1 %shard_map.112 = (f32[384,128]{1,0:T(8,128)S(1)}, f32[2,16,1024]{2,1,0:T(8,128)S(1)}, bf16[2,256,256]{2,1,0:T(8,128)(2,1)S(1)}) custom-call(bf16[16,1024]{1,0:T(8,128)(2,1)} %signal_hbm.1, bf16[16,1024]{1,0:T(8,128)(2,1)} %grad_hbm.1, f32[16,1024]{1,0:T(8,128)} %filter_hbm.1, f32[16]{0:T(128)} %gain_hbm.1, bf16[2,256,256]{2,1,0:T(8,128)(2,1)} %constant.10.clone.table_hbm), custom_call_target="tpu_custom_call" | custom-call | tf_op jit(solution)/shard_map/pallas_call | solution.py:203
  1.8 0.0 copy-start.2
  1.8 20.3 %all_to_all.20 = f32[16,24,128]{2,1,0:T(8,128)S(1)} all-to-all(f32[16,24,128]{2,1,0:T(8,128)S(1)} %bitcast.3), channel_id=1, replica_groups=mesh['chip'=16,'core'=2,'tp_far'=2,'tp_even'=4,'tp_next'=2] {'chip'}, dimensions={0} | all-to-all | bytes 393216 | tf_op jit(solution)/shard_map/all_to_all | solution.py:243
  22.1 0.0 copy-start
  22.1 0.0 copy-start.1
  22.1 2.2 %all_gather.3.in_ref = f32[32,24,128]{2,1,0:T(8,128)S(1)} all-gather(f32[16,24,128]{2,1,0:T(8,128)S(1)} %all_to_all.20), channel_id=1, replica_groups=mesh['chip'=16,'core'=2,'tp_far'=2,'tp_even'=4,'tp_next'=2] {'core'}, dimensions={0}, use_global_device_ids=true | all-gather | bytes 589824 | tf_op jit(solution)/shard_map/all_gather | solution.py:244
  24.3 0.0 copy-done.3
  24.3 0.0 copy-done.2
  24.3 0.0 copy-done
  24.3 0.0 copy-done.1
  24.3 1.8 %shard_map.113 = f32[16,24,128]{2,1,0:T(8,128)S(1)} custom-call(f32[32,24,128]{2,1,0:T(8,128)S(1)} %all_gather.3.in_ref, bf16[512,256]{1,0:T(8,128)(2,1)S(1)} %copy-done.3, bf16[512,256]{1,0:T(8,128)(2,1)S(1)} %copy-done.2, bf16[2,256,256]{2,1,0:T(8,128)(2,1)S(1)} %get-tuple-element.7.there, bf16[2,256,256]{2,1,0:T(8,128)(2,1)S(1)} %copy-done.1, ...), custom_call_target="tpu_custom_call" | custom-call | tf_op jit(solution)/shard_map/pallas_call | solution.py:203
  26.2 13.0 %all_to_all.21.in_ref = f32[16,24,128]{2,1,0:T(8,128)S(1)} all-to-all(f32[16,24,128]{2,1,0:T(8,128)S(1)} %shard_map.113), channel_id=1, replica_groups=mesh['chip'=16,'core'=2,'tp_far'=2,'tp_even'=4,'tp_next'=2] {'chip'}, dimensions={0} | all-to-all | bytes 393216 | tf_op jit(solution)/shard_map/all_to_all | solution.py:255
  39.2 11.4 %all_to_all.22.in_ref = f32[4,128,128]{2,1,0:T(8,128)S(1)} all-to-all(f32[4,128,128]{2,1,0:T(8,128)S(1)} %shard_map.114), channel_id=1, replica_groups=mesh['chip'=16,'core'=2,'tp_far'=2,'tp_even'=4,'tp_next'=2] {'tp_next','..., dimensions={0} | all-to-all | bytes 524288 | tf_op jit(solution)/shard_map/all_to_all | solution.py:259
  50.6 16.2 %all_to_all.23.shares_ref = f32[4,128,128]{2,1,0:T(8,128)S(1)} all-to-all(f32[4,128,128]{2,1,0:T(8,128)S(1)} %shard_map.115), channel_id=1, replica_groups=mesh['chip'=16,'core'=2,'tp_far'=2,'tp_even'=4,'tp_next'=2] {'tp_even'}, dimensions={0} | all-to-all | bytes 524288 | tf_op jit(solution)/shard_map/all_to_all | solution.py:261
  66.8 0.7 %shard_map.116 = (bf16[16,1024]{1,0:T(8,128)(2,1)}, bf16[16,1024]{1,0:T(8,128)(2,1)}, f32[16,1024]{1,0:T(8,128)}) custom-call(f32[384,128]{1,0:T(8,128)S(1)} %bitcast.2, f32[2,16,1024]{2,1,0:T(8,128)S(1)} %get-tuple-element.8.skip_ref, f32[4,128,128]{2,1,0:T(8,128)S(1)} %all_to_all.23.shares_ref), custom_call_target="tpu_custom_call" | custom-call | tf_op jit(solution)/shard_map/pallas_call | solution.py:203
  (2 shorter events, 0.0 us)
Async XLA Ops:
  0.6 23.7 %copy-start.3 = (bf16[512,256]{1,0:T(8,128)(2,1)S(1)}, bf16[512,256]{1,0:T(8,128)(2,1)}, u32[]{:S(2)}) copy-start(bf16[512,256]{1,0:T(8,128)(2,1)} %constant.11.clone.outer_ref_h) | copy-start | bytes 786436
  1.8 22.6 %copy-start.2 = (bf16[512,256]{1,0:T(8,128)(2,1)S(1)}, bf16[512,256]{1,0:T(8,128)(2,1)}, u32[]{:S(2)}) copy-start(bf16[512,256]{1,0:T(8,128)(2,1)} %constant.12.clone.outer_ref_l) | copy-start | bytes 786436
  22.1 2.2 %copy-start = (f32[272,256]{1,0:T(8,128)S(1)}, f32[272,256]{1,0:T(8,128)}, u32[]{:S(2)}) copy-start(f32[272,256]{1,0:T(8,128)} %constant.14.clone.twist) | copy-start | bytes 835588
  22.1 2.2 %copy-start.1 = (bf16[2,256,256]{2,1,0:T(8,128)(2,1)S(1)}, bf16[2,256,256]{2,1,0:T(8,128)(2,1)}, u32[]{:S(2)}) copy-start(bf16[2,256,256]{2,1,0:T(8,128)(2,1)} %constant.13.clone.back) | copy-start | bytes 786436

commit v16 on v15

--- a/solution.py
+++ b/solution.py
@@ -14,9 +14,9 @@
 LANES = 128
 SUBLANES = 8
 CTX = ("chip", "core")
-TP = ("tp_far", "tp_even", "tp_next")
+TP = ("tp_far", "tp_half", "tp_two", "tp_next")
 TP_FIRST = ("tp_next", "tp_far")
-TP_SECOND = ("tp_even",)
+TP_SECOND = ("tp_two", "tp_half")
 VMEM_BYTES = 24 * 1024 * 1024
 
 
@@ -274,7 +274,7 @@
 
 def solution(mesh):
     ctx, tp = mesh.shape["ctx"], mesh.shape["tp"]
-    parted = Mesh(mesh.devices.reshape(ctx // 2, 2, 2, tp // 4, 2), (*CTX, *TP))
+    parted = Mesh(mesh.devices.reshape(ctx // 2, 2, 2, tp // 8, 2, 2), (*CTX, *TP))
     in_specs = (P(TP, CTX), P(None, CTX), P(TP), P(TP, CTX))
     out_specs = (P(TP, CTX), P(TP, CTX), P(None, CTX))
     return jax.shard_map(

time: 67.8 us -> 67.8 us (level)
  no operation moved by 1% of the time
where the time goes in v16:
time: 67.8 us; the launch traced here: 67.5 us
  blocking collectives  63.2 us (93%)
  Pallas kernels  3.67 us (5%)
  between operations  0.68 us (1%)
    all_to_all x1, blocking collectives, on_device(): lax.all_to_all(packed.reshape(chips, 24, LANES), 'chip', 0, 0, tiled=True)  20.3 us
    all_to_all x1, blocking collectives, on_device(): shares = lax.all_to_all(everyone, TP_SECOND, 0, 0, tiled=True)  16.3 us
    all_to_all x1, blocking collectives, on_device(): returned = lax.all_to_all(results, 'chip', 0, 0, tiled=True)  13 us
    all_to_all x1, blocking collectives, on_device(): shares = lax.all_to_all(everyone, TP_FIRST, 0, 0, tiled=True)  11.4 us
    pallas_call x5, Pallas kernels, call(): pl.pallas_call(kernel, out_shape=out_shape, in_specs=[pl.BlockSpec(memory...  3.67 us
    all_gather x1, blocking collectives, on_device(): sequences = lax.all_gather(spread, 'core', tiled=True)  2.21 us

profile of v16, /device:TPU:8, one launch (start us, length us, event | category | flops | bytes accessed | tf_op | source)
XLA Modules:
  0.0 67.5 jit_solution(3163941496512495615)
XLA Ops:
  0.6 0.0 copy-start.3
  0.6 1.1 %shard_map.112 = (f32[384,128]{1,0:T(8,128)S(1)}, f32[2,16,1024]{2,1,0:T(8,128)S(1)}, bf16[2,256,256]{2,1,0:T(8,128)(2,1)S(1)}) custom-call(bf16[16,1024]{1,0:T(8,128)(2,1)} %signal_hbm.1, bf16[16,1024]{1,0:T(8,128)(2,1)} %grad_hbm.1, f32[16,1024]{1,0:T(8,128)} %filter_hbm.1, f32[16]{0:T(128)} %gain_hbm.1, bf16[2,256,256]{2,1,0:T(8,128)(2,1)} %constant.10.clone.table_hbm), custom_call_target="tpu_custom_call" | custom-call | tf_op jit(solution)/shard_map/pallas_call | solution.py:203
  1.8 0.0 copy-start.2
  1.8 20.3 %all_to_all.20 = f32[16,24,128]{2,1,0:T(8,128)S(1)} all-to-all(f32[16,24,128]{2,1,0:T(8,128)S(1)} %bitcast.3), channel_id=1, replica_groups=mesh['chip'=16,'core'=2,'tp_far'=2,'tp_half'=2,'tp_two'=2,'tp_next'=2] {..., dimensions={0} | all-to-all | bytes 393216 | tf_op jit(solution)/shard_map/all_to_all | solution.py:243
  22.1 0.0 copy-start
  22.1 0.0 copy-start.1
  22.1 2.2 %all_gather.3.in_ref = f32[32,24,128]{2,1,0:T(8,128)S(1)} all-gather(f32[16,24,128]{2,1,0:T(8,128)S(1)} %all_to_all.20), channel_id=1, replica_groups=mesh['chip'=16,'core'=2,'tp_far'=2,'tp_half'=2,'tp_two'=2,'tp_next'=2] {..., dimensions={0}, use_global_device_ids=true | all-gather | bytes 589824 | tf_op jit(solution)/shard_map/all_gather | solution.py:244
  24.3 0.0 copy-done.3
  24.3 0.0 copy-done.2
  24.3 0.0 copy-done
  24.3 0.0 copy-done.1
  24.3 1.8 %shard_map.113 = f32[16,24,128]{2,1,0:T(8,128)S(1)} custom-call(f32[32,24,128]{2,1,0:T(8,128)S(1)} %all_gather.3.in_ref, bf16[512,256]{1,0:T(8,128)(2,1)S(1)} %copy-done.3, bf16[512,256]{1,0:T(8,128)(2,1)S(1)} %copy-done.2, bf16[2,256,256]{2,1,0:T(8,128)(2,1)S(1)} %get-tuple-element.7.there, bf16[2,256,256]{2,1,0:T(8,128)(2,1)S(1)} %copy-done.1, ...), custom_call_target="tpu_custom_call" | custom-call | tf_op jit(solution)/shard_map/pallas_call | solution.py:203
  26.2 13.0 %all_to_all.21.in_ref = f32[16,24,128]{2,1,0:T(8,128)S(1)} all-to-all(f32[16,24,128]{2,1,0:T(8,128)S(1)} %shard_map.113), channel_id=1, replica_groups=mesh['chip'=16,'core'=2,'tp_far'=2,'tp_half'=2,'tp_two'=2,'tp_next'=2] {..., dimensions={0} | all-to-all | bytes 393216 | tf_op jit(solution)/shard_map/all_to_all | solution.py:255
  39.2 11.4 %all_to_all.22.in_ref = f32[4,128,128]{2,1,0:T(8,128)S(1)} all-to-all(f32[4,128,128]{2,1,0:T(8,128)S(1)} %shard_map.114), channel_id=1, replica_groups=mesh['chip'=16,'core'=2,'tp_far'=2,'tp_half'=2,'tp_two'=2,'tp_next'=2] {..., dimensions={0} | all-to-all | bytes 524288 | tf_op jit(solution)/shard_map/all_to_all | solution.py:259
  50.6 16.3 %all_to_all.23.shares_ref = f32[4,128,128]{2,1,0:T(8,128)S(1)} all-to-all(f32[4,128,128]{2,1,0:T(8,128)S(1)} %shard_map.115), channel_id=1, replica_groups=mesh['chip'=16,'core'=2,'tp_far'=2,'tp_half'=2,'tp_two'=2,'tp_next'=2] {..., dimensions={0} | all-to-all | bytes 524288 | tf_op jit(solution)/shard_map/all_to_all | solution.py:261
  66.8 0.7 %shard_map.116 = (bf16[16,1024]{1,0:T(8,128)(2,1)}, bf16[16,1024]{1,0:T(8,128)(2,1)}, f32[16,1024]{1,0:T(8,128)}) custom-call(f32[384,128]{1,0:T(8,128)S(1)} %bitcast.2, f32[2,16,1024]{2,1,0:T(8,128)S(1)} %get-tuple-element.8.skip_ref, f32[4,128,128]{2,1,0:T(8,128)S(1)} %all_to_all.23.shares_ref), custom_call_target="tpu_custom_call" | custom-call | tf_op jit(solution)/shard_map/pallas_call | solution.py:203
  (2 shorter events, 0.0 us)
Async XLA Ops:
  0.6 23.7 %copy-start.3 = (bf16[512,256]{1,0:T(8,128)(2,1)S(1)}, bf16[512,256]{1,0:T(8,128)(2,1)}, u32[]{:S(2)}) copy-start(bf16[512,256]{1,0:T(8,128)(2,1)} %constant.11.clone.outer_ref_h) | copy-start | bytes 786436
  1.8 22.6 %copy-start.2 = (bf16[512,256]{1,0:T(8,128)(2,1)S(1)}, bf16[512,256]{1,0:T(8,128)(2,1)}, u32[]{:S(2)}) copy-start(bf16[512,256]{1,0:T(8,128)(2,1)} %constant.12.clone.outer_ref_l) | copy-start | bytes 786436
  22.1 2.2 %copy-start = (f32[272,256]{1,0:T(8,128)S(1)}, f32[272,256]{1,0:T(8,128)}, u32[]{:S(2)}) copy-start(f32[272,256]{1,0:T(8,128)} %constant.14.clone.twist) | copy-start | bytes 835588
  22.1 2.2 %copy-start.1 = (bf16[2,256,256]{2,1,0:T(8,128)(2,1)S(1)}, bf16[2,256,256]{2,1,0:T(8,128)(2,1)}, u32[]{:S(2)}) copy-start(bf16[2,256,256]{2,1,0:T(8,128)(2,1)} %constant.13.clone.back) | copy-start | bytes 786436
